TPU v7x, 32 devices: a whole 2x2x4 slice. The times are simulated.
32 devices in a mesh: gx: 4 (over y, core), gy: 8 (over z, x).
Axes of the slice: x: 2, y: 2, z: 4, core: 2. Of those that a mesh axis runs over, the one named last changes fastest.
Arguments:
- pressure: float32 [256, 128, 512], P('gx', 'gy'), may hold values from -6 to 6
- divergence: float32 [256, 128, 512], P('gx', 'gy'), may hold values from -6 to 6
- diagonal: float32 [256, 128, 512], P('gx', 'gy'), may hold values from 0.05 to 0.5
- normals: float32 [3, 32768], P(None, ('gx', 'gy')), may hold values from -6 to 6
- traction: float32 [3, 32768], P(None, ('gx', 'gy')), may hold values from -3 to 3
- slot_of: int32 [4, 8192], P('gx'), may hold values from 0 to 24575, as said below
- counts: int32 [32], P(('gx', 'gy')), may hold values from 0 to 3072, as said below
- previous: float32 [3, 98304], P(None, ('gx', 'gy')), may hold values from -6 to 6
- secant_v: float32 [32, 3, 98304], P(None, None, ('gx', 'gy')), may hold values from -6 to 6
- secant_w: float32 [32, 3, 98304], P(None, None, ('gx', 'gy')), may hold values from -332.55374 to 332.55374
Outputs:
- pressure_new: float32 [256, 128, 512], P('gx', 'gy')
- coupled: float32 [3, 98304], P(None, ('gx', 'gy'))
Inputs may be any that keep to these rules, and one draw needn't show every extreme that they name: Within each group (row of slot_of) the places are distinct; place o * 3072 + s has s < counts[a * 8 + o]; every such place is used; the rows of one device (aligned blocks of 1024 entries) send at most 384 rows to one owner, and exactly 384 to some owner. The counts of one group sum to 8192; some owner of every group holds exactly 3072.
All inputs are finite; a program needn't handle non-finite values.
Results may differ from a plain program's by a relative error of at most 0.00019.
Values sent between devices are 32-bit elements; how exact they have to be, the bound alone decides.
No kernel may reach another device: no remote copies, remote signals or barrier semaphores. Data moves between devices by JAX's collectives and lax.ppermute only.
A program may use at most 128 MiB of HBM per device.

v0:
```python
import jax
import jax.numpy as jnp
from jax import lax
from jax.sharding import PartitionSpec as P

SWEEPS = 2


def extended(cells, sides, width):
    for axis, dim in sides:
        count = lax.axis_size(axis)
        ends = count - 1
        head = lax.slice_in_dim(cells, 0, width, axis=dim)
        tail = lax.slice_in_dim(cells, cells.shape[dim] - width, cells.shape[dim], axis=dim)
        cells = jnp.concatenate(
            [
                lax.ppermute(tail, axis, [(i, (i + 1) % count) for i in range(ends)]),
                cells,
                lax.ppermute(head, axis, [((i + 1) % count, i) for i in range(ends)]),
            ],
            axis=dim,
        )
    return cells


def stencil_sum(padded):
    padded = jnp.pad(padded, ((0, 0), (0, 0), (1, 1)))
    total = padded[2:, 1:-1, 1:-1] + padded[:-2, 1:-1, 1:-1]
    total = total + padded[1:-1, 2:, 1:-1] + padded[1:-1, :-2, 1:-1]
    total = total + padded[1:-1, 1:-1, 2:] + padded[1:-1, 1:-1, :-2]
    return total


def sweep_once(field, divergence, diagonal):
    padded = extended(field, (("gx", 0), ("gy", 1)), 1)
    return (divergence + stencil_sum(padded)) / (6.0 + diagonal)


def shards(
    pressure, divergence, diagonal, normals, traction, slot_of, counts, previous, secant_v, secant_w
):
    columns = secant_v.shape[0]
    capacity = previous.shape[1]
    slot_index = jnp.arange(capacity, dtype=jnp.int32)
    occupied = (slot_index < counts[0]).astype(jnp.float32)
    masked_v = (secant_v * occupied[None, None, :]).reshape(columns, 3 * capacity)
    gram_local = jnp.dot(masked_v, masked_v.T, precision=lax.Precision.HIGHEST)
    field = pressure
    for sweep_index in range(SWEEPS):
        field = sweep_once(field, divergence, diagonal)
    surface = field[:, :, -1].reshape(-1)
    forces = normals * surface[None, :] + traction
    own_index = lax.axis_index("gy")
    all_slots = slot_of[0]
    gathered = lax.all_gather(forces, "gy", axis=1, tiled=True)
    placed = jnp.where(all_slots // capacity == own_index, all_slots % capacity, capacity)
    owned = jnp.zeros((3, capacity), jnp.float32).at[:, placed].set(gathered, mode="drop")
    residual = occupied[None, :] * (owned - previous)
    projection_local = jnp.dot(
        masked_v, residual.reshape(3 * capacity), precision=lax.Precision.HIGHEST
    )
    gram, projection = lax.psum((gram_local, projection_local), ("gx", "gy"))
    factor = jnp.linalg.cholesky(gram)
    coefficient = -jax.scipy.linalg.cho_solve((factor, True), projection)
    update = jnp.dot(
        coefficient, secant_w.reshape(columns, 3 * capacity), precision=lax.Precision.HIGHEST
    ).reshape(3, capacity)
    coupled = occupied[None, :] * (owned + update)
    return (field, coupled)


def solution(mesh):
    placed = (
        P("gx", "gy", None),
        P("gx", "gy", None),
        P("gx", "gy", None),
        P(None, ("gx", "gy")),
        P(None, ("gx", "gy")),
        P("gx", None),
        P(("gx", "gy")),
        P(None, ("gx", "gy")),
        P(None, None, ("gx", "gy")),
        P(None, None, ("gx", "gy")),
    )
    return jax.shard_map(
        shards,
        mesh=mesh,
        in_specs=placed,
        out_specs=(P("gx", "gy", None), P(None, ("gx", "gy"))),
        check_vma=False,
    )
```

profile of v0, /device:TPU:0, one launch (start us, length us, event | category | flops | bytes accessed | tf_op | source)
XLA Modules:
  0.0 179.5 jit_solution(8628824472490217064)
XLA Ops:
  2.9 3.0 %collective-permute-start.1 = (f32[1,16,512]{2,0,1:T(1,128)S(1)}, f32[1,16,512]{2,0,1:T(1,128)S(1)}, u32[]{:S(2)}, u32[]{:S(2)}) collective-permute-start(f32[1,16,512]{2,0,1:T(1,128)S(1)} %copy.25), channel_id=1, source_target_pairs={{0,8},{8,16},{16,24},{1,9},{9,17},{17,25},{2,10},{10,18},{18,26},{... | collective-permute-start | bytes 98312 | tf_op jit(solution)/shard_map/ppermute | solution.py:17
  5.9 2.8 %copy.24 = f32[64,16,512]{2,0,1:T(8,128)S(1)} copy(f32[64,16,512]{2,1,0:T(8,128)} %param.10) | data formatting | bytes 4194304 | tf_op args[0]
  10.1 5.5 %collective-permute-start.3 = (f32[66,1,512]{2,0,1:T(8,128)S(1)}, f32[66,1,512]{2,0,1:T(8,128)S(1)}, u32[]{:S(2)}, u32[]{:S(2)}) collective-permute-start(f32[66,1,512]{2,0,1:T(8,128)S(1)} %get-tuple-element.12), channel_id=1, source_target_pairs={{0,1},{1,2},{2,3},{3,4},{4,5},{5,6},{6,7},{8,9},{9,10},{10,11},{11... | collective-permute-start | bytes 405512 | tf_op jit(solution)/shard_map/ppermute | solution.py:17
  17.7 4.2 %collective-permute-done.3 = f32[66,1,512]{2,0,1:T(8,128)S(1)} collective-permute-done((f32[66,1,512]{2,0,1:T(8,128)S(1)}, f32[66,1,512]{2,0,1:T(8,128)S(1)}, u32[]{:S(2)}, u32[]{:S(2)}) %collective-permute-start.3) | collective-permute-done | bytes 135200 | tf_op jit(solution)/shard_map/ppermute | solution.py:17
  21.9 2.8 %select_maximum_fusion.4 = f32[66,18,514]{2,0,1:T(8,128)S(1)} fusion(f32[66,1,512]{2,0,1:T(8,128)S(1)} %collective-permute-done.2, f32[66,1,512]{2,0,1:T(8,128)S(1)} %collective-permute-done.3, f32[1,16,512]{2,0,1:T(1,128)S(1)} %collective-permute-done, f32[64,16,512]{2,0,1:T(8,128)S(1)} %copy.24, f32[1,16,512]{2,0,1:T(1,128)S(1)} %collective-permute-done.1), kind=kLoop, calls=%fused_computation.7 | loop fusion | flops 7327584 | bytes 4875552 | tf_op jit(solution)/shard_map/concatenate | solution.py:15
  24.8 6.9 %fusion.7 = f32[64,16,512]{2,0,1:T(8,128)S(1)} fusion(f32[66,18,514]{2,0,1:T(8,128)S(1)} %select_maximum_fusion.4, f32[66,1,512]{2,0,1:T(8,128)S(1)} %collective-permute-done.3, f32[1,16,512]{2,0,1:T(1,128)S(1)} %collective-permute-done, f32[64,16,512]{2,0,1:T(8,128)} %copy-done.1, f32[1,16,512]{2,0,1:T(1,128)S(1)} %collective-permute-done.1, ...), kind=kLoop, calls=%fused_computation.29 | loop fusion | flops 8388608 | bytes 12918784 | tf_op jit(solution)/shard_map/div | solution.py:36
  33.1 3.0 %collective-permute-start.5 = (f32[1,16,512]{2,0,1:T(1,128)S(1)}, f32[1,16,512]{2,0,1:T(1,128)S(1)}, u32[]{:S(2)}, u32[]{:S(2)}) collective-permute-start(f32[1,16,512]{2,0,1:T(1,128)S(1)} %get-tuple-element.14), channel_id=1, source_target_pairs={{0,8},{8,16},{16,24},{1,9},{9,17},{17,25},{2,10},{10,18},{18,26},{... | collective-permute-start | bytes 98312 | tf_op jit(solution)/shard_map/ppermute | solution.py:17
  36.1 1.7 copy.35
  39.3 5.2 %collective-permute-start.7 = (f32[66,1,512]{2,0,1:T(8,128)S(1)}, f32[66,1,512]{2,0,1:T(8,128)S(1)}, u32[]{:S(2)}, u32[]{:S(2)}) collective-permute-start(f32[66,1,512]{2,0,1:T(8,128)S(1)} %get-tuple-element.10), channel_id=1, source_target_pairs={{0,1},{1,2},{2,3},{3,4},{4,5},{5,6},{6,7},{8,9},{9,10},{10,11},{11... | collective-permute-start | bytes 405512 | tf_op jit(solution)/shard_map/ppermute | solution.py:17
  46.5 4.2 %collective-permute-done.7 = f32[66,1,512]{2,0,1:T(8,128)S(1)} collective-permute-done((f32[66,1,512]{2,0,1:T(8,128)S(1)}, f32[66,1,512]{2,0,1:T(8,128)S(1)}, u32[]{:S(2)}, u32[]{:S(2)}) %collective-permute-start.7) | collective-permute-done | bytes 135200 | tf_op jit(solution)/shard_map/ppermute | solution.py:17
  50.6 2.8 %select_maximum_fusion = f32[66,18,514]{2,0,1:T(8,128)S(1)} fusion(f32[66,1,512]{2,0,1:T(8,128)S(1)} %collective-permute-done.6, f32[66,1,512]{2,0,1:T(8,128)S(1)} %collective-permute-done.7, f32[1,16,512]{2,0,1:T(1,128)S(1)} %collective-permute-done.4, f32[64,16,512]{2,0,1:T(8,128)S(1)} %fusion.7, f32[1,16,512]{2,0,1:T(1,128)S(1)} %collective-permute-done.5), kind=kLoop, calls=%fused_computation.3 | loop fusion | flops 7327584 | bytes 4875552 | tf_op jit(solution)/shard_map/concatenate | solution.py:15
  53.5 6.7 %fusion.2 = f32[64,16,512]{2,0,1:T(8,128)S(1)} fusion(f32[66,18,514]{2,0,1:T(8,128)S(1)} %select_maximum_fusion, f32[66,1,512]{2,0,1:T(8,128)S(1)} %collective-permute-done.7, f32[1,16,512]{2,0,1:T(1,128)S(1)} %collective-permute-done.4, f32[64,16,512]{2,0,1:T(8,128)S(1)} %fusion.7, f32[1,16,512]{2,0,1:T(1,128)S(1)} %collective-permute-done.5, ...), kind=kLoop, calls=%fused_computation.14 | loop fusion | flops 8388608 | bytes 12918784 | tf_op jit(solution)/shard_map/div | solution.py:36
  60.5 2.5 %copy.37 = f32[64,16,512]{2,1,0:T(8,128)} copy(f32[64,16,512]{2,0,1:T(8,128)S(1)} %fusion.2) | data formatting | bytes 4194304
  63.6 32.1 %all_gather.3 = f32[3,8192]{1,0:T(4,128)S(1)} all-gather(f32[3,1024]{1,0:T(4,128)S(1)} %multiply_add_fusion), channel_id=1, replica_groups=mesh['gx'=4,'gy'=8] {'gy'}, dimensions={1}, use_global_device_ids=true | all-gather | bytes 110592 | tf_op jit(solution)/shard_map/all_gather | solution.py:55
  95.7 2.6 %copy.32 = f32[8192,3]{1,0:T(8,128)} copy(f32[8192,3]{0,1:T(4,128)S(1)} %bitcast.77) | data formatting | bytes 196608 | tf_op jit(solution)/shard_map/all_gather | solution.py:55
  98.3 21.2 %scatter_custom_fusion = f32[3,3072]{0,1:T(8,128)S(1)} fusion(s32[8192]{0:T(1024)S(1)} %bitcast.78, f32[8192,3]{1,0:T(8,128)} %copy.32, f32[]{:T(128)} %constant.70.clone.1), kind=kCustom, calls=%fused_computation.58 | custom fusion | bytes 37376 | tf_op jit(solution)/shard_map/scatter | solution.py:57
  119.6 3.1 %multiply_bitcast_fusion = f32[3,3072,1]{0,1,2:T(8,128)} fusion(f32[3,3072]{0,1:T(8,128)S(1)} %scatter_custom_fusion, f32[3,3072]{0,1:T(8,128)} %copy.35, f32[3072]{0:T(1024)S(1)} %fusion.32), kind=kLoop, calls=%fused_computation.45 | loop fusion | flops 18432 | bytes 122880 | tf_op jit(solution)/shard_map/mul | solution.py:58
  122.6 1.9 %copy.40 = f32[3,3072,1]{1,2,0:T(1,128)S(1)} copy(f32[3,3072,1]{0,1,2:T(8,128)} %multiply_bitcast_fusion) | data formatting | bytes 73728 | tf_op jit(solution)/shard_map/mul | solution.py:58
  124.5 2.3 %fusion.20 = f32[32]{0:T(128)S(1)} fusion(f32[3,3072,1]{1,2,0:T(1,128)S(1)} %copy.40, f32[32,3,3072]{2,0,1:T(8,128)} %param.18, f32[3072]{0:T(1024)S(1)} %fusion.32), kind=kOutput, calls=%fused_computation.57 | convolution fusion | flops 3833856 | bytes 1228928 | tf_op jit(solution)/shard_map/dot_general | solution.py:59
  126.8 37.7 %all-reduce.2 = (f32[32,32]{0,1:T(8,128)S(1)}, f32[32]{0:T(128)S(1)}) all-reduce(f32[32,32]{0,1:T(8,128)S(1)} %convolution_bitcast_fusion, f32[32]{0:T(128)S(1)} %fusion.20), channel_id=1, replica_groups=mesh['gx'=4,'gy'=8] {'gx','gy'}, use_global_device_ids=true, to_apply=%region_1.2 | all-reduce | flops 1056 | bytes 8448 | tf_op jit(solution)/shard_map/psum | solution.py:62
  164.6 2.9 %cholesky.16 = f32[32,32]{1,0:T(8,128)S(1)} custom-call(f32[32,32]{1,0:T(8,128)S(1)} %fusion.31), custom_call_target="Cholesky" | custom-call | tf_op jit(solution)/shard_map/jit(cholesky)/cholesky | solution.py:63
  168.9 2.4 %custom-call.10 = f32[1,32,32]{1,2,0:T(8,128)S(1)} custom-call(f32[1,32,32]{2,1,0:T(8,128)S(1)} %fusion.28), custom_call_target="InvertDiagBlocksLowerTriangular" | custom-call | tf_op jit(solution)/shard_map/jit(_cho_solve)/triangular_solve | solution.py:64
  174.0 3.0 %fusion.11 = f32[3,3072]{0,1:T(8,128)} fusion(f32[3,3072]{0,1:T(8,128)S(1)} %scatter_custom_fusion, f32[1,3,3072]{1,2,0:T(8,128)} %copy.42, f32[3072]{0:T(1024)S(1)} %fusion.32), kind=kLoop, calls=%fused_computation.44 | loop fusion | flops 18432 | bytes 122880 | tf_op jit(solution)/shard_map/mul | solution.py:68
  177.0 2.5 %copy.38 = f32[3,3072]{1,0:T(4,128)} copy(f32[3,3072]{0,1:T(8,128)} %fusion.11) | data formatting | bytes 73728
  (54 shorter events, 14.6 us)
Async XLA Ops:
  0.6 171.0 %copy-start = (f32[32,3,3072]{2,0,1:T(8,128)S(1)}, f32[32,3,3072]{2,0,1:T(8,128)}, u32[]{:S(2)}) copy-start(f32[32,3,3072]{2,0,1:T(8,128)} %param.19) | copy-start | bytes 3538948
  1.6 7.2 %collective-permute-start = (f32[1,16,512]{2,0,1:T(1,128)S(1)}, f32[1,16,512]{2,0,1:T(1,128)S(1)}, u32[]{:S(2)}, u32[]{:S(2)}) collective-permute-start(f32[1,16,512]{2,0,1:T(1,128)S(1)} %copy.23), channel_id=1, source_target_pairs={{8,0},{16,8},{24,16},{9,1},{17,9},{25,17},{10,2},{18,10},{26,18},{... | collective-permute-start | bytes 98312 | tf_op jit(solution)/shard_map/ppermute | solution.py:19
  2.9 5.9 %collective-permute-start.1 = (f32[1,16,512]{2,0,1:T(1,128)S(1)}, f32[1,16,512]{2,0,1:T(1,128)S(1)}, u32[]{:S(2)}, u32[]{:S(2)}) collective-permute-start(f32[1,16,512]{2,0,1:T(1,128)S(1)} %copy.25), channel_id=1, source_target_pairs={{0,8},{8,16},{16,24},{1,9},{9,17},{17,25},{2,10},{10,18},{18,26},{... | collective-permute-start | bytes 98312 | tf_op jit(solution)/shard_map/ppermute | solution.py:17
  8.8 13.2 %copy-start.1 = (f32[64,16,512]{2,0,1:T(8,128)}, f32[64,16,512]{2,0,1:T(8,128)S(1)}, u32[]{:S(2)}) copy-start(f32[64,16,512]{2,0,1:T(8,128)S(1)} %copy.24) | copy-start | bytes 6291460
  8.8 6.9 %copy-start.8 = (s32[1,8192]{1,0:T(1,128)S(1)}, s32[1,8192]{1,0:T(1,128)}, u32[]{:S(2)}) copy-start(s32[1,8192]{1,0:T(1,128)} %param.15) | copy-start | bytes 98308
  8.8 8.9 %collective-permute-start.2 = (f32[66,1,512]{2,0,1:T(8,128)S(1)}, f32[66,1,512]{2,0,1:T(8,128)S(1)}, u32[]{:S(2)}, u32[]{:S(2)}) collective-permute-start(f32[66,1,512]{2,0,1:T(8,128)S(1)} %get-tuple-element.13), channel_id=1, source_target_pairs={{1,0},{2,1},{3,2},{4,3},{5,4},{6,5},{7,6},{9,8},{10,9},{11,10},{12... | collective-permute-start | bytes 405512 | tf_op jit(solution)/shard_map/ppermute | solution.py:19
  10.1 11.8 %collective-permute-start.3 = (f32[66,1,512]{2,0,1:T(8,128)S(1)}, f32[66,1,512]{2,0,1:T(8,128)S(1)}, u32[]{:S(2)}, u32[]{:S(2)}) collective-permute-start(f32[66,1,512]{2,0,1:T(8,128)S(1)} %get-tuple-element.12), channel_id=1, source_target_pairs={{0,1},{1,2},{2,3},{3,4},{4,5},{5,6},{6,7},{8,9},{9,10},{10,11},{11... | collective-permute-start | bytes 405512 | tf_op jit(solution)/shard_map/ppermute | solution.py:17
  16.6 8.2 %copy-start.2 = (f32[64,16,512]{2,1,0:T(8,128)S(1)}, f32[64,16,512]{2,1,0:T(8,128)}, u32[]{:S(2)}) copy-start(f32[64,16,512]{2,1,0:T(8,128)} %param.11) | copy-start | bytes 6291460
  16.6 8.2 %copy-start.4 = (f32[64,16,512]{2,1,0:T(8,128)S(1)}, f32[64,16,512]{2,1,0:T(8,128)}, u32[]{:S(2)}) copy-start(f32[64,16,512]{2,1,0:T(8,128)} %param.12) | copy-start | bytes 6291460
  24.8 11.3 %copy-start.7 = (f32[3,3072]{1,0:T(4,128)S(1)}, f32[3,3072]{1,0:T(4,128)}, u32[]{:S(2)}) copy-start(f32[3,3072]{1,0:T(4,128)} %param.17) | copy-start | bytes 110596
  31.8 6.1 %collective-permute-start.4 = (f32[1,16,512]{2,0,1:T(1,128)S(1)}, f32[1,16,512]{2,0,1:T(1,128)S(1)}, u32[]{:S(2)}, u32[]{:S(2)}) collective-permute-start(f32[1,16,512]{2,0,1:T(1,128)S(1)} %get-tuple-element.15), channel_id=1, source_target_pairs={{8,0},{16,8},{24,16},{9,1},{17,9},{25,17},{10,2},{18,10},{26,18},{... | collective-permute-start | bytes 98312 | tf_op jit(solution)/shard_map/ppermute | solution.py:19
  33.1 4.8 %collective-permute-start.5 = (f32[1,16,512]{2,0,1:T(1,128)S(1)}, f32[1,16,512]{2,0,1:T(1,128)S(1)}, u32[]{:S(2)}, u32[]{:S(2)}) collective-permute-start(f32[1,16,512]{2,0,1:T(1,128)S(1)} %get-tuple-element.14), channel_id=1, source_target_pairs={{0,8},{8,16},{16,24},{1,9},{9,17},{17,25},{2,10},{10,18},{18,26},{... | collective-permute-start | bytes 98312 | tf_op jit(solution)/shard_map/ppermute | solution.py:17
  37.8 6.7 %copy-start.6 = (f32[32,3,3072]{2,0,1:T(8,128)S(1)}, f32[32,3,3072]{2,0,1:T(8,128)}, u32[]{:S(2)}) copy-start(f32[32,3,3072]{2,0,1:T(8,128)} %param.18) | copy-start | bytes 3538948
  37.9 8.6 %collective-permute-start.6 = (f32[66,1,512]{2,0,1:T(8,128)S(1)}, f32[66,1,512]{2,0,1:T(8,128)S(1)}, u32[]{:S(2)}, u32[]{:S(2)}) collective-permute-start(f32[66,1,512]{2,0,1:T(8,128)S(1)} %get-tuple-element.11), channel_id=1, source_target_pairs={{1,0},{2,1},{3,2},{4,3},{5,4},{6,5},{7,6},{9,8},{10,9},{11,10},{12... | collective-permute-start | bytes 405512 | tf_op jit(solution)/shard_map/ppermute | solution.py:19
  39.3 11.3 %collective-permute-start.7 = (f32[66,1,512]{2,0,1:T(8,128)S(1)}, f32[66,1,512]{2,0,1:T(8,128)S(1)}, u32[]{:S(2)}, u32[]{:S(2)}) collective-permute-start(f32[66,1,512]{2,0,1:T(8,128)S(1)} %get-tuple-element.10), channel_id=1, source_target_pairs={{0,1},{1,2},{2,3},{3,4},{4,5},{5,6},{6,7},{8,9},{9,10},{10,11},{11... | collective-permute-start | bytes 405512 | tf_op jit(solution)/shard_map/ppermute | solution.py:17
  45.6 7.9 %copy-start.3 = (f32[64,16,512]{2,1,0:T(8,128)S(1)}, f32[64,16,512]{2,1,0:T(8,128)}, u32[]{:S(2)}) copy-start(f32[64,16,512]{2,1,0:T(8,128)} %param.11) | copy-start | bytes 6291460
  45.6 7.9 %copy-start.5 = (f32[64,16,512]{2,1,0:T(8,128)S(1)}, f32[64,16,512]{2,1,0:T(8,128)}, u32[]{:S(2)}) copy-start(f32[64,16,512]{2,1,0:T(8,128)} %param.12) | copy-start | bytes 6291460
  60.4 3.1 %copy-start.9 = (f32[3,1024]{1,0:T(4,128)S(1)}, f32[3,1024]{1,0:T(4,128)}, u32[]{:S(2)}) copy-start(f32[3,1024]{1,0:T(4,128)} %param.14) | copy-start | bytes 36868
  60.5 3.1 %copy-start.10 = (f32[3,1024]{1,0:T(4,128)S(1)}, f32[3,1024]{1,0:T(4,128)}, u32[]{:S(2)}) copy-start(f32[3,1024]{1,0:T(4,128)} %param.13) | copy-start | bytes 36868
where the time goes:
time: 180 us
  blocking collectives  69.8 us (39%)
  local copies, waits for them, and re-layouts  38.8 us (22%)
  other arithmetic  32.4 us (18%)
  starting transfers between devices  22 us (12%)
  waiting for transfers between devices  10.4 us (6%)
  matrix products  4.35 us (2%)
    psum x1, blocking collectives, shards(): gram, projection = lax.psum((gram_local, projection_local), ('gx', 'gy'))  37.7 us
    all_gather x1, blocking collectives, shards(): gathered = lax.all_gather(forces, 'gy', axis=1, tiled=True)  32.1 us
    scatter x1, local copies, waits for them, and re-layouts, shards(): jnp.zeros((3, capacity), jnp.float32).at[:, placed]  21.2 us
    ppermute x4, starting transfers between devices, extended(): lax.ppermute(tail, axis, [(i, (i + 1) % count) for i in range(ends)])  16.7 us
    div x2, other arithmetic, sweep_once(): return (divergence + stencil_sum(padded)) / (6.0 + diagonal)  13.6 us
    unnamed x26, local copies, waits for them, and re-layouts  9.61 us
    ppermute x4, waiting for transfers between devices, extended(): lax.ppermute(tail, axis, [(i, (i + 1) % count) for i in range(ends)])  8.38 us
    concatenate x4, other arithmetic, extended(): jnp.concatenate([lax.ppermute(tail, axis, [(i, (i + 1) % count) for i in...  5.71 us
  transfers between devices with their start and end apart: 8, of which 4 were waited for; matrix products, arithmetic and copies ran while one was open for 3% of the time, Pallas kernels for 0%

commit v1 on v0

v1 whole, which is shorter than its diff:
```python
import functools
import jax
import jax.numpy as jnp
from jax import lax
from jax.experimental import pallas as pl
from jax.experimental.pallas import tpu as pltpu
from jax.sharding import PartitionSpec as P

SWEEPS = 2
LANES = 128
F32 = jnp.float32
BF16 = jnp.bfloat16
VMEM = pl.BlockSpec(memory_space=pltpu.VMEM)
SMEM = pl.BlockSpec(memory_space=pltpu.SMEM)
HIGHEST = lax.Precision.HIGHEST


def pairs(count, parity):
    out = []
    for low in range(parity, count - 1, 2):
        out += [(low, low + 1), (low + 1, low)]
    return out


def swap(head, tail, axis):
    count = lax.axis_size(axis)
    even = lax.axis_index(axis) % 2 == 0
    first = lax.ppermute(jnp.where(even, tail, head), axis, pairs(count, 0))
    second = lax.ppermute(jnp.where(even, head, tail), axis, pairs(count, 1))
    return jnp.where(even, second, first), jnp.where(even, first, second)


def extended(cells, sides, width):
    for axis, dim in sides:
        head = lax.slice_in_dim(cells, 0, width, axis=dim)
        tail = lax.slice_in_dim(cells, cells.shape[dim] - width, cells.shape[dim], axis=dim)
        below, above = swap(head, tail, axis)
        cells = jnp.concatenate([below, cells, above], axis=dim)
    return cells


def stencil_sum(padded):
    padded = jnp.pad(padded, ((0, 0), (0, 0), (1, 1)))
    total = padded[2:, 1:-1, 1:-1] + padded[:-2, 1:-1, 1:-1]
    total = total + padded[1:-1, 2:, 1:-1] + padded[1:-1, :-2, 1:-1]
    total = total + padded[1:-1, 1:-1, 2:] + padded[1:-1, 1:-1, :-2]
    return total


def sweep_once(field, divergence, diagonal):
    padded = extended(field, (("gx", 0), ("gy", 1)), 1)
    return (divergence + stencil_sum(padded)) / (6.0 + diagonal)


def iota(shape, dim):
    return lax.broadcasted_iota(jnp.int32, shape, dim)


def occupied_rows(count, capacity):
    return (iota((1, capacity), 1) < count).astype(F32)


def gram_kernel(count_ref, v_ref, gram_ref):
    columns, capacity = v_ref.shape[1], v_ref.shape[2]
    occupied = occupied_rows(count_ref[0], capacity)
    total = jnp.zeros((columns, columns), F32)
    for c in range(v_ref.shape[0]):
        plain = v_ref[c]
        total += lax.dot_general(
            plain * occupied, plain, (((1,), (1,)), ((), ())), precision=HIGHEST, preferred_element_type=F32
        )
    rows = gram_ref.shape[0]
    gram_ref[...] = jnp.concatenate([total[j : j + rows] for j in range(0, columns, rows)], axis=1)


def gram_tile(counts, v):
    columns = v.shape[1]
    return pl.pallas_call(
        gram_kernel,
        out_shape=jax.ShapeDtypeStruct((columns * columns // LANES, LANES), F32),
        in_specs=[SMEM, VMEM],
        out_specs=VMEM,
        name="gram",
    )(counts, v)


def place_kernel(place_ref, count_ref, got_ref, slot_ref, previous_ref, v_ref, owned_ref, message_ref, gram_scratch):
    own = place_ref[0]
    sources, tiles = got_ref.shape[0], slot_ref.shape[0] // got_ref.shape[0]
    capacity = previous_ref.shape[1]
    high = capacity // LANES
    base = own * capacity

    def one_source(source, total):
        left, right = [], []
        for t in range(tiles):
            slots = slot_ref[pl.ds(source * tiles + t, 1), :]
            at_row = lax.shift_right_arithmetic(slots - base, 7) == iota((high, LANES), 0)
            right.append((jnp.bitwise_and(slots, LANES - 1) == iota((LANES, LANES), 0)).astype(F32))
            rough, fine = [], []
            for c in range(3):
                value = got_ref[source, pl.ds(c * tiles + t, 1), :]
                near = value.astype(BF16).astype(F32)
                rough.append(jnp.where(at_row, near, 0.0))
                fine.append(jnp.where(at_row, value - near, 0.0))
            left.append(jnp.concatenate(rough + fine, axis=0))
        left = jnp.concatenate(left, axis=1).astype(BF16)
        right = jnp.concatenate(right, axis=1).astype(BF16)
        return total + lax.dot_general(
            left, right, (((1,), (1,)), ((), ())), preferred_element_type=F32
        )

    total = lax.fori_loop(0, sources, one_source, jnp.zeros((6 * high, LANES), F32))
    owned = total[: 3 * high] + total[3 * high :]
    summed = jnp.zeros((v_ref.shape[1], LANES), F32)
    for c in range(3):
        for h in range(high):
            lanes = slice(h * LANES, (h + 1) * LANES)
            row = owned[c * high + h : c * high + h + 1]
            owned_ref[c : c + 1, lanes] = row
            held = iota((1, LANES), 1) + h * LANES < count_ref[0]
            residual = jnp.where(held, row - previous_ref[c : c + 1, lanes], 0.0)
            summed += v_ref[c, :, lanes] * residual
    projection = lax.dot_general(
        jnp.ones((8, LANES), F32), summed, (((1,), (1,)), ((), ())), precision=HIGHEST, preferred_element_type=F32
    )
    gram_rows = gram_scratch.shape[0]
    gram_scratch[...] = jnp.sum(got_ref[:, 3 * tiles : 3 * tiles + gram_rows, :], axis=0)
    chunk = gram_scratch[pl.ds(jnp.minimum(own, gram_rows - 1), 1), :]
    message_ref[:, :LANES] = jnp.where(own < gram_rows, chunk, 0.0)
    message_ref[:, LANES:] = jnp.concatenate(
        [projection[:1], jnp.zeros((1, LANES - projection.shape[1]), F32)], axis=1
    )


def place(own, counts, got, slots, previous, v):
    columns = v.shape[1]
    return pl.pallas_call(
        place_kernel,
        out_shape=(
            jax.ShapeDtypeStruct(previous.shape, F32),
            jax.ShapeDtypeStruct((1, 2 * LANES), F32),
        ),
        in_specs=[SMEM, SMEM, VMEM, VMEM, VMEM, VMEM],
        out_specs=(VMEM, VMEM),
        scratch_shapes=[pltpu.VMEM((columns * columns // LANES, LANES), F32)],
        name="place",
    )(own, counts, got, slots, previous, v)


def solve_kernel(groups, count_ref, got_ref, owned_ref, w_ref, coupled_ref):
    columns, capacity = w_ref.shape[1], w_ref.shape[2]
    gram_rows = columns * columns // LANES
    per_group = got_ref.shape[0] // groups
    tile = got_ref[:gram_rows, :LANES]
    for g in range(1, groups):
        tile += got_ref[g * per_group : g * per_group + gram_rows, :LANES]
    projection = jnp.sum(got_ref[:, LANES:], axis=0, keepdims=True)
    gram = jnp.concatenate([tile[:, j : j + columns] for j in range(0, LANES, columns)], axis=0)
    rows, lanes = iota((columns, LANES), 0), iota((columns, LANES), 1)
    right = jnp.sum(jnp.where(rows == lanes, projection, 0.0), axis=1, keepdims=True)
    system = jnp.concatenate([gram, jnp.zeros((columns, LANES - columns), F32)], axis=1)
    system = jnp.where(lanes == columns, right, system)
    for k in range(columns):
        pivot_row = system[k : k + 1] / system[k : k + 1, k : k + 1]
        system = jnp.where(rows == k, pivot_row, system - system[:, k : k + 1] * pivot_row)
    coefficient = -system[:, columns : columns + 1]
    for c in range(3):
        for h in range(capacity // LANES):
            at = slice(h * LANES, (h + 1) * LANES)
            update = jnp.sum(w_ref[c, :, at] * coefficient, axis=0, keepdims=True)
            held = iota((1, LANES), 1) + h * LANES < count_ref[0]
            coupled_ref[c : c + 1, at] = jnp.where(held, owned_ref[c : c + 1, at] + update, 0.0)


def solve(groups, counts, got, owned, w):
    return pl.pallas_call(
        functools.partial(solve_kernel, groups),
        out_shape=jax.ShapeDtypeStruct(owned.shape, F32),
        in_specs=[SMEM, VMEM, VMEM, VMEM],
        out_specs=VMEM,
        name="solve",
    )(counts, got, owned, w)


def exchanged(block, axes):
    count = lax.axis_size(axes)
    sent = jnp.broadcast_to(block[None], (count,) + block.shape)
    return lax.all_to_all(sent, axes, 0, 0, tiled=True)


def shards(
    pressure, divergence, diagonal, normals, traction, slot_of, counts, previous, secant_v, secant_w
):
    v = jnp.transpose(secant_v, (1, 0, 2))
    w = jnp.transpose(secant_w, (1, 0, 2))
    own = lax.axis_index("gy").astype(jnp.int32).reshape(1)
    gram = gram_tile(counts, v)
    field = pressure
    for sweep_index in range(SWEEPS):
        field = sweep_once(field, divergence, diagonal)
    surface = field[:, :, -1].reshape(-1)
    forces = normals * surface[None, :] + traction
    block = jnp.concatenate([forces.reshape(-1, LANES), gram], axis=0)
    got = exchanged(block, "gy")
    owned, message = place(own, counts, got, slot_of.reshape(-1, LANES), previous, v)
    shared = exchanged(message, ("gx", "gy")).reshape(-1, 2 * LANES)
    coupled = solve(lax.axis_size("gx"), counts, shared, owned, w)
    return (field, coupled)


def solution(mesh):
    placed = (
        P("gx", "gy", None),
        P("gx", "gy", None),
        P("gx", "gy", None),
        P(None, ("gx", "gy")),
        P(None, ("gx", "gy")),
        P("gx", None),
        P(("gx", "gy")),
        P(None, ("gx", "gy")),
        P(None, None, ("gx", "gy")),
        P(None, None, ("gx", "gy")),
    )
    return jax.shard_map(
        shards,
        mesh=mesh,
        in_specs=placed,
        out_specs=(P("gx", "gy", None), P(None, ("gx", "gy"))),
        check_vma=False,
    )
```

time: 180 us -> 89.2 us (0.50)
  blocking collectives: 69.8 us -> 16.5 us
  local copies, waits for them, and re-layouts: 38.8 us -> 9.35 us
  other arithmetic: 32.4 us -> 19.6 us
  Pallas kernels: 0 us -> 12.4 us
  matrix products: 4.35 us -> 0 us
  starting transfers between devices: 22 us -> 18.6 us
    psum x1 -> x0, blocking collectives: 37.7 us -> none  [shards(): gram, projection = lax.psum((gram_local, projection_local), ('gx', 'gy'))]
    all_gather x1 -> x0, blocking collectives: 32.1 us -> none  [shards(): gathered = lax.all_gather(forces, 'gy', axis=1, tiled=True)]
    scatter x1 -> x0, local copies, waits for them, and re-layouts: 21.2 us -> none  [shards(): jnp.zeros((3, capacity), jnp.float32).at[:, placed]]
    all_to_all x0 -> x1, blocking collectives: none -> 16.5 us  [exchanged(): return lax.all_to_all(sent, axes, 0, 0, tiled=True)]
    pallas_call x0 -> x3, Pallas kernels: none -> 12.4 us  [the longest x1 4.95 us: solve(): pl.pallas_call(functools.partial(solve_kernel, groups), out_shape=jax.Sha...]
    another operation x5 -> x0, other arithmetic: 6.68 us -> none  [the longest x3 3.6 us: shards(): factor = jnp.linalg.cholesky(gram)]
    mul x2 -> x0, other arithmetic: 6.1 us -> none  [the longest x1 3.06 us: shards(): residual = occupied[None, :] * (owned - previous)]
    ppermute x8, starting transfers between devices: 22 us -> 16.1 us  [the longest x4 13.3 us: swap(): first = lax.ppermute(jnp.where(even, tail, head), axis, pairs(count, 0))]
  transfers between devices with their start and end apart: 8 -> 9, of which waited for: 4 -> 5; matrix products, arithmetic and copies ran while one was open for 3% -> 3% of each run, Pallas kernels for 0% -> 3%
where the time goes in v1:
time: 89.2 us; the launch traced here: 88.8 us
  other arithmetic  19.6 us (22%)
  starting transfers between devices  18.6 us (21%)
  blocking collectives  16.5 us (18%)
  Pallas kernels  12.4 us (14%)
  waiting for transfers between devices  10.8 us (12%)
  local copies, waits for them, and re-layouts  9.35 us (10%)
  between operations  1.61 us (2%)
    all_to_all x1, blocking collectives, exchanged(): return lax.all_to_all(sent, axes, 0, 0, tiled=True)  16.5 us
    div x2, other arithmetic, sweep_once(): return (divergence + stencil_sum(padded)) / (6.0 + diagonal)  13.6 us
    ppermute x4, starting transfers between devices, swap(): first = lax.ppermute(jnp.where(even, tail, head), axis, pairs(count, 0))  13.3 us
    unnamed x23, local copies, waits for them, and re-layouts  7.32 us
    ppermute x4, waiting for transfers between devices, swap(): first = lax.ppermute(jnp.where(even, tail, head), axis, pairs(count, 0))  6.15 us
    concatenate x2, other arithmetic, extended(): cells = jnp.concatenate([below, cells, above], axis=dim)  5.7 us
    pallas_call x1, Pallas kernels, solve(): pl.pallas_call(functools.partial(solve_kernel, groups), out_shape=jax.Sha...  4.95 us
    all_to_all x1, waiting for transfers between devices, exchanged(): return lax.all_to_all(sent, axes, 0, 0, tiled=True)  4.64 us
  transfers between devices with their start and end apart: 9, of which 5 were waited for; matrix products, arithmetic and copies ran while one was open for 3% of the time, Pallas kernels for 3%

profile of v1, /device:TPU:0, one launch (start us, length us, event | category | flops | bytes accessed | tf_op | source)
XLA Modules:
  0.0 88.8 jit_solution(968389711521782293)
XLA Ops:
  0.6 2.8 %copy.14 = f32[64,16,512]{2,0,1:T(8,128)S(1)} copy(f32[64,16,512]{2,1,0:T(8,128)} %param.10) | data formatting | bytes 4194304 | tf_op args[0]
  3.5 0.7 collective-permute-start.1
  4.2 4.4 %collective-permute-start = (f32[1,16,512]{2,0,1:T(1,128)S(1)}, f32[1,16,512]{2,0,1:T(1,128)S(1)}, u32[]{:S(2)}, u32[]{:S(2)}) collective-permute-start(f32[1,16,512]{2,0,1:T(1,128)S(1)} %get-tuple-element.17), channel_id=1, source_target_pairs={{0,8},{8,0},{16,24},{24,16},{1,9},{9,1},{17,25},{25,17},{2,10},{10... | collective-permute-start | bytes 98312 | tf_op jit(solution)/shard_map/ppermute | solution.py:28
  8.6 0.9 collective-permute-done
  9.5 1.6 %collective-permute-start.2 = (f32[66,1,512]{2,0,1:T(8,128)S(1)}, f32[66,1,512]{2,0,1:T(8,128)S(1)}, u32[]{:S(2)}, u32[]{:S(2)}) collective-permute-start(f32[66,1,512]{2,0,1:T(8,128)S(1)} %broadcast_select_fusion.7), channel_id=1, source_target_pairs={{0,1},{1,0},{2,3},{3,2},{4,5},{5,4},{6,7},{7,6},{8,9},{9,8},{10,11... | collective-permute-start | bytes 405512 | tf_op jit(solution)/shard_map/ppermute | solution.py:28
  11.8 4.3 %collective-permute-done.2 = f32[66,1,512]{2,0,1:T(8,128)S(1)} collective-permute-done((f32[66,1,512]{2,0,1:T(8,128)S(1)}, f32[66,1,512]{2,0,1:T(8,128)S(1)}, u32[]{:S(2)}, u32[]{:S(2)}) %collective-permute-start.2) | collective-permute-done | bytes 135200 | tf_op jit(solution)/shard_map/ppermute | solution.py:28
  16.1 2.8 %select_maximum_fusion.4 = f32[66,18,514]{2,0,1:T(8,128)S(1)} fusion(f32[66,1,512]{2,0,1:T(8,128)S(1)} %get-tuple-element.21, f32[66,1,512]{2,0,1:T(8,128)S(1)} %get-tuple-element.20, f32[1,16,512]{2,0,1:T(1,128)S(1)} %bitcast.31, f32[64,16,512]{2,0,1:T(8,128)S(1)} %copy.14, f32[1,16,512]{2,0,1:T(1,128)S(1)} %bitcast.28), kind=kLoop, calls=%fused_computation.6 | loop fusion | flops 7327584 | bytes 4875552 | tf_op jit(solution)/shard_map/concatenate | solution.py:38
  19.0 6.8 %fusion.7 = f32[64,16,512]{2,0,1:T(8,128)S(1)} fusion(f32[66,18,514]{2,0,1:T(8,128)S(1)} %select_maximum_fusion.4, f32[66,1,512]{2,0,1:T(8,128)S(1)} %get-tuple-element.20, f32[1,16,512]{2,0,1:T(1,128)S(1)} %bitcast.32, f32[64,16,512]{2,0,1:T(8,128)} %copy-done, f32[1,16,512]{2,0,1:T(1,128)S(1)} %bitcast.29, f32[66,1,512]{2,0,1:T(8,128)S(1)} %get-tuple-element.21, ...), kind=kLoop, calls=%fused_computation.28 | loop fusion | flops 8388608 | bytes 12918784 | tf_op jit(solution)/shard_map/div | solution.py:52
  25.9 0.7 collective-permute-start.5
  26.5 3.0 %collective-permute-start.4 = (f32[1,16,512]{2,0,1:T(1,128)S(1)}, f32[1,16,512]{2,0,1:T(1,128)S(1)}, u32[]{:S(2)}, u32[]{:S(2)}) collective-permute-start(f32[1,16,512]{2,0,1:T(1,128)S(1)} %get-tuple-element.15), channel_id=1, source_target_pairs={{0,8},{8,0},{16,24},{24,16},{1,9},{9,1},{17,25},{25,17},{2,10},{10... | collective-permute-start | bytes 98312 | tf_op jit(solution)/shard_map/ppermute | solution.py:28
  29.6 0.9 collective-permute-done.4
  30.5 4.3 %collective-permute-start.6 = (f32[66,1,512]{2,0,1:T(8,128)S(1)}, f32[66,1,512]{2,0,1:T(8,128)S(1)}, u32[]{:S(2)}, u32[]{:S(2)}) collective-permute-start(f32[66,1,512]{2,0,1:T(8,128)S(1)} %broadcast_select_fusion.3), channel_id=1, source_target_pairs={{0,1},{1,0},{2,3},{3,2},{4,5},{5,4},{6,7},{7,6},{8,9},{9,8},{10,11... | collective-permute-start | bytes 405512 | tf_op jit(solution)/shard_map/ppermute | solution.py:28
  34.8 0.8 collective-permute-start.7
  36.3 3.0 %gram.1 = f32[8,128]{1,0:T(8,128)} custom-call(s32[1]{0:T(128)S(6)} %copy.32.count_ref, f32[3,32,3072]{2,1,0:T(8,128)} %bitcast.18), custom_call_target="tpu_custom_call" | custom-call | tf_op jit(solution)/shard_map/gram/pallas_call | solution.py:78
  39.5 2.8 %select_maximum_fusion = f32[66,18,514]{2,0,1:T(8,128)S(1)} fusion(f32[66,1,512]{2,0,1:T(8,128)S(1)} %get-tuple-element.19, f32[66,1,512]{2,0,1:T(8,128)S(1)} %get-tuple-element.18, f32[1,16,512]{2,0,1:T(1,128)S(1)} %bitcast.25, f32[64,16,512]{2,0,1:T(8,128)S(1)} %fusion.7, f32[1,16,512]{2,0,1:T(1,128)S(1)} %bitcast.22), kind=kLoop, calls=%fused_computation.2 | loop fusion | flops 7327584 | bytes 4875552 | tf_op jit(solution)/shard_map/concatenate | solution.py:38
  42.4 6.8 %fusion.2 = f32[64,16,512]{2,0,1:T(8,128)S(1)} fusion(f32[66,18,514]{2,0,1:T(8,128)S(1)} %select_maximum_fusion, f32[66,1,512]{2,0,1:T(8,128)S(1)} %get-tuple-element.18, f32[1,16,512]{2,0,1:T(1,128)S(1)} %bitcast.26, f32[64,16,512]{2,0,1:T(8,128)S(1)} %fusion.7, f32[1,16,512]{2,0,1:T(1,128)S(1)} %bitcast.23, f32[66,1,512]{2,0,1:T(8,128)S(1)} %get-tuple-element.19, ...), kind=kLoop, calls=%fused_computation.13 | loop fusion | flops 8388608 | bytes 12918784 | tf_op jit(solution)/shard_map/div | solution.py:52
  49.2 1.3 %copy-done.1 = f32[64,16,512]{2,0,1:T(8,128)} copy-done((f32[64,16,512]{2,0,1:T(8,128)}, f32[64,16,512]{2,0,1:T(8,128)S(1)}, u32[]{:S(2)}) %copy-start.1) | copy-done | bytes 2097176
  51.4 16.5 %all_to_all.10.got_ref = f32[8,32,128]{2,1,0:T(8,128)} all-to-all(f32[8,32,128]{2,1,0:T(8,128)S(1)} %broadcast_in_dim.6), channel_id=1, replica_groups=mesh['gx'=4,'gy'=8] {'gy'}, dimensions={0} | all-to-all | bytes 262144 | tf_op jit(solution)/shard_map/all_to_all | solution.py:189
  67.9 4.4 %place.1 = (f32[3,3072]{1,0:T(4,128)}, f32[1,256]{1,0:T(1,128)}) custom-call(s32[1]{0:T(128)} %bitcast.place_ref, s32[1]{0:T(128)S(6)} %copy.32.count_ref, f32[8,32,128]{2,1,0:T(8,128)} %all_to_all.10.got_ref, s32[64,128]{1,0:T(8,128)} %bitcast.34, f32[3,3072]{1,0:T(4,128)} %previous_ref.1, f32[3,32,3072]{2,1,0:T(8,128)} %bitcast.19), custom_call_target="tpu_custom_call" | custom-call | tf_op jit(solution)/shard_map/place/pallas_call | solution.py:138
  72.3 1.2 %broadcast_in_dim.16 = f32[32,1,256]{2,1,0:T(1,128)} broadcast(f32[256]{0:T(256)} %bitcast.39), dimensions={2} | broadcast | bytes 33792 | tf_op jit(solution)/shard_map/broadcast_in_dim | solution.py:188
  73.5 2.6 %all-to-all-start.1 = ((f32[32,1,256]{2,1,0:T(1,128)}), f32[32,1,256]{2,1,0:T(1,128)S(1)}, u32[]{:S(2)}, u32[]{:S(2)}) async-start(f32[32,1,256]{2,1,0:T(1,128)} %broadcast_in_dim.16), calls=%async_computation.1 | async-start | bytes 65536 | tf_op jit(solution)/shard_map/all_to_all | solution.py:189
  76.1 2.5 %copy.21 = f32[64,16,512]{2,1,0:T(8,128)} copy(f32[64,16,512]{2,0,1:T(8,128)S(1)} %copy-done.2) | data formatting | bytes 4194304
  78.6 4.6 %all-to-all-done.1 = f32[32,1,256]{2,1,0:T(1,128)S(1)} async-done(((f32[32,1,256]{2,1,0:T(1,128)}), f32[32,1,256]{2,1,0:T(1,128)S(1)}, u32[]{:S(2)}, u32[]{:S(2)}) %all-to-all-start.1) | async-done | bytes 32800 | tf_op jit(solution)/shard_map/all_to_all | solution.py:189
  83.9 4.9 %solve.1 = f32[3,3072]{1,0:T(4,128)} custom-call(s32[1]{0:T(128)S(6)} %copy.32.count_ref, f32[32,256]{1,0:T(8,128)} %bitcast.33, f32[3,3072]{1,0:T(4,128)} %get-tuple-element.5.owned_ref, f32[3,32,3072]{2,1,0:T(8,128)} %bitcast.20), custom_call_target="tpu_custom_call" | custom-call | tf_op jit(solution)/shard_map/solve/pallas_call | solution.py:177
  (43 shorter events, 2.6 us)
Async XLA Ops:
  3.5 12.6 %copy-start = (f32[64,16,512]{2,0,1:T(8,128)}, f32[64,16,512]{2,0,1:T(8,128)S(1)}, u32[]{:S(2)}) copy-start(f32[64,16,512]{2,0,1:T(8,128)S(1)} %copy.14) | copy-start | bytes 6291460
  3.5 5.1 %collective-permute-start.1 = (f32[1,16,512]{2,0,1:T(1,128)S(1)}, f32[1,16,512]{2,0,1:T(1,128)S(1)}, u32[]{:S(2)}, u32[]{:S(2)}) collective-permute-start(f32[1,16,512]{2,0,1:T(1,128)S(1)} %get-tuple-element.16), channel_id=1, source_target_pairs={{8,16},{16,8},{9,17},{17,9},{10,18},{18,10},{11,19},{19,11},{12,20... | collective-permute-start | bytes 98312 | tf_op jit(solution)/shard_map/ppermute | solution.py:29
  4.2 5.3 %collective-permute-start = (f32[1,16,512]{2,0,1:T(1,128)S(1)}, f32[1,16,512]{2,0,1:T(1,128)S(1)}, u32[]{:S(2)}, u32[]{:S(2)}) collective-permute-start(f32[1,16,512]{2,0,1:T(1,128)S(1)} %get-tuple-element.17), channel_id=1, source_target_pairs={{0,8},{8,0},{16,24},{24,16},{1,9},{9,1},{17,25},{25,17},{2,10},{10... | collective-permute-start | bytes 98312 | tf_op jit(solution)/shard_map/ppermute | solution.py:28
  9.5 6.5 %collective-permute-start.2 = (f32[66,1,512]{2,0,1:T(8,128)S(1)}, f32[66,1,512]{2,0,1:T(8,128)S(1)}, u32[]{:S(2)}, u32[]{:S(2)}) collective-permute-start(f32[66,1,512]{2,0,1:T(8,128)S(1)} %broadcast_select_fusion.7), channel_id=1, source_target_pairs={{0,1},{1,0},{2,3},{3,2},{4,5},{5,4},{6,7},{7,6},{8,9},{9,8},{10,11... | collective-permute-start | bytes 405512 | tf_op jit(solution)/shard_map/ppermute | solution.py:28
  11.1 4.9 %collective-permute-start.3 = (f32[66,1,512]{2,0,1:T(8,128)S(1)}, f32[66,1,512]{2,0,1:T(8,128)S(1)}, u32[]{:S(2)}, u32[]{:S(2)}) collective-permute-start(f32[66,1,512]{2,0,1:T(8,128)S(1)} %get-tuple-element.11), channel_id=1, source_target_pairs={{1,2},{2,1},{3,4},{4,3},{5,6},{6,5},{9,10},{10,9},{11,12},{12,11},... | collective-permute-start | bytes 405512 | tf_op jit(solution)/shard_map/ppermute | solution.py:29
  16.1 2.9 %copy-start.3 = (f32[64,16,512]{2,1,0:T(8,128)S(1)}, f32[64,16,512]{2,1,0:T(8,128)}, u32[]{:S(2)}) copy-start(f32[64,16,512]{2,1,0:T(8,128)} %param.11) | copy-start | bytes 6291460
  16.1 2.9 %copy-start.5 = (f32[64,16,512]{2,1,0:T(8,128)S(1)}, f32[64,16,512]{2,1,0:T(8,128)}, u32[]{:S(2)}) copy-start(f32[64,16,512]{2,1,0:T(8,128)} %param.12) | copy-start | bytes 6291460
  25.9 3.7 %collective-permute-start.5 = (f32[1,16,512]{2,0,1:T(1,128)S(1)}, f32[1,16,512]{2,0,1:T(1,128)S(1)}, u32[]{:S(2)}, u32[]{:S(2)}) collective-permute-start(f32[1,16,512]{2,0,1:T(1,128)S(1)} %get-tuple-element.14), channel_id=1, source_target_pairs={{8,16},{16,8},{9,17},{17,9},{10,18},{18,10},{11,19},{19,11},{12,20... | collective-permute-start | bytes 98312 | tf_op jit(solution)/shard_map/ppermute | solution.py:29
  26.5 3.9 %collective-permute-start.4 = (f32[1,16,512]{2,0,1:T(1,128)S(1)}, f32[1,16,512]{2,0,1:T(1,128)S(1)}, u32[]{:S(2)}, u32[]{:S(2)}) collective-permute-start(f32[1,16,512]{2,0,1:T(1,128)S(1)} %get-tuple-element.15), channel_id=1, source_target_pairs={{0,8},{8,0},{16,24},{24,16},{1,9},{9,1},{17,25},{25,17},{2,10},{10... | collective-permute-start | bytes 98312 | tf_op jit(solution)/shard_map/ppermute | solution.py:28
  30.5 9.0 %collective-permute-start.6 = (f32[66,1,512]{2,0,1:T(8,128)S(1)}, f32[66,1,512]{2,0,1:T(8,128)S(1)}, u32[]{:S(2)}, u32[]{:S(2)}) collective-permute-start(f32[66,1,512]{2,0,1:T(8,128)S(1)} %broadcast_select_fusion.3), channel_id=1, source_target_pairs={{0,1},{1,0},{2,3},{3,2},{4,5},{5,4},{6,7},{7,6},{8,9},{9,8},{10,11... | collective-permute-start | bytes 405512 | tf_op jit(solution)/shard_map/ppermute | solution.py:28
  34.8 4.7 %collective-permute-start.7 = (f32[66,1,512]{2,0,1:T(8,128)S(1)}, f32[66,1,512]{2,0,1:T(8,128)S(1)}, u32[]{:S(2)}, u32[]{:S(2)}) collective-permute-start(f32[66,1,512]{2,0,1:T(8,128)S(1)} %get-tuple-element.8), channel_id=1, source_target_pairs={{1,2},{2,1},{3,4},{4,3},{5,6},{6,5},{9,10},{10,9},{11,12},{12,11},... | collective-permute-start | bytes 405512 | tf_op jit(solution)/shard_map/ppermute | solution.py:29
  39.5 2.9 %copy-start.4 = (f32[64,16,512]{2,1,0:T(8,128)S(1)}, f32[64,16,512]{2,1,0:T(8,128)}, u32[]{:S(2)}) copy-start(f32[64,16,512]{2,1,0:T(8,128)} %param.11) | copy-start | bytes 6291460
  39.5 2.9 %copy-start.6 = (f32[64,16,512]{2,1,0:T(8,128)S(1)}, f32[64,16,512]{2,1,0:T(8,128)}, u32[]{:S(2)}) copy-start(f32[64,16,512]{2,1,0:T(8,128)} %param.12) | copy-start | bytes 6291460
  42.4 8.9 %copy-start.8 = (f32[3,1024]{1,0:T(4,128)S(1)}, f32[3,1024]{1,0:T(4,128)}, u32[]{:S(2)}) copy-start(f32[3,1024]{1,0:T(4,128)} %param.14) | copy-start | bytes 36868
  42.4 8.9 %copy-start.9 = (f32[3,1024]{1,0:T(4,128)S(1)}, f32[3,1024]{1,0:T(4,128)}, u32[]{:S(2)}) copy-start(f32[3,1024]{1,0:T(4,128)} %param.13) | copy-start | bytes 36868
  42.4 8.9 %copy-start.7 = (f32[8,128]{1,0:T(8,128)S(1)}, f32[8,128]{1,0:T(8,128)}, u32[]{:S(2)}) copy-start(f32[8,128]{1,0:T(8,128)} %gram.1) | copy-start | bytes 12292
  49.2 1.3 %copy-start.1 = (f32[64,16,512]{2,0,1:T(8,128)}, f32[64,16,512]{2,0,1:T(8,128)S(1)}, u32[]{:S(2)}) copy-start(f32[64,16,512]{2,0,1:T(8,128)S(1)} %fusion.2) | copy-start | bytes 6291460
  50.7 25.4 %copy-start.2 = (f32[64,16,512]{2,0,1:T(8,128)S(1)}, f32[64,16,512]{2,0,1:T(8,128)}, u32[]{:S(2)}) copy-start(f32[64,16,512]{2,0,1:T(8,128)} %copy-done.1) | copy-start | bytes 6291460
  73.5 9.8 %all-to-all-start.1 = ((f32[32,1,256]{2,1,0:T(1,128)}), f32[32,1,256]{2,1,0:T(1,128)S(1)}, u32[]{:S(2)}, u32[]{:S(2)}) async-start(f32[32,1,256]{2,1,0:T(1,128)} %broadcast_in_dim.16), calls=%async_computation.1 | async-start | bytes 65536 | tf_op jit(solution)/shard_map/all_to_all | solution.py:189

commit v2 on v1

--- a/solution.py
+++ b/solution.py
@@ -6,7 +6,6 @@
 from jax.experimental.pallas import tpu as pltpu
 from jax.sharding import PartitionSpec as P
 
-SWEEPS = 2
 LANES = 128
 F32 = jnp.float32
 BF16 = jnp.bfloat16
@@ -28,28 +27,6 @@
     first = lax.ppermute(jnp.where(even, tail, head), axis, pairs(count, 0))
     second = lax.ppermute(jnp.where(even, head, tail), axis, pairs(count, 1))
     return jnp.where(even, second, first), jnp.where(even, first, second)
-
-
-def extended(cells, sides, width):
-    for axis, dim in sides:
-        head = lax.slice_in_dim(cells, 0, width, axis=dim)
-        tail = lax.slice_in_dim(cells, cells.shape[dim] - width, cells.shape[dim], axis=dim)
-        below, above = swap(head, tail, axis)
-        cells = jnp.concatenate([below, cells, above], axis=dim)
-    return cells
-
-
-def stencil_sum(padded):
-    padded = jnp.pad(padded, ((0, 0), (0, 0), (1, 1)))
-    total = padded[2:, 1:-1, 1:-1] + padded[:-2, 1:-1, 1:-1]
-    total = total + padded[1:-1, 2:, 1:-1] + padded[1:-1, :-2, 1:-1]
-    total = total + padded[1:-1, 1:-1, 2:] + padded[1:-1, 1:-1, :-2]
-    return total
-
-
-def sweep_once(field, divergence, diagonal):
-    padded = extended(field, (("gx", 0), ("gy", 1)), 1)
-    return (divergence + stencil_sum(padded)) / (6.0 + diagonal)
 
 
 def iota(shape, dim):
@@ -84,12 +61,152 @@
     )(counts, v)
 
 
-def place_kernel(place_ref, count_ref, got_ref, slot_ref, previous_ref, v_ref, owned_ref, message_ref, gram_scratch):
+def slab_kernel(pressure_ref, divergence_ref, diagonal_ref, planes_ref):
+    cx, cy, width = pressure_ref.shape
+    step = LANES // cy
+    for k in range(cx // step):
+        lanes = slice(k * LANES, (k + 1) * LANES)
+        turned = [
+            ref[k * step : (k + 1) * step].reshape(LANES, width).T
+            for ref in (pressure_ref, divergence_ref, diagonal_ref)
+        ]
+        for row, (which, back) in enumerate(((0, 1), (0, 2), (0, 3), (1, 1), (1, 2), (2, 1), (2, 2))):
+            line = turned[which][width - back : width - back + 1]
+            planes_ref[row : row + 1, lanes] = 1.0 / (6.0 + line) if which == 2 else line
+        planes_ref[7:8, lanes] = jnp.zeros((1, LANES), F32)
+
+
+def slab(pressure, divergence, diagonal):
+    cx, cy, cz = pressure.shape
+    last = pl.BlockSpec((cx, cy, LANES), lambda i: (0, 0, cz // LANES - 1))
+    return pl.pallas_call(
+        slab_kernel,
+        grid=(1,),
+        out_shape=jax.ShapeDtypeStruct((8, cx * cy), F32),
+        in_specs=[last, last, last],
+        out_specs=pl.BlockSpec((8, cx * cy), lambda i: (0, 0)),
+        name="slab",
+    )(pressure, divergence, diagonal)
+
+
+def rolled(block, shift, axis=1):
+    return pltpu.roll(block, shift % block.shape[axis], axis)
+
+
+def packed(parts, cy):
+    place = lax.rem(iota(parts[0].shape, 1) + 2, cy) // 4
+    out = parts[0]
+    for k in range(1, 4):
+        out = jnp.where(place == k, rolled(parts[k], 4 * k), out)
+    return out
+
+
+def surface_kernel(cy, planes_ref, below_ref, above_ref, normals_ref, traction_ref, gram_ref, out_ref, scratch):
+    rows = planes_ref.shape[1]
+    tiles = rows // LANES
+    ext = jnp.concatenate([below_ref[...], planes_ref[...], above_ref[...]], axis=1)
+    y = lax.rem(iota(ext.shape, 1), cy)
+
+    def around(block):
+        inner = jnp.where(y == 0, 0.0, rolled(block, 1)) + jnp.where(y == cy - 1, 0.0, rolled(block, -1))
+        return rolled(block, cy) + rolled(block, -cy) + inner
+
+    def line(row):
+        return ext[row : row + 1]
+
+    near = around(ext)
+    once = (line(3) + near[0:1] + line(1)) * line(5)
+    beneath = (line(4) + near[1:2] + line(0) + line(2)) * line(6)
+    twice = (line(3) + around(jnp.broadcast_to(once, ext.shape))[0:1] + beneath) * line(5)
+    surface = twice[:, LANES : LANES + rows]
+    normals = normals_ref[...]
+    forces = normals * surface + traction_ref[...]
+    own = slice(LANES, LANES + rows)
+    wide = lambda part: jnp.broadcast_to(part, (8, rows))
+    first = packed(
+        [wide(normals[0:1]), wide(normals[1:2]), wide(normals[2:3]), wide(line(0)[:, own])], cy
+    )
+    second = packed(
+        [wide(part[:, own]) for part in (line(1), once, line(5), line(5) * line(6))], cy
+    )
+    for t in range(tiles):
+        lanes = slice(t * LANES, (t + 1) * LANES)
+        for c in range(3):
+            scratch[c * tiles + t : c * tiles + t + 1] = forces[c : c + 1, lanes]
+        scratch[3 * tiles + t : 3 * tiles + t + 1] = first[0:1, lanes]
+        scratch[4 * tiles + t : 4 * tiles + t + 1] = second[0:1, lanes]
+    low, high = ext[:, :LANES], ext[:, LANES + rows :]
+    lane = iota((8, LANES), 1)
+    side = jnp.where(
+        lane < cy,
+        rolled(low, cy)[0:1],
+        jnp.where(
+            lane < 2 * cy,
+            rolled(high, cy)[0:1],
+            jnp.where(lane < 3 * cy, rolled(low, 3 * cy)[5:6], rolled(high, 3 * cy)[5:6]),
+        ),
+    )
+    scratch[5 * tiles : 5 * tiles + 8] = side
+    scratch[5 * tiles + 8 :] = gram_ref[...]
+    for d in range(out_ref.shape[0]):
+        out_ref[d] = scratch[...]
+
+
+def surface_message(count, cy, planes, below, above, normals, traction, gram):
+    rows = 5 * planes.shape[1] // LANES + 8 + gram.shape[0]
+    return pl.pallas_call(
+        functools.partial(surface_kernel, cy),
+        out_shape=jax.ShapeDtypeStruct((count, rows, LANES), F32),
+        in_specs=[VMEM] * 6,
+        out_specs=VMEM,
+        scratch_shapes=[pltpu.VMEM((rows, LANES), F32)],
+        name="surface",
+    )(planes, below, above, normals, traction, gram)
+
+
+def corrected(cy, got_ref, tiles, forces_ref):
+    sources = got_ref.shape[0]
+    rows = tiles * LANES
+
+    def plane(index):
+        return jnp.concatenate([got_ref[:, index * tiles + t, :] for t in range(tiles)], axis=1)
+
+    def across(block):
+        y, source = lax.rem(iota(block.shape, 1), cy), iota(block.shape, 0)
+        before = rolled(rolled(block, 1, 0), 1 - cy)
+        after = rolled(rolled(block, -1, 0), cy - 1)
+        return jnp.where(
+            (y == 0) & (source > 0), before, jnp.where((y == cy - 1) & (source < sources - 1), after, 0.0)
+        )
+
+    first, second = plane(3), plane(4)
+    y = lax.rem(iota(first.shape, 1), cy)
+    lane = iota(first.shape, 1)
+    edge = lax.rem(y + 2, cy) < 4
+    ratio = jnp.where(edge, rolled(second, -8), 0.0)
+    both = jnp.where(edge, rolled(second, -12), 0.0)
+    delta = ratio * across(rolled(first, -12))
+    side = got_ref[:, 5 * tiles, :]
+    side = rolled(side, -2 * cy) * across(side)
+    end = jnp.concatenate([side] + [jnp.zeros_like(side)] * (tiles - 2) + [rolled(side, -2 * cy)], axis=1)
+    total = jnp.where(lane < cy, end, rolled(delta, cy)) + jnp.where(lane >= rows - cy, end, rolled(delta, -cy))
+    total += across(rolled(second, -4) + delta)
+    total += jnp.where(y == 1, rolled(delta, 1), 0.0) + jnp.where(y == cy - 2, rolled(delta, -1), 0.0)
+    change = ratio * total + both * across(second)
+    for c in range(3):
+        normal = jnp.where(edge, rolled(first, -4 * c), 0.0)
+        forces = plane(c) + normal * change
+        for t in range(tiles):
+            forces_ref[c * tiles + t] = forces[:, t * LANES : (t + 1) * LANES]
+
+
+def place_kernel(cy, place_ref, count_ref, got_ref, slot_ref, previous_ref, v_ref, owned_ref, message_ref, gram_scratch, forces_ref):
     own = place_ref[0]
     sources, tiles = got_ref.shape[0], slot_ref.shape[0] // got_ref.shape[0]
     capacity = previous_ref.shape[1]
     high = capacity // LANES
     base = own * capacity
+    corrected(cy, got_ref, tiles, forces_ref)
 
     def one_source(source, total):
         left, right = [], []
@@ -99,7 +216,7 @@
             right.append((jnp.bitwise_and(slots, LANES - 1) == iota((LANES, LANES), 0)).astype(F32))
             rough, fine = [], []
             for c in range(3):
-                value = got_ref[source, pl.ds(c * tiles + t, 1), :]
+                value = forces_ref[c * tiles + t, pl.ds(source, 1), :]
                 near = value.astype(BF16).astype(F32)
                 rough.append(jnp.where(at_row, near, 0.0))
                 fine.append(jnp.where(at_row, value - near, 0.0))
@@ -125,25 +242,33 @@
         jnp.ones((8, LANES), F32), summed, (((1,), (1,)), ((), ())), precision=HIGHEST, preferred_element_type=F32
     )
     gram_rows = gram_scratch.shape[0]
-    gram_scratch[...] = jnp.sum(got_ref[:, 3 * tiles : 3 * tiles + gram_rows, :], axis=0)
+    gram_scratch[...] = jnp.sum(got_ref[:, 5 * tiles + 8 :, :], axis=0)
     chunk = gram_scratch[pl.ds(jnp.minimum(own, gram_rows - 1), 1), :]
-    message_ref[:, :LANES] = jnp.where(own < gram_rows, chunk, 0.0)
-    message_ref[:, LANES:] = jnp.concatenate(
-        [projection[:1], jnp.zeros((1, LANES - projection.shape[1]), F32)], axis=1
-    )
-
-
-def place(own, counts, got, slots, previous, v):
+    message = jnp.concatenate(
+        [
+            jnp.where(own < gram_rows, chunk, 0.0),
+            projection[:1],
+            jnp.zeros((1, LANES - projection.shape[1]), F32),
+        ],
+        axis=1,
+    )
+    message_ref[...] = jnp.broadcast_to(message, message_ref.shape)
+
+
+def place(devices, cy, own, counts, got, slots, previous, v):
     columns = v.shape[1]
     return pl.pallas_call(
-        place_kernel,
+        functools.partial(place_kernel, cy),
         out_shape=(
             jax.ShapeDtypeStruct(previous.shape, F32),
-            jax.ShapeDtypeStruct((1, 2 * LANES), F32),
+            jax.ShapeDtypeStruct((devices, 2 * LANES), F32),
         ),
         in_specs=[SMEM, SMEM, VMEM, VMEM, VMEM, VMEM],
         out_specs=(VMEM, VMEM),
-        scratch_shapes=[pltpu.VMEM((columns * columns // LANES, LANES), F32)],
+        scratch_shapes=[
+            pltpu.VMEM((columns * columns // LANES, LANES), F32),
+            pltpu.VMEM((3 * slots.shape[0] // got.shape[0], got.shape[0], LANES), F32),
+        ],
         name="place",
     )(own, counts, got, slots, previous, v)
 
@@ -183,29 +308,131 @@
     )(counts, got, owned, w)
 
 
-def exchanged(block, axes):
-    count = lax.axis_size(axes)
-    sent = jnp.broadcast_to(block[None], (count,) + block.shape)
-    return lax.all_to_all(sent, axes, 0, 0, tiled=True)
+BIG = pltpu.CompilerParams(vmem_limit_bytes=40 * 1024 * 1024)
+
+
+def shifted(here, low, high):
+    y, z = iota(here.shape, 0), iota(here.shape, 1)
+    before = jnp.where(y == 0, low, rolled(here, 1, 0))
+    after = jnp.where(y == here.shape[0] - 1, high, rolled(here, -1, 0))
+    left = jnp.where(z == 0, 0.0, rolled(here, 1))
+    right = jnp.where(z == here.shape[1] - 1, 0.0, rolled(here, -1))
+    return before + after + left + right
+
+
+def first_kernel(p_ref, d_ref, g_ref, below_ref, above_ref, once_ref, ratio_ref, low_ref, high_ref):
+    cx, cy = p_ref.shape[0], p_ref.shape[1]
+
+    def sweep(before, here, after, source, ratio):
+        return (source + before + after + shifted(here, 0.0, 0.0)) * ratio
+
+    once_ref[0] = sweep(below_ref[1], below_ref[0], p_ref[0], below_ref[2], below_ref[3])
+    once_ref[cx + 1] = sweep(above_ref[1], above_ref[0], p_ref[cx - 1], above_ref[2], above_ref[3])
+
+    def step(x, carry):
+        before, here = carry
+        after = jnp.where(x == cx - 1, above_ref[0], p_ref[jnp.minimum(x + 1, cx - 1)])
+        ratio = 1.0 / (6.0 + g_ref[x])
+        ratio_ref[x] = ratio
+        once_ref[x + 1] = sweep(before, here, after, d_ref[x], ratio)
+        return here, after
+
+    lax.fori_loop(0, cx, step, (below_ref[0], p_ref[0]), unroll=4)
+    for out_ref, y in ((low_ref, 0), (high_ref, cy - 1)):
+        out_ref[:cx] = p_ref[:, y, :]
+        out_ref[cx : 2 * cx] = once_ref[1 : cx + 1, y, :]
+        out_ref[2 * cx : 3 * cx] = ratio_ref[:, y, :]
+        ends = [ref[row, y : y + 1, :] for ref, row in ((below_ref, 0), (above_ref, 0), (below_ref, 3), (above_ref, 3))]
+        out_ref[3 * cx :] = jnp.concatenate(ends + [jnp.zeros((4, p_ref.shape[2]), F32)], axis=0)
+
+
+def first_sweep(p, d, g, below, above):
+    cx, cy, cz = p.shape
+    face = jax.ShapeDtypeStruct((3 * cx + 8, cz), F32)
+    return pl.pallas_call(
+        first_kernel,
+        out_shape=(jax.ShapeDtypeStruct((cx + 2, cy, cz), F32), jax.ShapeDtypeStruct(p.shape, F32), face, face),
+        in_specs=[VMEM] * 5,
+        out_specs=(VMEM,) * 4,
+        compiler_params=BIG,
+        name="first_sweep",
+    )(p, d, g, below, above)
+
+
+def second_kernel(once_ref, ratio_ref, d_ref, low_ref, high_ref, below_ref, above_ref, out_ref, rows_ref):
+    cx, cy, cz = out_ref.shape
+    corners = 3 * cx
+    for side, (own_ref, far_ref) in enumerate(((low_ref, below_ref), (high_ref, above_ref))):
+        rows_ref[side] = far_ref[cx : 2 * cx] + far_ref[2 * cx : 3 * cx] * own_ref[:cx]
+        lacking = own_ref[2 * cx : 3 * cx] * far_ref[:cx]
+        last = own_ref[corners + 3 : corners + 4] * far_ref[corners + 1 : corners + 2]
+        rows_ref[2 + side] = jnp.concatenate([lacking[1:], last], axis=0)
+    y = iota((cy, cz), 0)
+
+    def completed(plane, low, high):
+        return plane + jnp.where(y == 0, low, jnp.where(y == cy - 1, high, 0.0))
+
+    def owed(row, far_row):
+        return [
+            own_ref[row : row + 1] * far_ref[far_row : far_row + 1]
+            for own_ref, far_ref in ((low_ref, below_ref), (high_ref, above_ref))
+        ]
+
+    def chunk(c, carry):
+        before, here = carry
+        rows = [rows_ref[k, pl.ds(8 * c, 8), :] for k in range(4)]
+        for j in range(8):
+            x = 8 * c + j
+            low, high, low_next, high_next = [block[j : j + 1] for block in rows]
+            after = completed(once_ref[x + 2], low_next, high_next)
+            out_ref[x] = (d_ref[x] + before + after + shifted(here, low, high)) * ratio_ref[x]
+            before, here = here, after
+        return before, here
+
+    start = (
+        completed(once_ref[0], *owed(corners + 2, corners)),
+        completed(once_ref[1], *owed(2 * cx, 0)),
+    )
+    lax.fori_loop(0, cx // 8, chunk, start)
+
+
+def second_sweep(once, ratio, d, low, high, below, above):
+    cx, cy, cz = d.shape
+    return pl.pallas_call(
+        second_kernel,
+        out_shape=jax.ShapeDtypeStruct(d.shape, F32),
+        in_specs=[VMEM] * 7,
+        out_specs=VMEM,
+        scratch_shapes=[pltpu.VMEM((4, cx, cz), F32)],
+        compiler_params=BIG,
+        name="second_sweep",
+    )(once, ratio, d, low, high, below, above)
 
 
 def shards(
     pressure, divergence, diagonal, normals, traction, slot_of, counts, previous, secant_v, secant_w
 ):
+    groups, owners = lax.axis_size("gx"), lax.axis_size("gy")
+    cy = pressure.shape[1]
     v = jnp.transpose(secant_v, (1, 0, 2))
     w = jnp.transpose(secant_w, (1, 0, 2))
     own = lax.axis_index("gy").astype(jnp.int32).reshape(1)
+    planes = slab(pressure, divergence, diagonal)
+    below, above = swap(planes[:, :LANES], planes[:, -LANES:], "gx")
     gram = gram_tile(counts, v)
-    field = pressure
-    for sweep_index in range(SWEEPS):
-        field = sweep_once(field, divergence, diagonal)
-    surface = field[:, :, -1].reshape(-1)
-    forces = normals * surface[None, :] + traction
-    block = jnp.concatenate([forces.reshape(-1, LANES), gram], axis=0)
-    got = exchanged(block, "gy")
-    owned, message = place(own, counts, got, slot_of.reshape(-1, LANES), previous, v)
-    shared = exchanged(message, ("gx", "gy")).reshape(-1, 2 * LANES)
-    coupled = solve(lax.axis_size("gx"), counts, shared, owned, w)
+    block = surface_message(owners, cy, planes, below, above, normals, traction, gram)
+    got = lax.all_to_all(block, "gy", 0, 0, tiled=True)
+    owned, message = place(
+        groups * owners, cy, own, counts, got, slot_of.reshape(-1, LANES), previous, v
+    )
+    shared = lax.all_to_all(message, ("gx", "gy"), 0, 0, tiled=True)
+    coupled = solve(groups, counts, shared, owned, w)
+    head = jnp.concatenate([pressure[:2], divergence[:1], 1.0 / (6.0 + diagonal[:1])])
+    tail = jnp.concatenate([pressure[-1:], pressure[-2:-1], divergence[-1:], 1.0 / (6.0 + diagonal[-1:])])
+    left, right = swap(head, tail, "gx")
+    once, ratio, low, high = first_sweep(pressure, divergence, diagonal, left, right)
+    beneath, beyond = swap(low, high, "gy")
+    field = second_sweep(once, ratio, divergence, low, high, beneath, beyond)
     return (field, coupled)
 
 

time: 89.2 us -> 70.7 us (0.79)
  other arithmetic: 19.6 us -> 4.22 us
  waiting for transfers between devices: 10.8 us -> 0.02 us
  Pallas kernels: 12.4 us -> 22.7 us
  blocking collectives: 16.5 us -> 11.7 us
  local copies, waits for them, and re-layouts: 9.35 us -> 11.1 us
    div x2 -> x1, other arithmetic: 13.6 us -> 0.82 us  [shards(): 1.0 / (6.0 + diagonal[-1:])]
    pallas_call x1 -> x5, Pallas kernels: 4.4 us -> 14.8 us  [the longest x1 4.82 us: place(): pl.pallas_call(functools.partial(place_kernel, cy), out_shape=(jax.ShapeD...]
    ppermute x4 -> x3, waiting for transfers between devices: 6.15 us -> 0.01 us  [swap(): first = lax.ppermute(jnp.where(even, tail, head), axis, pairs(count, 0))]
    concatenate x3 -> x0, other arithmetic: 5.7 us -> none  [the longest x2 5.7 us: extended(): cells = jnp.concatenate([below, cells, above], axis=dim)]
    all_to_all x1, blocking collectives: 16.5 us -> 11.7 us  [shards(): shared = lax.all_to_all(message, ('gx', 'gy'), 0, 0, tiled=True)]
    all_to_all x1, waiting for transfers between devices: 4.64 us -> 0.01 us  [shards(): got = lax.all_to_all(block, 'gy', 0, 0, tiled=True)]
    all_to_all x1, starting transfers between devices: 2.57 us -> 5.81 us  [shards(): got = lax.all_to_all(block, 'gy', 0, 0, tiled=True)]
    unnamed x23 -> x17, local copies, waits for them, and re-layouts: 7.32 us -> 10.3 us
  transfers between devices with their start and end apart: 9 -> 7, of which waited for: 5 -> 0; matrix products, arithmetic and copies ran while one was open for 3% -> 6% of each run, Pallas kernels for 3% -> 25%
where the time goes in v2:
time: 70.7 us; the launch traced here: 69.5 us
  Pallas kernels  22.7 us (32%)
  starting transfers between devices  18.3 us (26%)
  blocking collectives  11.7 us (17%)
  local copies, waits for them, and re-layouts  11.1 us (16%)
  other arithmetic  4.22 us (6%)
  between operations  1.44 us (2%)
    all_to_all x1, blocking collectives, shards(): shared = lax.all_to_all(message, ('gx', 'gy'), 0, 0, tiled=True)  11.7 us
    ppermute x3, starting transfers between devices, swap(): first = lax.ppermute(jnp.where(even, tail, head), axis, pairs(count, 0))  10.5 us
    unnamed x17, local copies, waits for them, and re-layouts  10.3 us
    all_to_all x1, starting transfers between devices, shards(): got = lax.all_to_all(block, 'gy', 0, 0, tiled=True)  5.81 us
    pallas_call x1, Pallas kernels, solve(): pl.pallas_call(functools.partial(solve_kernel, groups), out_shape=jax.Sha...  4.95 us
    pallas_call x1, Pallas kernels, place(): pl.pallas_call(functools.partial(place_kernel, cy), out_shape=(jax.ShapeD...  4.82 us
    pallas_call x1, Pallas kernels, second_sweep(): pl.pallas_call(second_kernel, out_shape=jax.ShapeDtypeStruct(d.shape, F32...  3.05 us
    pallas_call x1, Pallas kernels, gram_tile(): pl.pallas_call(gram_kernel, out_shape=jax.ShapeDtypeStruct((columns * col...  3 us
  transfers between devices with their start and end apart: 7, of which 0 were waited for; matrix products, arithmetic and copies ran while one was open for 6% of the time, Pallas kernels for 25%

profile of v2, /device:TPU:0, one launch (start us, length us, event | category | flops | bytes accessed | tf_op | source)
XLA Modules:
  0.0 69.5 jit_solution(11529954288752722025)
XLA Ops:
  0.7 2.6 %slab.1.planes_ref = f32[8,1024]{1,0:T(8,128)} custom-call(f32[64,16,512]{2,1,0:T(8,128)} %pressure_ref.1, f32[64,16,512]{2,1,0:T(8,128)} %divergence_ref.1, f32[64,16,512]{2,1,0:T(8,128)} %diagonal_ref.1), custom_call_target="tpu_custom_call" | custom-call | tf_op jit(solution)/shard_map/slab/pallas_call | solution.py:82
  3.3 0.7 %slice_select_fusion = (f32[8,128]{1,0:T(8,128)S(1)}, f32[8,128]{1,0:T(8,128)S(1)}) fusion(f32[8,1024]{1,0:T(8,128)} %slab.1.planes_ref, pred[]{:T(512)S(6)} %eq.11), kind=kLoop, calls=%fused_computation.13 | loop fusion | flops 2048 | bytes 16385 | tf_op jit(solution)/shard_map/jit(_where)/select_n | solution.py:27
  4.6 4.4 %collective-permute-start.5 = (f32[8,128]{1,0:T(8,128)S(1)}, f32[8,128]{1,0:T(8,128)S(1)}, u32[]{:S(2)}, u32[]{:S(2)}) collective-permute-start(f32[8,128]{1,0:T(8,128)S(1)} %get-tuple-element.28), channel_id=1, source_target_pairs={{0,8},{8,0},{16,24},{24,16},{1,9},{9,1},{17,25},{25,17},{2,10},{10... | collective-permute-start | bytes 12296 | tf_op jit(solution)/shard_map/ppermute | solution.py:27
  9.0 0.8 %add_divide_fusion = (f32[1,16,512]{2,1,0:T(8,128)S(1)}, f32[1,16,512]{2,1,0:T(8,128)S(1)}, f32[1,16,512]{2,1,0:T(8,128)S(1)}, f32[1,16,512]{2,1,0:T(8,128)S(1)}) fusion(f32[64,16,512]{2,1,0:T(8,128)} %diagonal_ref.1, f32[64,16,512]{2,1,0:T(8,128)} %pressure_ref.1), kind=kLoop, calls=%fused_computation.11 | loop fusion | flops 32768 | bytes 262144 | tf_op jit(solution)/shard_map/div | solution.py:431
  10.6 1.3 %collective-permute-start.1 = (f32[4,16,512]{2,1,0:T(8,128)S(1)}, f32[4,16,512]{2,1,0:T(8,128)S(1)}, u32[]{:S(2)}, u32[]{:S(2)}) collective-permute-start(f32[4,16,512]{2,1,0:T(8,128)S(1)} %get-tuple-element.26), channel_id=1, source_target_pairs={{0,8},{8,0},{16,24},{24,16},{1,9},{9,1},{17,25},{25,17},{2,10},{10... | collective-permute-start | bytes 393224 | tf_op jit(solution)/shard_map/ppermute | solution.py:27
  12.6 3.0 %gram.1.gram_ref = f32[8,128]{1,0:T(8,128)} custom-call(s32[1]{0:T(128)S(6)} %copy.16.count_ref, f32[3,32,3072]{2,1,0:T(8,128)} %bitcast.8), custom_call_target="tpu_custom_call" | custom-call | tf_op jit(solution)/shard_map/gram/pallas_call | solution.py:55
  16.2 1.7 %surface.1 = f32[8,56,128]{2,1,0:T(8,128)} custom-call(f32[8,1024]{1,0:T(8,128)} %slab.1.planes_ref, f32[8,128]{1,0:T(8,128)} %get-tuple-element.31.below_ref, f32[8,128]{1,0:T(8,128)} %get-tuple-element.30.above_ref, f32[3,1024]{1,0:T(4,128)} %normals_ref.1, f32[3,1024]{1,0:T(4,128)} %traction_ref.1, f32[8,128]{1,0:T(8,128)} %gram.1.gram_ref), custom_call_target="tpu_custom_call" | custom-call | tf_op jit(solution)/shard_map/surface/pallas_call | solution.py:157
  18.0 5.8 %all-to-all-start = ((f32[8,56,128]{2,1,0:T(8,128)}), f32[8,56,128]{2,1,0:T(8,128)S(1)}, u32[]{:S(2)}, u32[]{:S(2)}) async-start(f32[8,56,128]{2,1,0:T(8,128)} %surface.1), calls=%async_computation | async-start | bytes 458752 | tf_op jit(solution)/shard_map/all_to_all | solution.py:424
  23.8 1.6 %copy-done.1 = f32[64,16,512]{2,1,0:T(8,128)S(1)} copy-done((f32[64,16,512]{2,1,0:T(8,128)S(1)}, f32[64,16,512]{2,1,0:T(8,128)}, u32[]{:S(2)}) %copy-start.1) | copy-done | bytes 2097176
  25.4 1.6 %copy-done.2 = f32[64,16,512]{2,1,0:T(8,128)S(1)} copy-done((f32[64,16,512]{2,1,0:T(8,128)S(1)}, f32[64,16,512]{2,1,0:T(8,128)}, u32[]{:S(2)}) %copy-start.2) | copy-done | bytes 2097176
  27.0 2.5 %first_sweep.1 = (f32[66,16,512]{2,1,0:T(8,128)S(1)}, f32[64,16,512]{2,1,0:T(8,128)S(1)}, f32[200,512]{1,0:T(8,128)S(1)}, f32[200,512]{1,0:T(8,128)S(1)}) custom-call(f32[64,16,512]{2,1,0:T(8,128)S(1)} %copy-done.1, f32[64,16,512]{2,1,0:T(8,128)S(1)} %copy-done, f32[64,16,512]{2,1,0:T(8,128)S(1)} %copy-done.2, ...), custom_call_target="tpu_custom_call" | custom-call | tf_op jit(solution)/shard_map/first_sweep/pallas_call | solution.py:352
  29.5 1.4 %copy-done.3 = f32[66,16,512]{2,1,0:T(8,128)} copy-done((f32[66,16,512]{2,1,0:T(8,128)}, f32[66,16,512]{2,1,0:T(8,128)S(1)}, u32[]{:S(2)}) %copy-start.3) | copy-done | bytes 2162712
  30.9 1.3 %copy-done.5 = f32[64,16,512]{2,1,0:T(8,128)} copy-done((f32[64,16,512]{2,1,0:T(8,128)}, f32[64,16,512]{2,1,0:T(8,128)S(1)}, u32[]{:S(2)}) %copy-start.5) | copy-done | bytes 2097176
  32.2 1.0 %broadcast_select_fusion.2 = (f32[200,512]{1,0:T(8,128)}, f32[200,512]{1,0:T(8,128)}) fusion(f32[200,512]{1,0:T(8,128)S(1)} %get-tuple-element.11.high_ref, f32[200,512]{1,0:T(8,128)S(1)} %get-tuple-element.10.low_ref, pred[]{:T(512)S(6)} %eq.12), kind=kLoop, calls=%fused_computation.2 | loop fusion | flops 204800 | bytes 1638401 | tf_op jit(solution)/shard_map/jit(_where)/select_n | solution.py:27
  33.9 4.8 %collective-permute-start.3 = (f32[200,512]{1,0:T(8,128)}, f32[200,512]{1,0:T(8,128)}, u32[]{:S(2)}, u32[]{:S(2)}) collective-permute-start(f32[200,512]{1,0:T(8,128)} %get-tuple-element.22), channel_id=1, source_target_pairs={{0,1},{1,0},{2,3},{3,2},{4,5},{5,4},{6,7},{7,6},{8,9},{9,8},{10,11... | collective-permute-start | bytes 1228808 | tf_op jit(solution)/shard_map/ppermute | solution.py:27
  38.6 0.7 copy-done.7
  39.3 4.8 %place.1 = (f32[3,3072]{1,0:T(4,128)}, f32[32,256]{1,0:T(8,128)}) custom-call(s32[1]{0:T(128)} %bitcast.place_ref, s32[1]{0:T(128)S(6)} %copy.16.count_ref, f32[8,56,128]{2,1,0:T(8,128)} %copy-done.7, s32[64,128]{1,0:T(8,128)} %bitcast.12, f32[3,3072]{1,0:T(4,128)} %previous_ref.1, f32[3,32,3072]{2,1,0:T(8,128)} %bitcast.9), custom_call_target="tpu_custom_call" | custom-call | tf_op jit(solution)/shard_map/place/pallas_call | solution.py:260
  44.1 0.8 %copy.12 = f32[32,1,256]{2,1,0:T(1,128)S(1)} copy(f32[32,1,256]{2,0,1:T(8,128)} %bitcast.13) | data formatting | bytes 65536 | tf_op jit(solution)/shard_map/all_to_all | solution.py:428
  44.9 11.7 %all_to_all.16 = f32[32,1,256]{2,1,0:T(1,128)S(1)} all-to-all(f32[32,1,256]{2,1,0:T(1,128)S(1)} %copy.12), channel_id=1, replica_groups=mesh['gx'=4,'gy'=8] {'gx','gy'}, dimensions={0} | all-to-all | bytes 65536 | tf_op jit(solution)/shard_map/all_to_all | solution.py:428
  57.2 4.9 %solve.1 = f32[3,3072]{1,0:T(4,128)} custom-call(s32[1]{0:T(128)S(6)} %copy.16.count_ref, f32[32,256]{1,0:T(8,128)} %bitcast.11, f32[3,3072]{1,0:T(4,128)} %get-tuple-element.13.owned_ref, f32[3,32,3072]{2,1,0:T(8,128)} %bitcast.10), custom_call_target="tpu_custom_call" | custom-call | tf_op jit(solution)/shard_map/solve/pallas_call | solution.py:302
  62.2 1.1 %broadcast_select_fusion = (f32[200,512]{1,0:T(8,128)S(1)}, f32[200,512]{1,0:T(8,128)S(1)}) fusion(f32[200,512]{1,0:T(8,128)} %collective-permute-done.3, f32[200,512]{1,0:T(8,128)S(1)} %collective-permute-done.2, pred[]{:T(512)S(6)} %eq.12), kind=kLoop, calls=%fused_computation | loop fusion | flops 204800 | bytes 1638401 | tf_op jit(solution)/shard_map/jit(_where)/select_n | solution.py:29
  63.3 1.6 %copy-done.4 = f32[66,16,512]{2,1,0:T(8,128)S(1)} copy-done((f32[66,16,512]{2,1,0:T(8,128)S(1)}, f32[66,16,512]{2,1,0:T(8,128)}, u32[]{:S(2)}) %copy-start.4) | copy-done | bytes 2162712
  64.9 1.6 %copy-done.6 = f32[64,16,512]{2,1,0:T(8,128)S(1)} copy-done((f32[64,16,512]{2,1,0:T(8,128)S(1)}, f32[64,16,512]{2,1,0:T(8,128)}, u32[]{:S(2)}) %copy-start.6) | copy-done | bytes 2097176
  66.5 3.1 %second_sweep.1 = f32[64,16,512]{2,1,0:T(8,128)} custom-call(f32[66,16,512]{2,1,0:T(8,128)S(1)} %copy-done.4, f32[64,16,512]{2,1,0:T(8,128)S(1)} %copy-done.6, f32[64,16,512]{2,1,0:T(8,128)S(1)} %copy-done, f32[200,512]{1,0:T(8,128)S(1)} %get-tuple-element.10.low_ref, f32[200,512]{1,0:T(8,128)S(1)} %get-tuple-element.11.high_ref, ...), custom_call_target="tpu_custom_call" | custom-call | tf_op jit(solution)/shard_map/second_sweep/pallas_call | solution.py:401
  (26 shorter events, 3.3 us)
Async XLA Ops:
  0.6 9.2 %copy-start = (f32[64,16,512]{2,1,0:T(8,128)S(1)}, f32[64,16,512]{2,1,0:T(8,128)}, u32[]{:S(2)}) copy-start(f32[64,16,512]{2,1,0:T(8,128)} %divergence_ref.1) | copy-start | bytes 6291460
  0.7 9.2 %slice-start = ((f32[64,16,512]{2,1,0:T(8,128)}), f32[2,16,512]{2,1,0:T(8,128)S(1)}, s32[]{:S(2)}) async-start(f32[64,16,512]{2,1,0:T(8,128)} %pressure_ref.1), calls=%async_computation.2 | async-start | bytes 131072 | tf_op jit(solution)/shard_map/slice | solution.py:430
  4.0 11.6 %collective-permute-start.4 = (f32[8,128]{1,0:T(8,128)S(1)}, f32[8,128]{1,0:T(8,128)S(1)}, u32[]{:S(2)}, u32[]{:S(2)}) collective-permute-start(f32[8,128]{1,0:T(8,128)S(1)} %get-tuple-element.29), channel_id=1, source_target_pairs={{8,16},{16,8},{9,17},{17,9},{10,18},{18,10},{11,19},{19,11},{12,20... | collective-permute-start | bytes 12296 | tf_op jit(solution)/shard_map/ppermute | solution.py:28
  4.6 11.0 %collective-permute-start.5 = (f32[8,128]{1,0:T(8,128)S(1)}, f32[8,128]{1,0:T(8,128)S(1)}, u32[]{:S(2)}, u32[]{:S(2)}) collective-permute-start(f32[8,128]{1,0:T(8,128)S(1)} %get-tuple-element.28), channel_id=1, source_target_pairs={{0,8},{8,0},{16,24},{24,16},{1,9},{9,1},{17,25},{25,17},{2,10},{10... | collective-permute-start | bytes 12296 | tf_op jit(solution)/shard_map/ppermute | solution.py:27
  9.9 13.8 %collective-permute-start = (f32[4,16,512]{2,1,0:T(8,128)S(1)}, f32[4,16,512]{2,1,0:T(8,128)S(1)}, u32[]{:S(2)}, u32[]{:S(2)}) collective-permute-start(f32[4,16,512]{2,1,0:T(8,128)S(1)} %get-tuple-element.27), channel_id=1, source_target_pairs={{8,16},{16,8},{9,17},{17,9},{10,18},{18,10},{11,19},{19,11},{12,20... | collective-permute-start | bytes 393224 | tf_op jit(solution)/shard_map/ppermute | solution.py:28
  10.6 13.2 %collective-permute-start.1 = (f32[4,16,512]{2,1,0:T(8,128)S(1)}, f32[4,16,512]{2,1,0:T(8,128)S(1)}, u32[]{:S(2)}, u32[]{:S(2)}) collective-permute-start(f32[4,16,512]{2,1,0:T(8,128)S(1)} %get-tuple-element.26), channel_id=1, source_target_pairs={{0,8},{8,0},{16,24},{24,16},{1,9},{9,1},{17,25},{25,17},{2,10},{10... | collective-permute-start | bytes 393224 | tf_op jit(solution)/shard_map/ppermute | solution.py:27
  18.0 20.7 %all-to-all-start = ((f32[8,56,128]{2,1,0:T(8,128)}), f32[8,56,128]{2,1,0:T(8,128)S(1)}, u32[]{:S(2)}, u32[]{:S(2)}) async-start(f32[8,56,128]{2,1,0:T(8,128)} %surface.1), calls=%async_computation | async-start | bytes 458752 | tf_op jit(solution)/shard_map/all_to_all | solution.py:424
  23.8 1.6 %copy-start.1 = (f32[64,16,512]{2,1,0:T(8,128)S(1)}, f32[64,16,512]{2,1,0:T(8,128)}, u32[]{:S(2)}) copy-start(f32[64,16,512]{2,1,0:T(8,128)} %pressure_ref.1) | copy-start | bytes 6291460
  25.4 1.6 %copy-start.2 = (f32[64,16,512]{2,1,0:T(8,128)S(1)}, f32[64,16,512]{2,1,0:T(8,128)}, u32[]{:S(2)}) copy-start(f32[64,16,512]{2,1,0:T(8,128)} %diagonal_ref.1) | copy-start | bytes 6291460
  29.5 1.4 %copy-start.3 = (f32[66,16,512]{2,1,0:T(8,128)}, f32[66,16,512]{2,1,0:T(8,128)S(1)}, u32[]{:S(2)}) copy-start(f32[66,16,512]{2,1,0:T(8,128)S(1)} %get-tuple-element.8.once_ref) | copy-start | bytes 6488068
  30.9 1.3 %copy-start.5 = (f32[64,16,512]{2,1,0:T(8,128)}, f32[64,16,512]{2,1,0:T(8,128)S(1)}, u32[]{:S(2)}) copy-start(f32[64,16,512]{2,1,0:T(8,128)S(1)} %get-tuple-element.9.ratio_ref) | copy-start | bytes 6291460
  33.2 29.0 %collective-permute-start.2 = (f32[200,512]{1,0:T(8,128)}, f32[200,512]{1,0:T(8,128)S(1)}, u32[]{:S(2)}, u32[]{:S(2)}) collective-permute-start(f32[200,512]{1,0:T(8,128)} %get-tuple-element.23), channel_id=1, source_target_pairs={{1,2},{2,1},{3,4},{4,3},{5,6},{6,5},{9,10},{10,9},{11,12},{12,11},... | collective-permute-start | bytes 1228808 | tf_op jit(solution)/shard_map/ppermute | solution.py:28
  33.9 28.3 %collective-permute-start.3 = (f32[200,512]{1,0:T(8,128)}, f32[200,512]{1,0:T(8,128)}, u32[]{:S(2)}, u32[]{:S(2)}) collective-permute-start(f32[200,512]{1,0:T(8,128)} %get-tuple-element.22), channel_id=1, source_target_pairs={{0,1},{1,0},{2,3},{3,2},{4,5},{5,4},{6,7},{7,6},{8,9},{9,8},{10,11... | collective-permute-start | bytes 1228808 | tf_op jit(solution)/shard_map/ppermute | solution.py:27
  38.6 0.7 copy-start.7
  63.3 1.6 %copy-start.4 = (f32[66,16,512]{2,1,0:T(8,128)S(1)}, f32[66,16,512]{2,1,0:T(8,128)}, u32[]{:S(2)}) copy-start(f32[66,16,512]{2,1,0:T(8,128)} %copy-done.3) | copy-start | bytes 6488068
  64.9 1.6 %copy-start.6 = (f32[64,16,512]{2,1,0:T(8,128)S(1)}, f32[64,16,512]{2,1,0:T(8,128)}, u32[]{:S(2)}) copy-start(f32[64,16,512]{2,1,0:T(8,128)} %copy-done.5) | copy-start | bytes 6291460

commit v3 on v2

v3 whole, which is shorter than its diff:
```python
import functools
import jax
import jax.numpy as jnp
from jax import lax
from jax.experimental import pallas as pl
from jax.experimental.pallas import tpu as pltpu
from jax.sharding import PartitionSpec as P

LANES = 128
F32 = jnp.float32
BF16 = jnp.bfloat16
VMEM = pl.BlockSpec(memory_space=pltpu.VMEM)
ANY = pl.BlockSpec(memory_space=pl.ANY)
SMEM = pl.BlockSpec(memory_space=pltpu.SMEM)
HIGHEST = lax.Precision.HIGHEST


def pairs(count, parity):
    out = []
    for low in range(parity, count - 1, 2):
        out += [(low, low + 1), (low + 1, low)]
    return out


def traded(first, second, axis):
    count = lax.axis_size(axis)
    return lax.ppermute(first, axis, pairs(count, 0)), lax.ppermute(second, axis, pairs(count, 1))


def iota(shape, dim):
    return lax.broadcasted_iota(jnp.int32, shape, dim)


def occupied_rows(count, capacity):
    return (iota((1, capacity), 1) < count).astype(F32)


def gram_kernel(count_ref, v_ref, gram_ref):
    columns, capacity = v_ref.shape[1], v_ref.shape[2]
    occupied = occupied_rows(count_ref[0], capacity)
    total = jnp.zeros((columns, columns), F32)
    for c in range(v_ref.shape[0]):
        plain = v_ref[c]
        total += lax.dot_general(
            plain * occupied, plain, (((1,), (1,)), ((), ())), precision=HIGHEST, preferred_element_type=F32
        )
    rows = gram_ref.shape[0]
    gram_ref[...] = jnp.concatenate([total[j : j + rows] for j in range(0, columns, rows)], axis=1)


def gram_tile(counts, v):
    columns = v.shape[1]
    return pl.pallas_call(
        gram_kernel,
        out_shape=jax.ShapeDtypeStruct((columns * columns // LANES, LANES), F32),
        in_specs=[SMEM, VMEM],
        out_specs=VMEM,
        compiler_params=limit(8),
        name="gram",
    )(counts, v)


def slab_kernel(
    even_x_ref, even_y_ref, p_ref, d_ref, g_ref, planes_ref, first_ref, second_ref, y_first_ref, y_second_ref,
    held, ratios, tile_sems, face_sems, y_sems,
):
    cx, cy, cz = p_ref.shape
    step = LANES // cy
    half = cx // 2
    even, even_y = even_x_ref[0] == 1, even_y_ref[0] == 1
    fetches = []
    for part in range(2):
        for which, ref in enumerate((p_ref, d_ref, g_ref)):
            at = pl.ds(part * half, half)
            fetches.append(
                pltpu.make_async_copy(
                    ref.at[at, :, pl.ds(cz - LANES, LANES)], held.at[which, at], tile_sems.at[part, which]
                )
            )
    for fetch in fetches:
        fetch.start()

    def face(out_ref, side, sources):
        return [
            pltpu.make_async_copy(
                ref.at[plane],
                ratios.at[side] if k == 3 else out_ref.at[pl.ds(k * cy, cy)],
                face_sems.at[side, k],
            )
            for k, (ref, plane) in enumerate(sources)
        ]

    head = ((p_ref, 0), (p_ref, 1), (d_ref, 0), (g_ref, 0))
    tail = ((p_ref, cx - 1), (p_ref, cx - 2), (d_ref, cx - 1), (g_ref, cx - 1))

    @pl.when(even)
    def _():
        for copy in face(second_ref, 0, head) + face(first_ref, 1, tail):
            copy.start()

    @pl.when(~even)
    def _():
        for copy in face(first_ref, 0, head) + face(second_ref, 1, tail):
            copy.start()

    def edge(out_ref, y, at):
        return pltpu.make_async_copy(p_ref.at[:, y, :], out_ref, y_sems.at[at])

    @pl.when(even_y)
    def _():
        edge(y_first_ref, cy - 1, 0).start()
        edge(y_second_ref, 0, 1).start()

    @pl.when(~even_y)
    def _():
        edge(y_first_ref, 0, 0).start()
        edge(y_second_ref, cy - 1, 1).start()

    planes_ref[7:8] = jnp.zeros((1, cx * cy), F32)
    for part in range(2):
        for fetch in fetches[3 * part : 3 * part + 3]:
            fetch.wait()
        for k in range(part * half // step, (part + 1) * half // step):
            lanes = slice(k * LANES, (k + 1) * LANES)
            turned = [held[which, k * step : (k + 1) * step].reshape(LANES, LANES).T for which in range(3)]
            for row, (which, back) in enumerate(((0, 1), (0, 2), (0, 3), (1, 1), (1, 2), (2, 1), (2, 2))):
                line = turned[which][LANES - back : LANES - back + 1]
                planes_ref[row : row + 1, lanes] = 1.0 / (6.0 + line) if which == 2 else line
    for copy in face(first_ref, 0, head) + face(first_ref, 1, tail):
        copy.wait()
    edge(y_first_ref, 0, 0).wait()
    edge(y_second_ref, 0, 1).wait()
    low, high = 1.0 / (6.0 + ratios[0]), 1.0 / (6.0 + ratios[1])
    own_low, own_high = planes_ref[:, :LANES], planes_ref[:, cx * cy - LANES :]
    for out_ref, above in ((first_ref, even), (second_ref, ~even)):
        out_ref[3 * cy : 4 * cy] = jnp.where(above, high, low)
        out_ref[4 * cy :] = jnp.zeros((8, cz), F32)
        out_ref[4 * cy :, :LANES] = jnp.where(above, own_high, own_low)


def in_hbm(array):
    return pltpu.with_memory_space_constraint(array, pltpu.HBM)


def limit(mib):
    return pltpu.CompilerParams(vmem_limit_bytes=mib * 1024 * 1024)


def slab(even_x, even_y, p, d, g):
    cx, cy, cz = p.shape
    face = jax.ShapeDtypeStruct((4 * cy + 8, cz), F32)
    edge = jax.ShapeDtypeStruct((cx, cz), F32)
    return pl.pallas_call(
        slab_kernel,
        out_shape=(jax.ShapeDtypeStruct((8, cx * cy), F32), face, face, edge, edge),
        in_specs=[SMEM, SMEM] + [ANY] * 3,
        out_specs=(VMEM,) * 5,
        scratch_shapes=[
            pltpu.VMEM((3, cx, cy, LANES), F32),
            pltpu.VMEM((2, cy, cz), F32),
            pltpu.SemaphoreType.DMA((2, 3)),
            pltpu.SemaphoreType.DMA((2, 4)),
            pltpu.SemaphoreType.DMA((2,)),
        ],
        compiler_params=limit(8),
        name="slab",
    )(even_x, even_y, in_hbm(p), in_hbm(d), in_hbm(g))


def rolled(block, shift, axis=1):
    return pltpu.roll(block, shift % block.shape[axis], axis)


def packed(parts, cy):
    place = lax.rem(iota(parts[0].shape, 1) + 2, cy) // 4
    out = parts[0]
    for k in range(1, 4):
        out = jnp.where(place == k, rolled(parts[k], 4 * k), out)
    return out


def surface_kernel(cy, even_ref, planes_ref, first_ref, second_ref, normals_ref, traction_ref, gram_ref, out_ref, scratch):
    rows = planes_ref.shape[1]
    tiles = rows // LANES
    first, second = first_ref[4 * cy :, :LANES], second_ref[4 * cy :, :LANES]
    even = even_ref[0] == 1
    ext = jnp.concatenate(
        [jnp.where(even, second, first), planes_ref[...], jnp.where(even, first, second)], axis=1
    )
    y = lax.rem(iota(ext.shape, 1), cy)

    def around(block):
        inner = jnp.where(y == 0, 0.0, rolled(block, 1)) + jnp.where(y == cy - 1, 0.0, rolled(block, -1))
        return rolled(block, cy) + rolled(block, -cy) + inner

    def line(row):
        return ext[row : row + 1]

    near = around(ext)
    once = (line(3) + near[0:1] + line(1)) * line(5)
    beneath = (line(4) + near[1:2] + line(0) + line(2)) * line(6)
    twice = (line(3) + around(jnp.broadcast_to(once, ext.shape))[0:1] + beneath) * line(5)
    surface = twice[:, LANES : LANES + rows]
    normals = normals_ref[...]
    forces = normals * surface + traction_ref[...]
    own = slice(LANES, LANES + rows)
    wide = lambda part: jnp.broadcast_to(part, (8, rows))
    first = packed(
        [wide(normals[0:1]), wide(normals[1:2]), wide(normals[2:3]), wide(line(0)[:, own])], cy
    )
    second = packed(
        [wide(part[:, own]) for part in (line(1), once, line(5), line(5) * line(6))], cy
    )
    for t in range(tiles):
        lanes = slice(t * LANES, (t + 1) * LANES)
        for c in range(3):
            scratch[c * tiles + t : c * tiles + t + 1] = forces[c : c + 1, lanes]
        scratch[3 * tiles + t : 3 * tiles + t + 1] = first[0:1, lanes]
        scratch[4 * tiles + t : 4 * tiles + t + 1] = second[0:1, lanes]
    low, high = ext[:, :LANES], ext[:, LANES + rows :]
    lane = iota((8, LANES), 1)
    side = jnp.where(
        lane < cy,
        rolled(low, cy)[0:1],
        jnp.where(
            lane < 2 * cy,
            rolled(high, cy)[0:1],
            jnp.where(lane < 3 * cy, rolled(low, 3 * cy)[5:6], rolled(high, 3 * cy)[5:6]),
        ),
    )
    scratch[5 * tiles : 5 * tiles + 8] = side
    scratch[5 * tiles + 8 :] = gram_ref[...]
    for d in range(out_ref.shape[0]):
        out_ref[d] = scratch[...]


def surface_message(count, cy, even, planes, first, second, normals, traction, gram):
    rows = 5 * planes.shape[1] // LANES + 8 + gram.shape[0]
    return pl.pallas_call(
        functools.partial(surface_kernel, cy),
        out_shape=jax.ShapeDtypeStruct((count, rows, LANES), F32),
        in_specs=[SMEM] + [VMEM] * 6,
        out_specs=VMEM,
        scratch_shapes=[pltpu.VMEM((rows, LANES), F32)],
        compiler_params=limit(8),
        name="surface",
    )(even, planes, first, second, normals, traction, gram)


def corrected(cy, got_ref, tiles, forces_ref):
    sources = got_ref.shape[0]
    rows = tiles * LANES

    def plane(index):
        return jnp.concatenate([got_ref[:, index * tiles + t, :] for t in range(tiles)], axis=1)

    def across(block):
        y, source = lax.rem(iota(block.shape, 1), cy), iota(block.shape, 0)
        before = rolled(rolled(block, 1, 0), 1 - cy)
        after = rolled(rolled(block, -1, 0), cy - 1)
        return jnp.where(
            (y == 0) & (source > 0), before, jnp.where((y == cy - 1) & (source < sources - 1), after, 0.0)
        )

    first, second = plane(3), plane(4)
    y = lax.rem(iota(first.shape, 1), cy)
    lane = iota(first.shape, 1)
    edge = lax.rem(y + 2, cy) < 4
    ratio = jnp.where(edge, rolled(second, -8), 0.0)
    both = jnp.where(edge, rolled(second, -12), 0.0)
    delta = ratio * across(rolled(first, -12))
    side = got_ref[:, 5 * tiles, :]
    side = rolled(side, -2 * cy) * across(side)
    end = jnp.concatenate([side] + [jnp.zeros_like(side)] * (tiles - 2) + [rolled(side, -2 * cy)], axis=1)
    total = jnp.where(lane < cy, end, rolled(delta, cy)) + jnp.where(lane >= rows - cy, end, rolled(delta, -cy))
    total += across(rolled(second, -4) + delta)
    total += jnp.where(y == 1, rolled(delta, 1), 0.0) + jnp.where(y == cy - 2, rolled(delta, -1), 0.0)
    change = ratio * total + both * across(second)
    for c in range(3):
        normal = jnp.where(edge, rolled(first, -4 * c), 0.0)
        forces = plane(c) + normal * change
        for t in range(tiles):
            forces_ref[c * tiles + t] = forces[:, t * LANES : (t + 1) * LANES]


def place_kernel(cy, place_ref, count_ref, got_ref, slot_ref, previous_ref, v_ref, owned_ref, message_ref, gram_scratch, forces_ref, held_v, arrived):
    own = place_ref[0]
    sources, tiles = got_ref.shape[0], slot_ref.shape[0] // got_ref.shape[0]
    capacity = previous_ref.shape[1]
    high = capacity // LANES
    base = own * capacity
    fetch = pltpu.make_async_copy(v_ref, held_v, arrived)
    fetch.start()
    corrected(cy, got_ref, tiles, forces_ref)

    def one_source(source, total):
        left, right = [], []
        for t in range(tiles):
            slots = slot_ref[pl.ds(source * tiles + t, 1), :]
            at_row = lax.shift_right_arithmetic(slots - base, 7) == iota((high, LANES), 0)
            right.append((jnp.bitwise_and(slots, LANES - 1) == iota((LANES, LANES), 0)).astype(F32))
            rough, fine = [], []
            for c in range(3):
                value = forces_ref[c * tiles + t, pl.ds(source, 1), :]
                near = value.astype(BF16).astype(F32)
                rough.append(jnp.where(at_row, near, 0.0))
                fine.append(jnp.where(at_row, value - near, 0.0))
            left.append(jnp.concatenate(rough + fine, axis=0))
        left = jnp.concatenate(left, axis=1).astype(BF16)
        right = jnp.concatenate(right, axis=1).astype(BF16)
        return total + lax.dot_general(
            left, right, (((1,), (1,)), ((), ())), preferred_element_type=F32
        )

    total = lax.fori_loop(0, sources, one_source, jnp.zeros((6 * high, LANES), F32))
    owned = total[: 3 * high] + total[3 * high :]
    fetch.wait()
    summed = jnp.zeros((v_ref.shape[1], LANES), F32)
    for c in range(3):
        for h in range(high):
            lanes = slice(h * LANES, (h + 1) * LANES)
            row = owned[c * high + h : c * high + h + 1]
            owned_ref[c : c + 1, lanes] = row
            held = iota((1, LANES), 1) + h * LANES < count_ref[0]
            residual = jnp.where(held, row - previous_ref[c : c + 1, lanes], 0.0)
            summed += held_v[c, :, lanes] * residual
    projection = lax.dot_general(
        jnp.ones((8, LANES), F32), summed, (((1,), (1,)), ((), ())), precision=HIGHEST, preferred_element_type=F32
    )
    gram_rows = gram_scratch.shape[0]
    gram_scratch[...] = jnp.sum(got_ref[:, 5 * tiles + 8 :, :], axis=0)
    chunk = gram_scratch[pl.ds(jnp.minimum(own, gram_rows - 1), 1), :]
    message = jnp.concatenate(
        [
            jnp.where(own < gram_rows, chunk, 0.0),
            projection[:1],
            jnp.zeros((1, LANES - projection.shape[1]), F32),
        ],
        axis=1,
    )
    message_ref[...] = jnp.broadcast_to(message[None], message_ref.shape)


def place(devices, cy, own, counts, got, slots, previous, v):
    columns = v.shape[1]
    return pl.pallas_call(
        functools.partial(place_kernel, cy),
        out_shape=(
            jax.ShapeDtypeStruct(previous.shape, F32),
            jax.ShapeDtypeStruct((devices, 1, 2 * LANES), F32),
        ),
        in_specs=[SMEM, SMEM, VMEM, VMEM, VMEM, ANY],
        out_specs=(VMEM, VMEM),
        scratch_shapes=[
            pltpu.VMEM((columns * columns // LANES, LANES), F32),
            pltpu.VMEM((3 * slots.shape[0] // got.shape[0], got.shape[0], LANES), F32),
            pltpu.VMEM(v.shape, F32),
            pltpu.SemaphoreType.DMA,
        ],
        compiler_params=limit(12),
        name="place",
    )(own, counts, got, slots, previous, v)


def solve_kernel(groups, count_ref, got_ref, owned_ref, w_ref, coupled_ref, held_w, arrived):
    fetch = pltpu.make_async_copy(w_ref, held_w, arrived)
    fetch.start()
    columns, capacity = w_ref.shape[1], w_ref.shape[2]
    gram_rows = columns * columns // LANES
    per_group = got_ref.shape[0] // groups
    tile = got_ref[:gram_rows, 0, :LANES]
    for g in range(1, groups):
        tile += got_ref[g * per_group : g * per_group + gram_rows, 0, :LANES]
    projection = jnp.sum(got_ref[:, 0, LANES:], axis=0, keepdims=True)
    gram = jnp.concatenate([tile[:, j : j + columns] for j in range(0, LANES, columns)], axis=0)
    rows, lanes = iota((columns, LANES), 0), iota((columns, LANES), 1)
    right = jnp.sum(jnp.where(rows == lanes, projection, 0.0), axis=1, keepdims=True)
    system = jnp.concatenate([gram, jnp.zeros((columns, LANES - columns), F32)], axis=1)
    system = jnp.where(lanes == columns, right, system)
    for k in range(columns):
        pivot_row = system[k : k + 1] / system[k : k + 1, k : k + 1]
        system = jnp.where(rows == k, pivot_row, system - system[:, k : k + 1] * pivot_row)
    coefficient = -system[:, columns : columns + 1]
    fetch.wait()
    for c in range(3):
        for h in range(capacity // LANES):
            at = slice(h * LANES, (h + 1) * LANES)
            update = jnp.sum(held_w[c, :, at] * coefficient, axis=0, keepdims=True)
            held = iota((1, LANES), 1) + h * LANES < count_ref[0]
            coupled_ref[c : c + 1, at] = jnp.where(held, owned_ref[c : c + 1, at] + update, 0.0)


def solve(groups, counts, got, owned, w):
    return pl.pallas_call(
        functools.partial(solve_kernel, groups),
        out_shape=jax.ShapeDtypeStruct(owned.shape, F32),
        in_specs=[SMEM, VMEM, VMEM, ANY],
        out_specs=VMEM,
        scratch_shapes=[pltpu.VMEM(w.shape, F32), pltpu.SemaphoreType.DMA],
        compiler_params=limit(8),
        name="solve",
    )(counts, got, owned, w)


def shifted(here, low, high):
    y, z = iota(here.shape, 0), iota(here.shape, 1)
    before = jnp.where(y == 0, low, rolled(here, 1, 0))
    after = jnp.where(y == here.shape[0] - 1, high, rolled(here, -1, 0))
    left = jnp.where(z == 0, 0.0, rolled(here, 1))
    right = jnp.where(z == here.shape[1] - 1, 0.0, rolled(here, -1))
    return before + after + left + right


CHUNK = 8


def halo_plane(even, first_ref, second_ref, k, above, cy):
    rows = slice(k * cy, (k + 1) * cy)
    return jnp.where(even != above, second_ref[rows], first_ref[rows])


def edge_kernel(
    even_x_ref, even_y_ref, p_ref, d_ref, g_ref, first_ref, second_ref, y_first_ref, y_second_ref,
    to_first_ref, to_second_ref, held, sems,
):
    cx, cy, cz = p_ref.shape
    columns = [(p_ref, 0), (p_ref, 1), (d_ref, 0), (g_ref, 0), (p_ref, cy - 1), (p_ref, cy - 2), (d_ref, cy - 1), (g_ref, cy - 1)]
    fetches = [
        pltpu.make_async_copy(ref.at[:, y, :], held.at[k], sems.at[k]) for k, (ref, y) in enumerate(columns)
    ]
    for fetch in fetches:
        fetch.start()
    for fetch in fetches:
        fetch.wait()
    even_x, even_y = even_x_ref[0] == 1, even_y_ref[0] == 1
    x, z = iota((cx, cz), 0), iota((cx, cz), 1)
    rows = []
    for side, y in enumerate((0, cy - 1)):
        here, inner, source, diagonal = [held[4 * side + k] for k in range(4)]
        below = halo_plane(even_x, first_ref, second_ref, 0, False, cy)[y : y + 1]
        above = halo_plane(even_x, first_ref, second_ref, 0, True, cy)[y : y + 1]
        total = source + inner + jnp.where(even_y != (side == 1), y_second_ref[...], y_first_ref[...])
        total += jnp.where(x == 0, below, rolled(here, 1, 0)) + jnp.where(x == cx - 1, above, rolled(here, -1, 0))
        total += jnp.where(z == 0, 0.0, rolled(here, 1)) + jnp.where(z == cz - 1, 0.0, rolled(here, -1))
        once = total * (1.0 / (6.0 + diagonal))
        rows.append((once, jnp.concatenate([below, above, jnp.zeros((6, cz), F32)], axis=0)))
    for at, k in ((slice(0, cx), 0), (slice(cx, cx + 8), 1)):
        to_first_ref[at] = jnp.where(even_y, rows[1][k], rows[0][k])
        to_second_ref[at] = jnp.where(even_y, rows[0][k], rows[1][k])


def swept_edges(even_x, even_y, p, d, g, first, second, y_first, y_second):
    cx, cy, cz = p.shape
    out = jax.ShapeDtypeStruct((cx + 8, cz), F32)
    return pl.pallas_call(
        edge_kernel,
        out_shape=(out, out),
        in_specs=[SMEM, SMEM] + [ANY] * 3 + [VMEM] * 4,
        out_specs=(VMEM, VMEM),
        scratch_shapes=[pltpu.VMEM((8, cx, cz), F32), pltpu.SemaphoreType.DMA((8,))],
        compiler_params=limit(8),
        name="edges",
    )(even_x, even_y, in_hbm(p), in_hbm(d), in_hbm(g), first, second, y_first, y_second)


def sweeps_kernel(
    even_x_ref, even_y_ref, p_ref, d_ref, g_ref, first_ref, second_ref, y_first_ref, y_second_ref,
    far_first_ref, far_second_ref, out_ref, held_p, held_d, held_g, once_ref, rows_ref, in_sems, out_sems,
):
    cx, cy, cz = p_ref.shape
    steps = cx // CHUNK
    even_x, even_y = even_x_ref[0] == 1, even_y_ref[0] == 1

    def arrive(at):
        planes = pl.ds(at * CHUNK, CHUNK)
        return [
            pltpu.make_async_copy(ref.at[planes], held.at[planes], in_sems.at[k, at])
            for k, (ref, held) in enumerate(((p_ref, held_p), (d_ref, held_d), (g_ref, held_g)))
        ]

    def leave(at):
        planes = pl.ds(at * CHUNK, CHUNK)
        return pltpu.make_async_copy(held_p.at[planes], out_ref.at[planes], out_sems.at[at])

    for at in range(steps):
        for copy in arrive(at):
            copy.start()
    for k, (one, two) in enumerate(((y_first_ref, y_second_ref), (far_first_ref, far_second_ref))):
        rows_ref[2 * k, : one.shape[0]] = jnp.where(even_y, two[...], one[...])
        rows_ref[2 * k + 1, : one.shape[0]] = jnp.where(even_y, one[...], two[...])
    halo = lambda k, above: halo_plane(even_x, first_ref, second_ref, k, above, cy)

    def sweep(before, here, after, source, ratio, low, high):
        return (source + before + after + shifted(here, low, high)) * ratio

    def rows(k, at):
        return [rows_ref[2 * k + side, pl.ds(pl.multiple_of(at * CHUNK, CHUNK), CHUNK), :] for side in range(2)]

    for copy in arrive(0):
        copy.wait()

    def first_chunk(at, carry):
        @pl.when(at + 1 < steps)
        def _():
            for copy in arrive(jnp.minimum(at + 1, steps - 1)):
                copy.wait()

        before, here = carry
        lows, highs = rows(0, at)
        for j in range(CHUNK):
            x = at * CHUNK + j
            after = held_p[jnp.minimum(x + 1, cx - 1)]
            if j == CHUNK - 1:
                after = jnp.where(x == cx - 1, halo(0, True), after)
            ratio = 1.0 / (6.0 + held_g[x])
            once_ref[x] = sweep(before, here, after, held_d[x], ratio, lows[j : j + 1], highs[j : j + 1])
            held_g[x] = ratio
            before, here = here, after
        return before, here

    lax.fori_loop(0, steps, first_chunk, (halo(0, False), held_p[0]))
    ends = [rows_ref[2 + side, cx : cx + 8] for side in range(2)]
    start = sweep(
        halo(1, False), halo(0, False), held_p[0], halo(2, False), halo(3, False), ends[0][:1], ends[1][:1]
    )
    once_ref[cx] = sweep(
        held_p[cx - 1], halo(0, True), halo(1, True), halo(2, True), halo(3, True), ends[0][1:2], ends[1][1:2]
    )

    def second_chunk(at, carry):
        before, here = carry
        lows, highs = rows(1, at)
        for j in range(CHUNK):
            x = at * CHUNK + j
            after = once_ref[x + 1]
            held_p[x] = sweep(before, here, after, held_d[x], held_g[x], lows[j : j + 1], highs[j : j + 1])
            before, here = here, after
        leave(at).start()
        return before, here

    lax.fori_loop(0, steps, second_chunk, (start, once_ref[0]))
    for at in range(steps):
        leave(at).wait()


def both_sweeps(even_x, even_y, p, d, g, *beside):
    cx, cy, cz = p.shape
    return pl.pallas_call(
        sweeps_kernel,
        out_shape=jax.ShapeDtypeStruct(p.shape, F32),
        in_specs=[SMEM, SMEM] + [ANY] * 3 + [VMEM] * 6,
        out_specs=ANY,
        scratch_shapes=[pltpu.VMEM(p.shape, F32)] * 3
        + [
            pltpu.VMEM((cx + 1, cy, cz), F32),
            pltpu.VMEM((4, cx + 8, cz), F32),
            pltpu.SemaphoreType.DMA((3, cx // CHUNK)),
            pltpu.SemaphoreType.DMA((cx // CHUNK,)),
        ],
        compiler_params=limit(20),
        name="sweeps",
    )(even_x, even_y, in_hbm(p), in_hbm(d), in_hbm(g), *beside)


def shards(
    pressure, divergence, diagonal, normals, traction, slot_of, counts, previous, secant_v, secant_w
):
    groups, owners = lax.axis_size("gx"), lax.axis_size("gy")
    cy = pressure.shape[1]
    v = jnp.transpose(secant_v, (1, 0, 2))
    w = jnp.transpose(secant_w, (1, 0, 2))
    own = lax.axis_index("gy").astype(jnp.int32).reshape(1)
    even_x, even_y = [(1 - lax.axis_index(axis) % 2).astype(jnp.int32).reshape(1) for axis in ("gx", "gy")]
    fluid = (even_x, even_y, pressure, divergence, diagonal)
    planes, first, second, y_first, y_second = slab(*fluid)
    faces = traded(first, second, "gx")
    y_edges = traded(y_first, y_second, "gy")
    faces, y_edges = lax.optimization_barrier((faces, y_edges))
    gram = gram_tile(counts, v)
    block = surface_message(owners, cy, even_x, planes, *faces, normals, traction, gram)
    got = lax.all_to_all(block, "gy", 0, 0, tiled=True)
    far_edges = traded(*swept_edges(*fluid, *faces, *y_edges), "gy")
    owned, message = place(
        groups * owners, cy, own, counts, got, slot_of.reshape(-1, LANES), previous, v
    )
    shared = lax.all_to_all(message, ("gx", "gy"), 0, 0, tiled=True)
    field = both_sweeps(*fluid, *faces, *y_edges, *far_edges)
    coupled = solve(groups, counts, shared, owned, w)
    return (field, coupled)


def solution(mesh):
    placed = (
        P("gx", "gy", None),
        P("gx", "gy", None),
        P("gx", "gy", None),
        P(None, ("gx", "gy")),
        P(None, ("gx", "gy")),
        P("gx", None),
        P(("gx", "gy")),
        P(None, ("gx", "gy")),
        P(None, None, ("gx", "gy")),
        P(None, None, ("gx", "gy")),
    )
    return jax.shard_map(
        shards,
        mesh=mesh,
        in_specs=placed,
        out_specs=(P("gx", "gy", None), P(None, ("gx", "gy"))),
        check_vma=False,
    )
```

time: 70.7 us -> 48.9 us (0.69); the launches traced: 69.5 us -> 48.6 us
  blocking collectives: 11.7 us -> 0 us
  local copies, waits for them, and re-layouts: 11.1 us -> 0.03 us
  waiting for transfers between devices: 0.02 us -> 6.58 us
  other arithmetic: 4.22 us -> 0 us
  Pallas kernels: 22.7 us -> 19.5 us
  starting transfers between devices: 18.3 us -> 21 us
    all_to_all x1 -> x0, blocking collectives: 11.7 us -> none  [shards(): shared = lax.all_to_all(message, ('gx', 'gy'), 0, 0, tiled=True)]
    unnamed x17 -> x12, local copies, waits for them, and re-layouts: 10.3 us -> 0.03 us
    ppermute x6, starting transfers between devices: 12.5 us -> 7.12 us  [the longest x3 5.15 us: traded(): lax.ppermute(first, axis, pairs(count, 0))]
    all_to_all x1, waiting for transfers between devices: 0.01 us -> 4.95 us  [shards(): got = lax.all_to_all(block, 'gy', 0, 0, tiled=True)]
    all_to_all x0 -> x1, starting transfers between devices: none -> 4.21 us  [shards(): shared = lax.all_to_all(message, ('gx', 'gy'), 0, 0, tiled=True)]
    all_to_all x1, starting transfers between devices: 5.81 us -> 9.67 us  [shards(): got = lax.all_to_all(block, 'gy', 0, 0, tiled=True)]
    select_n x6 -> x0, other arithmetic: 3.4 us -> none  [the longest x3 1.7 us: swap(): first = lax.ppermute(jnp.where(even, tail, head), axis, pairs(count, 0))]
    pallas_call x1, Pallas kernels: 3 us -> 1.15 us  [gram_tile(): pl.pallas_call(gram_kernel, out_shape=jax.ShapeDtypeStruct((columns * col...]
  transfers between devices with their start and end apart: 7 -> 8, of which waited for: 0 -> 3; matrix products, arithmetic and copies ran while one was open for 6% -> 0% of each run, Pallas kernels for 25% -> 26%
where the time goes in v3:
time: 48.9 us; the launch traced here: 48.6 us
  starting transfers between devices  21 us (43%)
  Pallas kernels  19.5 us (40%)
  waiting for transfers between devices  6.58 us (13%)
  between operations  1.45 us (3%)
    all_to_all x1, starting transfers between devices, shards(): got = lax.all_to_all(block, 'gy', 0, 0, tiled=True)  9.67 us
    pallas_call x1, Pallas kernels, both_sweeps(): pl.pallas_call(sweeps_kernel, out_shape=jax.ShapeDtypeStruct(p.shape, F32...  6.01 us
    ppermute x3, starting transfers between devices, traded(): lax.ppermute(first, axis, pairs(count, 0))  5.15 us
    all_to_all x1, waiting for transfers between devices, shards(): got = lax.all_to_all(block, 'gy', 0, 0, tiled=True)  4.95 us
    all_to_all x1, starting transfers between devices, shards(): shared = lax.all_to_all(message, ('gx', 'gy'), 0, 0, tiled=True)  4.21 us
    pallas_call x1, Pallas kernels, solve(): pl.pallas_call(functools.partial(solve_kernel, groups), out_shape=jax.Sha...  3.89 us
    pallas_call x1, Pallas kernels, place(): pl.pallas_call(functools.partial(place_kernel, cy), out_shape=(jax.ShapeD...  3.62 us
    pallas_call x1, Pallas kernels, slab(): pl.pallas_call(slab_kernel, out_shape=(jax.ShapeDtypeStruct((8, cx * cy),...  2.08 us
  transfers between devices with their start and end apart: 8, of which 3 were waited for; matrix products, arithmetic and copies ran while one was open for 0% of the time, Pallas kernels for 26%

profile of v3, /device:TPU:0, one launch (start us, length us, event | category | flops | bytes accessed | tf_op | source)
XLA Modules:
  0.0 48.6 jit_solution(13529200169811850221)
XLA Ops:
  0.7 2.1 %slab.1 = (f32[8,1024]{1,0:T(8,128)S(1)}, f32[72,512]{1,0:T(8,128)S(1)}, f32[72,512]{1,0:T(8,128)S(1)}, f32[64,512]{1,0:T(8,128)S(1)}, f32[64,512]{1,0:T(8,128)S(1)}) custom-call(s32[1]{0:T(128)} %bitcast.even_x_ref.even_ref, s32[1]{0:T(128)} %bitcast.1.even_y_ref, f32[64,16,512]{2,1,0:T(8,128)} %p_ref.5, f32[64,16,512]{2,1,0:T(8,128)} %d_ref.5, ...), custom_call_target="tpu_custom_call" | custom-call | tf_op jit(solution)/shard_map/slab/pallas_call | solution.py:153
  2.8 0.5 collective-permute-start
  3.2 0.7 %collective-permute-start.1 = (f32[72,512]{1,0:T(8,128)S(1)}, f32[72,512]{1,0:T(8,128)S(1)}, u32[]{:S(2)}, u32[]{:S(2)}) collective-permute-start(f32[72,512]{1,0:T(8,128)S(1)} %get-tuple-element.16), channel_id=1, source_target_pairs={{8,16},{16,8},{9,17},{17,9},{10,18},{18,10},{11,19},{19,11},{12,20... | collective-permute-start | bytes 442376 | tf_op jit(solution)/shard_map/ppermute | solution.py:27
  3.9 2.6 %collective-permute-start.2 = (f32[64,512]{1,0:T(8,128)S(1)}, f32[64,512]{1,0:T(8,128)S(1)}, u32[]{:S(2)}, u32[]{:S(2)}) collective-permute-start(f32[64,512]{1,0:T(8,128)S(1)} %get-tuple-element.17), channel_id=1, source_target_pairs={{0,1},{1,0},{2,3},{3,2},{4,5},{5,4},{6,7},{7,6},{8,9},{9,8},{10,11... | collective-permute-start | bytes 393224 | tf_op jit(solution)/shard_map/ppermute | solution.py:27
  6.5 0.7 %collective-permute-start.3 = (f32[64,512]{1,0:T(8,128)S(1)}, f32[64,512]{1,0:T(8,128)S(1)}, u32[]{:S(2)}, u32[]{:S(2)}) collective-permute-start(f32[64,512]{1,0:T(8,128)S(1)} %get-tuple-element.18), channel_id=1, source_target_pairs={{1,2},{2,1},{3,4},{4,3},{5,6},{6,5},{9,10},{10,9},{11,12},{12,11},... | collective-permute-start | bytes 393224 | tf_op jit(solution)/shard_map/ppermute | solution.py:27
  7.9 1.1 %gram.1.gram_ref = f32[8,128]{1,0:T(8,128)S(1)} custom-call(s32[1]{0:T(128)S(6)} %copy.12.count_ref, f32[3,32,3072]{2,1,0:T(8,128)S(1)} %bitcast.6), custom_call_target="tpu_custom_call" | custom-call | tf_op jit(solution)/shard_map/gram/pallas_call | solution.py:53
  9.0 0.5 collective-permute-done.2.y_first_ref
  9.5 0.0 collective-permute-done.3.y_second_ref
  9.5 0.0 collective-permute-done.1.second_ref
  9.5 1.0 %surface.1 = f32[8,56,128]{2,1,0:T(8,128)} custom-call(s32[1]{0:T(128)} %bitcast.even_x_ref.even_ref, f32[8,1024]{1,0:T(8,128)S(1)} %get-tuple-element.25.planes_ref, f32[72,512]{1,0:T(8,128)S(1)} %collective-permute-done.first_ref, f32[72,512]{1,0:T(8,128)S(1)} %collective-permute-done.1.second_ref, f32[3,1024]{1,0:T(4,128)S(1)} %copy-done.4, ...), custom_call_target="tpu_custom_call" | custom-call | tf_op jit(solution)/shard_map/surface/pallas_call | solution.py:239
  10.5 9.7 %all-to-all-start = ((f32[8,56,128]{2,1,0:T(8,128)}), f32[8,56,128]{2,1,0:T(8,128)S(1)}, u32[]{:S(2)}, u32[]{:S(2)}) async-start(f32[8,56,128]{2,1,0:T(8,128)} %surface.1), calls=%async_computation | async-start | bytes 458752 | tf_op jit(solution)/shard_map/all_to_all | solution.py:581
  20.2 0.0 copy-start.3
  20.2 1.8 %edges.1 = (f32[72,512]{1,0:T(8,128)S(1)}, f32[72,512]{1,0:T(8,128)S(1)}) custom-call(s32[1]{0:T(128)} %bitcast.even_x_ref.even_ref, s32[1]{0:T(128)} %bitcast.1.even_y_ref, f32[64,16,512]{2,1,0:T(8,128)} %p_ref.5, f32[64,16,512]{2,1,0:T(8,128)} %d_ref.5, f32[64,16,512]{2,1,0:T(8,128)} %g_ref.5, f32[72,512]{1,0:T(8,128)S(1)} %collective-permute-done.first_ref, ...), custom_call_target="tpu_custom_call" | custom-call | tf_op jit(solution)/shard_map/edges/pallas_call | solution.py:455
  22.0 2.1 %collective-permute-start.4 = (f32[72,512]{1,0:T(8,128)S(1)}, f32[72,512]{1,0:T(8,128)S(1)}, u32[]{:S(2)}, u32[]{:S(2)}) collective-permute-start(f32[72,512]{1,0:T(8,128)S(1)} %get-tuple-element.23), channel_id=1, source_target_pairs={{0,1},{1,0},{2,3},{3,2},{4,5},{5,4},{6,7},{7,6},{8,9},{9,8},{10,11... | collective-permute-start | bytes 442376 | tf_op jit(solution)/shard_map/ppermute | solution.py:27
  24.0 0.7 %collective-permute-start.5 = (f32[72,512]{1,0:T(8,128)S(1)}, f32[72,512]{1,0:T(8,128)S(1)}, u32[]{:S(2)}, u32[]{:S(2)}) collective-permute-start(f32[72,512]{1,0:T(8,128)S(1)} %get-tuple-element.24), channel_id=1, source_target_pairs={{1,2},{2,1},{3,4},{4,3},{5,6},{6,5},{9,10},{10,9},{11,12},{12,11},... | collective-permute-start | bytes 442376 | tf_op jit(solution)/shard_map/ppermute | solution.py:27
  24.7 5.0 %all-to-all-done.got_ref = f32[8,56,128]{2,1,0:T(8,128)S(1)} async-done(((f32[8,56,128]{2,1,0:T(8,128)}), f32[8,56,128]{2,1,0:T(8,128)S(1)}, u32[]{:S(2)}, u32[]{:S(2)}) %all-to-all-start) | async-done | bytes 229408 | tf_op jit(solution)/shard_map/all_to_all | solution.py:581
  29.6 3.6 %place.1 = (f32[3,3072]{1,0:T(4,128)S(1)}, f32[32,1,256]{2,1,0:T(1,128)}) custom-call(s32[1]{0:T(128)} %bitcast.2.place_ref, s32[1]{0:T(128)S(6)} %copy.12.count_ref, f32[8,56,128]{2,1,0:T(8,128)S(1)} %all-to-all-done.got_ref, s32[64,128]{1,0:T(8,128)S(1)} %bitcast.9, f32[3,3072]{1,0:T(4,128)S(1)} %copy-done.2, f32[3,32,3072]{2,1,0:T(8,128)S(1)} %bitcast.7), custom_call_target="tpu_custom_call" | custom-call | tf_op jit(solution)/shard_map/place/pallas_call | solution.py:346
  33.3 4.2 %all-to-all-start.1 = ((f32[32,1,256]{2,1,0:T(1,128)}), f32[32,1,256]{2,1,0:T(1,128)S(1)}, u32[]{:S(2)}, u32[]{:S(2)}) async-start(f32[32,1,256]{2,1,0:T(1,128)} %get-tuple-element.26), calls=%async_computation.1 | async-start | bytes 65536 | tf_op jit(solution)/shard_map/all_to_all | solution.py:586
  37.5 0.0 copy-start.1
  37.5 0.0 collective-permute-done.4.far_first_ref
  37.5 0.0 collective-permute-done.5.far_second_ref
  37.5 6.0 %sweeps.1 = f32[64,16,512]{2,1,0:T(8,128)} custom-call(s32[1]{0:T(128)} %bitcast.even_x_ref.even_ref, s32[1]{0:T(128)} %bitcast.1.even_y_ref, f32[64,16,512]{2,1,0:T(8,128)} %p_ref.5, f32[64,16,512]{2,1,0:T(8,128)} %d_ref.5, f32[64,16,512]{2,1,0:T(8,128)} %g_ref.5, f32[72,512]{1,0:T(8,128)S(1)} %collective-permute-done.first_ref, ...), custom_call_target="tpu_custom_call" | custom-call | tf_op jit(solution)/shard_map/sweeps/pallas_call | solution.py:548
  43.5 1.1 %all-to-all-done.1.got_ref = f32[32,1,256]{2,1,0:T(1,128)S(1)} async-done(((f32[32,1,256]{2,1,0:T(1,128)}), f32[32,1,256]{2,1,0:T(1,128)S(1)}, u32[]{:S(2)}, u32[]{:S(2)}) %all-to-all-start.1) | async-done | bytes 32800 | tf_op jit(solution)/shard_map/all_to_all | solution.py:586
  44.7 3.9 %solve.1 = f32[3,3072]{1,0:T(4,128)} custom-call(s32[1]{0:T(128)S(6)} %copy.12.count_ref, f32[32,1,256]{2,1,0:T(1,128)S(1)} %all-to-all-done.1.got_ref, f32[3,3072]{1,0:T(4,128)S(1)} %get-tuple-element.27.owned_ref, f32[3,32,3072]{2,1,0:T(8,128)S(1)} %bitcast.8), custom_call_target="tpu_custom_call" | custom-call | tf_op jit(solution)/shard_map/solve/pallas_call | solution.py:394
  (11 shorter events, 0.0 us)
Async XLA Ops:
  0.7 7.2 %copy-start = (f32[32,3,3072]{2,0,1:T(8,128)S(1)}, f32[32,3,3072]{2,0,1:T(8,128)}, u32[]{:S(2)}) copy-start(f32[32,3,3072]{2,0,1:T(8,128)} %param.18) | copy-start | bytes 3538948
  0.7 8.8 %copy-start.4 = (f32[3,1024]{1,0:T(4,128)S(1)}, f32[3,1024]{1,0:T(4,128)}, u32[]{:S(2)}) copy-start(f32[3,1024]{1,0:T(4,128)} %normals_ref.1) | copy-start | bytes 36868
  0.7 8.8 %copy-start.5 = (f32[3,1024]{1,0:T(4,128)S(1)}, f32[3,1024]{1,0:T(4,128)}, u32[]{:S(2)}) copy-start(f32[3,1024]{1,0:T(4,128)} %traction_ref.1) | copy-start | bytes 36868
  2.8 6.7 %collective-permute-start = (f32[72,512]{1,0:T(8,128)S(1)}, f32[72,512]{1,0:T(8,128)S(1)}, u32[]{:S(2)}, u32[]{:S(2)}) collective-permute-start(f32[72,512]{1,0:T(8,128)S(1)} %get-tuple-element.15), channel_id=1, source_target_pairs={{0,8},{8,0},{16,24},{24,16},{1,9},{9,1},{17,25},{25,17},{2,10},{10... | collective-permute-start | bytes 442376 | tf_op jit(solution)/shard_map/ppermute | solution.py:27
  3.2 6.3 %collective-permute-start.1 = (f32[72,512]{1,0:T(8,128)S(1)}, f32[72,512]{1,0:T(8,128)S(1)}, u32[]{:S(2)}, u32[]{:S(2)}) collective-permute-start(f32[72,512]{1,0:T(8,128)S(1)} %get-tuple-element.16), channel_id=1, source_target_pairs={{8,16},{16,8},{9,17},{17,9},{10,18},{18,10},{11,19},{19,11},{12,20... | collective-permute-start | bytes 442376 | tf_op jit(solution)/shard_map/ppermute | solution.py:27
  3.9 5.6 %collective-permute-start.2 = (f32[64,512]{1,0:T(8,128)S(1)}, f32[64,512]{1,0:T(8,128)S(1)}, u32[]{:S(2)}, u32[]{:S(2)}) collective-permute-start(f32[64,512]{1,0:T(8,128)S(1)} %get-tuple-element.17), channel_id=1, source_target_pairs={{0,1},{1,0},{2,3},{3,2},{4,5},{5,4},{6,7},{7,6},{8,9},{9,8},{10,11... | collective-permute-start | bytes 393224 | tf_op jit(solution)/shard_map/ppermute | solution.py:27
  6.5 3.0 %collective-permute-start.3 = (f32[64,512]{1,0:T(8,128)S(1)}, f32[64,512]{1,0:T(8,128)S(1)}, u32[]{:S(2)}, u32[]{:S(2)}) collective-permute-start(f32[64,512]{1,0:T(8,128)S(1)} %get-tuple-element.18), channel_id=1, source_target_pairs={{1,2},{2,1},{3,4},{4,3},{5,6},{6,5},{9,10},{10,9},{11,12},{12,11},... | collective-permute-start | bytes 393224 | tf_op jit(solution)/shard_map/ppermute | solution.py:27
  10.5 19.2 %all-to-all-start = ((f32[8,56,128]{2,1,0:T(8,128)}), f32[8,56,128]{2,1,0:T(8,128)S(1)}, u32[]{:S(2)}, u32[]{:S(2)}) async-start(f32[8,56,128]{2,1,0:T(8,128)} %surface.1), calls=%async_computation | async-start | bytes 458752 | tf_op jit(solution)/shard_map/all_to_all | solution.py:581
  20.2 9.5 %copy-start.2 = (f32[3,3072]{1,0:T(4,128)S(1)}, f32[3,3072]{1,0:T(4,128)}, u32[]{:S(2)}) copy-start(f32[3,3072]{1,0:T(4,128)} %previous_ref.1) | copy-start | bytes 110596
  20.2 9.5 %copy-start.3 = (s32[1,8192]{1,0:T(1,128)S(1)}, s32[1,8192]{1,0:T(1,128)}, u32[]{:S(2)}) copy-start(s32[1,8192]{1,0:T(1,128)} %param.15) | copy-start | bytes 98308
  22.0 15.5 %collective-permute-start.4 = (f32[72,512]{1,0:T(8,128)S(1)}, f32[72,512]{1,0:T(8,128)S(1)}, u32[]{:S(2)}, u32[]{:S(2)}) collective-permute-start(f32[72,512]{1,0:T(8,128)S(1)} %get-tuple-element.23), channel_id=1, source_target_pairs={{0,1},{1,0},{2,3},{3,2},{4,5},{5,4},{6,7},{7,6},{8,9},{9,8},{10,11... | collective-permute-start | bytes 442376 | tf_op jit(solution)/shard_map/ppermute | solution.py:27
  24.0 13.5 %collective-permute-start.5 = (f32[72,512]{1,0:T(8,128)S(1)}, f32[72,512]{1,0:T(8,128)S(1)}, u32[]{:S(2)}, u32[]{:S(2)}) collective-permute-start(f32[72,512]{1,0:T(8,128)S(1)} %get-tuple-element.24), channel_id=1, source_target_pairs={{1,2},{2,1},{3,4},{4,3},{5,6},{6,5},{9,10},{10,9},{11,12},{12,11},... | collective-permute-start | bytes 442376 | tf_op jit(solution)/shard_map/ppermute | solution.py:27
  33.3 11.4 %all-to-all-start.1 = ((f32[32,1,256]{2,1,0:T(1,128)}), f32[32,1,256]{2,1,0:T(1,128)S(1)}, u32[]{:S(2)}, u32[]{:S(2)}) async-start(f32[32,1,256]{2,1,0:T(1,128)} %get-tuple-element.26), calls=%async_computation.1 | async-start | bytes 65536 | tf_op jit(solution)/shard_map/all_to_all | solution.py:586
  37.5 7.2 %copy-start.1 = (f32[32,3,3072]{2,0,1:T(8,128)S(1)}, f32[32,3,3072]{2,0,1:T(8,128)}, u32[]{:S(2)}) copy-start(f32[32,3,3072]{2,0,1:T(8,128)} %param.19) | copy-start | bytes 3538948

commit v4 on v3

--- a/solution.py
+++ b/solution.py
@@ -60,14 +60,81 @@
     )(counts, v)
 
 
-def slab_kernel(
-    even_x_ref, even_y_ref, p_ref, d_ref, g_ref, planes_ref, first_ref, second_ref, y_first_ref, y_second_ref,
-    held, ratios, tile_sems, face_sems, y_sems,
+def faces_kernel(
+    even_x_ref, even_y_ref, p_ref, d_ref, g_ref, first_ref, second_ref, y_first_ref, y_second_ref,
+    ratios, face_sems, y_sems,
 ):
+    cx, cy, cz = p_ref.shape
+    even_x, even_y = even_x_ref[0] == 1, even_y_ref[0] == 1
+
+    def face(out_ref, side, sources):
+        return [
+            pltpu.make_async_copy(
+                ref.at[plane],
+                ratios.at[side] if k == 3 else out_ref.at[pl.ds(k * cy, cy)],
+                face_sems.at[side, k],
+            )
+            for k, (ref, plane) in enumerate(sources)
+        ]
+
+    def edge(out_ref, y, at):
+        return pltpu.make_async_copy(p_ref.at[:, y, :], out_ref, y_sems.at[at])
+
+    head = ((p_ref, 0), (p_ref, 1), (d_ref, 0), (g_ref, 0))
+    tail = ((p_ref, cx - 1), (p_ref, cx - 2), (d_ref, cx - 1), (g_ref, cx - 1))
+
+    @pl.when(even_x)
+    def _():
+        for copy in face(second_ref, 0, head) + face(first_ref, 1, tail):
+            copy.start()
+
+    @pl.when(~even_x)
+    def _():
+        for copy in face(first_ref, 0, head) + face(second_ref, 1, tail):
+            copy.start()
+
+    @pl.when(even_y)
+    def _():
+        edge(y_first_ref, cy - 1, 0).start()
+        edge(y_second_ref, 0, 1).start()
+
+    @pl.when(~even_y)
+    def _():
+        edge(y_first_ref, 0, 0).start()
+        edge(y_second_ref, cy - 1, 1).start()
+
+    for copy in face(first_ref, 0, head) + face(first_ref, 1, tail):
+        copy.wait()
+    low, high = 1.0 / (6.0 + ratios[0]), 1.0 / (6.0 + ratios[1])
+    for out_ref, above in ((first_ref, even_x), (second_ref, ~even_x)):
+        out_ref[3 * cy :] = jnp.where(above, high, low)
+    edge(y_first_ref, 0, 0).wait()
+    edge(y_second_ref, 0, 1).wait()
+
+
+def outer_faces(even_x, even_y, p, d, g):
+    cx, cy, cz = p.shape
+    face = jax.ShapeDtypeStruct((4 * cy, cz), F32)
+    edge = jax.ShapeDtypeStruct((cx, cz), F32)
+    return pl.pallas_call(
+        faces_kernel,
+        out_shape=(face, face, edge, edge),
+        in_specs=[SMEM, SMEM] + [ANY] * 3,
+        out_specs=(VMEM,) * 4,
+        scratch_shapes=[
+            pltpu.VMEM((2, cy, cz), F32),
+            pltpu.SemaphoreType.DMA((2, 4)),
+            pltpu.SemaphoreType.DMA((2,)),
+        ],
+        compiler_params=limit(8),
+        name="faces",
+    )(even_x, even_y, in_hbm(p), in_hbm(d), in_hbm(g))
+
+
+def slab_kernel(p_ref, d_ref, g_ref, planes_ref, columns_ref, held, tile_sems, column_sems):
     cx, cy, cz = p_ref.shape
     step = LANES // cy
     half = cx // 2
-    even, even_y = even_x_ref[0] == 1, even_y_ref[0] == 1
     fetches = []
     for part in range(2):
         for which, ref in enumerate((p_ref, d_ref, g_ref)):
@@ -77,45 +144,12 @@
                     ref.at[at, :, pl.ds(cz - LANES, LANES)], held.at[which, at], tile_sems.at[part, which]
                 )
             )
+    for side, (outer, inner) in enumerate(((0, 1), (cy - 1, cy - 2))):
+        for k, (ref, y) in enumerate(((p_ref, outer), (p_ref, inner), (d_ref, outer), (g_ref, outer))):
+            at = 4 * side + k
+            fetches.append(pltpu.make_async_copy(ref.at[:, y, :], columns_ref.at[at], column_sems.at[at]))
     for fetch in fetches:
         fetch.start()
-
-    def face(out_ref, side, sources):
-        return [
-            pltpu.make_async_copy(
-                ref.at[plane],
-                ratios.at[side] if k == 3 else out_ref.at[pl.ds(k * cy, cy)],
-                face_sems.at[side, k],
-            )
-            for k, (ref, plane) in enumerate(sources)
-        ]
-
-    head = ((p_ref, 0), (p_ref, 1), (d_ref, 0), (g_ref, 0))
-    tail = ((p_ref, cx - 1), (p_ref, cx - 2), (d_ref, cx - 1), (g_ref, cx - 1))
-
-    @pl.when(even)
-    def _():
-        for copy in face(second_ref, 0, head) + face(first_ref, 1, tail):
-            copy.start()
-
-    @pl.when(~even)
-    def _():
-        for copy in face(first_ref, 0, head) + face(second_ref, 1, tail):
-            copy.start()
-
-    def edge(out_ref, y, at):
-        return pltpu.make_async_copy(p_ref.at[:, y, :], out_ref, y_sems.at[at])
-
-    @pl.when(even_y)
-    def _():
-        edge(y_first_ref, cy - 1, 0).start()
-        edge(y_second_ref, 0, 1).start()
-
-    @pl.when(~even_y)
-    def _():
-        edge(y_first_ref, 0, 0).start()
-        edge(y_second_ref, cy - 1, 1).start()
-
     planes_ref[7:8] = jnp.zeros((1, cx * cy), F32)
     for part in range(2):
         for fetch in fetches[3 * part : 3 * part + 3]:
@@ -126,45 +160,37 @@
             for row, (which, back) in enumerate(((0, 1), (0, 2), (0, 3), (1, 1), (1, 2), (2, 1), (2, 2))):
                 line = turned[which][LANES - back : LANES - back + 1]
                 planes_ref[row : row + 1, lanes] = 1.0 / (6.0 + line) if which == 2 else line
-    for copy in face(first_ref, 0, head) + face(first_ref, 1, tail):
-        copy.wait()
-    edge(y_first_ref, 0, 0).wait()
-    edge(y_second_ref, 0, 1).wait()
-    low, high = 1.0 / (6.0 + ratios[0]), 1.0 / (6.0 + ratios[1])
-    own_low, own_high = planes_ref[:, :LANES], planes_ref[:, cx * cy - LANES :]
-    for out_ref, above in ((first_ref, even), (second_ref, ~even)):
-        out_ref[3 * cy : 4 * cy] = jnp.where(above, high, low)
-        out_ref[4 * cy :] = jnp.zeros((8, cz), F32)
-        out_ref[4 * cy :, :LANES] = jnp.where(above, own_high, own_low)
-
-
-def in_hbm(array):
-    return pltpu.with_memory_space_constraint(array, pltpu.HBM)
-
-
-def limit(mib):
-    return pltpu.CompilerParams(vmem_limit_bytes=mib * 1024 * 1024)
-
-
-def slab(even_x, even_y, p, d, g):
+    for fetch in fetches[6:]:
+        fetch.wait()
+
+
+def slab(p, d, g):
     cx, cy, cz = p.shape
-    face = jax.ShapeDtypeStruct((4 * cy + 8, cz), F32)
-    edge = jax.ShapeDtypeStruct((cx, cz), F32)
     return pl.pallas_call(
         slab_kernel,
-        out_shape=(jax.ShapeDtypeStruct((8, cx * cy), F32), face, face, edge, edge),
-        in_specs=[SMEM, SMEM] + [ANY] * 3,
-        out_specs=(VMEM,) * 5,
+        out_shape=(pltpu.VMEM((8, cx * cy), F32), pltpu.VMEM((8, cx, cz), F32)),
+        in_specs=[ANY] * 3,
+        out_specs=(VMEM, VMEM),
         scratch_shapes=[
             pltpu.VMEM((3, cx, cy, LANES), F32),
-            pltpu.VMEM((2, cy, cz), F32),
             pltpu.SemaphoreType.DMA((2, 3)),
-            pltpu.SemaphoreType.DMA((2, 4)),
-            pltpu.SemaphoreType.DMA((2,)),
+            pltpu.SemaphoreType.DMA((8,)),
         ],
         compiler_params=limit(8),
         name="slab",
-    )(even_x, even_y, in_hbm(p), in_hbm(d), in_hbm(g))
+    )(in_hbm(p), in_hbm(d), in_hbm(g))
+
+
+def in_hbm(array):
+    return pltpu.with_memory_space_constraint(array, pltpu.HBM)
+
+
+def in_vmem(array):
+    return pltpu.with_memory_space_constraint(array, pltpu.VMEM)
+
+
+def limit(mib):
+    return pltpu.CompilerParams(vmem_limit_bytes=mib * 1024 * 1024)
 
 
 def rolled(block, shift, axis=1):
@@ -182,11 +208,23 @@
 def surface_kernel(cy, even_ref, planes_ref, first_ref, second_ref, normals_ref, traction_ref, gram_ref, out_ref, scratch):
     rows = planes_ref.shape[1]
     tiles = rows // LANES
-    first, second = first_ref[4 * cy :, :LANES], second_ref[4 * cy :, :LANES]
+    first, second = first_ref[:, first_ref.shape[1] - LANES :], second_ref[:, first_ref.shape[1] - LANES :]
     even = even_ref[0] == 1
-    ext = jnp.concatenate(
-        [jnp.where(even, second, first), planes_ref[...], jnp.where(even, first, second)], axis=1
-    )
+    lane = iota((8, LANES), 1)
+
+    def tile(face, above):
+        turned = jnp.concatenate([face, jnp.zeros((LANES - face.shape[0], LANES), F32)], axis=0).T[LANES - 8 :]
+        nearest = turned if above else rolled(turned, -cy)
+        at = lambda k, back: rolled(nearest, -k * cy)[8 - back : 9 - back]
+        blank = jnp.zeros((1, LANES), F32)
+        next_out = turned[7:8] if above else rolled(turned, -3 * cy)[7:8]
+        near = lane[:1] < cy if above else lane[:1] >= LANES - cy
+        return jnp.concatenate(
+            [jnp.where(near, at(0, 1), next_out), at(0, 2), blank, at(2, 1), blank, at(3, 1), blank, blank], axis=0
+        )
+
+    below, above = tile(jnp.where(even, second, first), False), tile(jnp.where(even, first, second), True)
+    ext = jnp.concatenate([below, planes_ref[...], above], axis=1)
     y = lax.rem(iota(ext.shape, 1), cy)
 
     def around(block):
@@ -217,8 +255,7 @@
             scratch[c * tiles + t : c * tiles + t + 1] = forces[c : c + 1, lanes]
         scratch[3 * tiles + t : 3 * tiles + t + 1] = first[0:1, lanes]
         scratch[4 * tiles + t : 4 * tiles + t + 1] = second[0:1, lanes]
-    low, high = ext[:, :LANES], ext[:, LANES + rows :]
-    lane = iota((8, LANES), 1)
+    low, high = below, above
     side = jnp.where(
         lane < cy,
         rolled(low, cy)[0:1],
@@ -244,7 +281,7 @@
         scratch_shapes=[pltpu.VMEM((rows, LANES), F32)],
         compiler_params=limit(8),
         name="surface",
-    )(even, planes, first, second, normals, traction, gram)
+    )(even, in_vmem(planes), first, second, normals, traction, gram)
 
 
 def corrected(cy, got_ref, tiles, forces_ref):
@@ -312,7 +349,7 @@
             left, right, (((1,), (1,)), ((), ())), preferred_element_type=F32
         )
 
-    total = lax.fori_loop(0, sources, one_source, jnp.zeros((6 * high, LANES), F32))
+    total = lax.fori_loop(0, sources, one_source, jnp.zeros((6 * high, LANES), F32), unroll=8)
     owned = total[: 3 * high] + total[3 * high :]
     fetch.wait()
     summed = jnp.zeros((v_ref.shape[1], LANES), F32)
@@ -377,9 +414,30 @@
     right = jnp.sum(jnp.where(rows == lanes, projection, 0.0), axis=1, keepdims=True)
     system = jnp.concatenate([gram, jnp.zeros((columns, LANES - columns), F32)], axis=1)
     system = jnp.where(lanes == columns, right, system)
-    for k in range(columns):
-        pivot_row = system[k : k + 1] / system[k : k + 1, k : k + 1]
-        system = jnp.where(rows == k, pivot_row, system - system[:, k : k + 1] * pivot_row)
+    block = 8
+    for k in range(0, columns, block):
+        pivots = [system[k + i : k + i + 1] for i in range(block)]
+        entry = [
+            [jnp.broadcast_to(pivots[i][:, k + j : k + j + 1], (1, LANES)) for j in range(block)]
+            for i in range(block)
+        ]
+        for i in range(block):
+            inverse = 1.0 / entry[i][i]
+            pivots[i] = pivots[i] * inverse
+            entry[i] = [part * inverse if j > i else part for j, part in enumerate(entry[i])]
+            for m in range(block):
+                if m != i:
+                    share = entry[m][i]
+                    pivots[m] = pivots[m] - share * pivots[i]
+                    entry[m] = [
+                        part - share * entry[i][j] if j > i else part for j, part in enumerate(entry[m])
+                    ]
+        rest = system
+        for i in range(block):
+            rest = rest - system[:, k + i : k + i + 1] * pivots[i]
+        for i in range(block):
+            rest = jnp.where(rows == k + i, pivots[i], rest)
+        system = rest
     coefficient = -system[:, columns : columns + 1]
     fetch.wait()
     for c in range(3):
@@ -420,18 +478,9 @@
 
 
 def edge_kernel(
-    even_x_ref, even_y_ref, p_ref, d_ref, g_ref, first_ref, second_ref, y_first_ref, y_second_ref,
-    to_first_ref, to_second_ref, held, sems,
+    cy, even_x_ref, even_y_ref, held, first_ref, second_ref, y_first_ref, y_second_ref, to_first_ref, to_second_ref
 ):
-    cx, cy, cz = p_ref.shape
-    columns = [(p_ref, 0), (p_ref, 1), (d_ref, 0), (g_ref, 0), (p_ref, cy - 1), (p_ref, cy - 2), (d_ref, cy - 1), (g_ref, cy - 1)]
-    fetches = [
-        pltpu.make_async_copy(ref.at[:, y, :], held.at[k], sems.at[k]) for k, (ref, y) in enumerate(columns)
-    ]
-    for fetch in fetches:
-        fetch.start()
-    for fetch in fetches:
-        fetch.wait()
+    cx, cz = held.shape[1:]
     even_x, even_y = even_x_ref[0] == 1, even_y_ref[0] == 1
     x, z = iota((cx, cz), 0), iota((cx, cz), 1)
     rows = []
@@ -449,18 +498,17 @@
         to_second_ref[at] = jnp.where(even_y, rows[0][k], rows[1][k])
 
 
-def swept_edges(even_x, even_y, p, d, g, first, second, y_first, y_second):
-    cx, cy, cz = p.shape
+def swept_edges(even_x, even_y, cy, columns, first, second, y_first, y_second):
+    cx, cz = columns.shape[1:]
     out = jax.ShapeDtypeStruct((cx + 8, cz), F32)
     return pl.pallas_call(
-        edge_kernel,
+        functools.partial(edge_kernel, cy),
         out_shape=(out, out),
-        in_specs=[SMEM, SMEM] + [ANY] * 3 + [VMEM] * 4,
+        in_specs=[SMEM, SMEM] + [VMEM] * 5,
         out_specs=(VMEM, VMEM),
-        scratch_shapes=[pltpu.VMEM((8, cx, cz), F32), pltpu.SemaphoreType.DMA((8,))],
         compiler_params=limit(8),
         name="edges",
-    )(even_x, even_y, in_hbm(p), in_hbm(d), in_hbm(g), first, second, y_first, y_second)
+    )(even_x, even_y, in_vmem(columns), first, second, y_first, y_second)
 
 
 def sweeps_kernel(
@@ -572,14 +620,15 @@
     own = lax.axis_index("gy").astype(jnp.int32).reshape(1)
     even_x, even_y = [(1 - lax.axis_index(axis) % 2).astype(jnp.int32).reshape(1) for axis in ("gx", "gy")]
     fluid = (even_x, even_y, pressure, divergence, diagonal)
-    planes, first, second, y_first, y_second = slab(*fluid)
+    first, second, y_first, y_second = outer_faces(*fluid)
     faces = traded(first, second, "gx")
     y_edges = traded(y_first, y_second, "gy")
+    planes, columns = slab(pressure, divergence, diagonal)
     faces, y_edges = lax.optimization_barrier((faces, y_edges))
     gram = gram_tile(counts, v)
     block = surface_message(owners, cy, even_x, planes, *faces, normals, traction, gram)
     got = lax.all_to_all(block, "gy", 0, 0, tiled=True)
-    far_edges = traded(*swept_edges(*fluid, *faces, *y_edges), "gy")
+    far_edges = traded(*swept_edges(even_x, even_y, cy, columns, *faces, *y_edges), "gy")
     owned, message = place(
         groups * owners, cy, own, counts, got, slot_of.reshape(-1, LANES), previous, v
     )

time: 48.9 us -> 45.5 us (0.930)
  Pallas kernels: 19.5 us -> 16.3 us
  starting transfers between devices: 21 us -> 20.1 us
  waiting for transfers between devices: 6.58 us -> 7.19 us
    pallas_call x1, Pallas kernels: 3.89 us -> 2.18 us  [solve(): pl.pallas_call(functools.partial(solve_kernel, groups), out_shape=jax.Sha...]
    all_to_all x1, starting transfers between devices: 9.67 us -> 8.08 us  [shards(): got = lax.all_to_all(block, 'gy', 0, 0, tiled=True)]
    pallas_call x1, Pallas kernels: 3.62 us -> 2.32 us  [place(): pl.pallas_call(functools.partial(place_kernel, cy), out_shape=(jax.ShapeD...]
    all_to_all x1, waiting for transfers between devices: 4.95 us -> 6.04 us  [shards(): got = lax.all_to_all(block, 'gy', 0, 0, tiled=True)]
    all_to_all x1, starting transfers between devices: 4.21 us -> 4.73 us  [shards(): shared = lax.all_to_all(message, ('gx', 'gy'), 0, 0, tiled=True)]
    pallas_call x2 -> x3, Pallas kernels: 3.87 us -> 3.49 us  [the longest x1 1.97 us: slab(): pl.pallas_call(slab_kernel, out_shape=(pltpu.VMEM((8, cx * cy), F32), plt...]
  transfers between devices with their start and end apart: 8 -> 8, of which waited for: 3 -> 2; matrix products, arithmetic and copies ran while one was open for 0% -> 0% of each run, Pallas kernels for 26% -> 26%
where the time goes in v4:
time: 45.5 us; the launch traced here: 45.1 us
  starting transfers between devices  20.1 us (44%)
  Pallas kernels  16.3 us (36%)
  waiting for transfers between devices  7.19 us (16%)
  between operations  1.48 us (3%)
    all_to_all x1, starting transfers between devices, shards(): got = lax.all_to_all(block, 'gy', 0, 0, tiled=True)  8.08 us
    all_to_all x1, waiting for transfers between devices, shards(): got = lax.all_to_all(block, 'gy', 0, 0, tiled=True)  6.04 us
    pallas_call x1, Pallas kernels, both_sweeps(): pl.pallas_call(sweeps_kernel, out_shape=jax.ShapeDtypeStruct(p.shape, F32...  6.01 us
    ppermute x3, starting transfers between devices, traded(): lax.ppermute(first, axis, pairs(count, 0))  5.18 us
    all_to_all x1, starting transfers between devices, shards(): shared = lax.all_to_all(message, ('gx', 'gy'), 0, 0, tiled=True)  4.73 us
    pallas_call x1, Pallas kernels, place(): pl.pallas_call(functools.partial(place_kernel, cy), out_shape=(jax.ShapeD...  2.32 us
    pallas_call x1, Pallas kernels, solve(): pl.pallas_call(functools.partial(solve_kernel, groups), out_shape=jax.Sha...  2.18 us
    ppermute x3, starting transfers between devices, traded(): lax.ppermute(second, axis, pairs(count, 1))  2.1 us
  transfers between devices with their start and end apart: 8, of which 2 were waited for; matrix products, arithmetic and copies ran while one was open for 0% of the time, Pallas kernels for 26%

profile of v4, /device:TPU:0, one launch (start us, length us, event | category | flops | bytes accessed | tf_op | source)
XLA Modules:
  0.0 45.1 jit_solution(9730530244530399094)
XLA Ops:
  0.6 1.3 %faces.1 = (f32[64,512]{1,0:T(8,128)S(1)}, f32[64,512]{1,0:T(8,128)S(1)}, f32[64,512]{1,0:T(8,128)S(1)}, f32[64,512]{1,0:T(8,128)S(1)}) custom-call(s32[1]{0:T(128)} %bitcast.even_x_ref.even_ref, s32[1]{0:T(128)} %bitcast.1.even_y_ref, f32[64,16,512]{2,1,0:T(8,128)} %p_ref.5, f32[64,16,512]{2,1,0:T(8,128)} %d_ref.5, f32[64,16,512]{2,1,0:T(8,128)} %g_ref.5), custom_call_target="tpu_custom_call" | custom-call | tf_op jit(solution)/shard_map/faces/pallas_call | solution.py:119
  1.9 0.5 %collective-permute-start = (f32[64,512]{1,0:T(8,128)S(1)}, f32[64,512]{1,0:T(8,128)S(1)}, u32[]{:S(2)}, u32[]{:S(2)}) collective-permute-start(f32[64,512]{1,0:T(8,128)S(1)} %get-tuple-element.16), channel_id=1, source_target_pairs={{0,8},{8,0},{16,24},{24,16},{1,9},{9,1},{17,25},{25,17},{2,10},{10... | collective-permute-start | bytes 393224 | tf_op jit(solution)/shard_map/ppermute | solution.py:27
  2.5 0.7 %collective-permute-start.1 = (f32[64,512]{1,0:T(8,128)S(1)}, f32[64,512]{1,0:T(8,128)S(1)}, u32[]{:S(2)}, u32[]{:S(2)}) collective-permute-start(f32[64,512]{1,0:T(8,128)S(1)} %get-tuple-element.17), channel_id=1, source_target_pairs={{8,16},{16,8},{9,17},{17,9},{10,18},{18,10},{11,19},{19,11},{12,20... | collective-permute-start | bytes 393224 | tf_op jit(solution)/shard_map/ppermute | solution.py:27
  3.1 2.6 %collective-permute-start.2 = (f32[64,512]{1,0:T(8,128)S(1)}, f32[64,512]{1,0:T(8,128)S(1)}, u32[]{:S(2)}, u32[]{:S(2)}) collective-permute-start(f32[64,512]{1,0:T(8,128)S(1)} %get-tuple-element.18), channel_id=1, source_target_pairs={{0,1},{1,0},{2,3},{3,2},{4,5},{5,4},{6,7},{7,6},{8,9},{9,8},{10,11... | collective-permute-start | bytes 393224 | tf_op jit(solution)/shard_map/ppermute | solution.py:27
  5.7 0.8 %collective-permute-start.3 = (f32[64,512]{1,0:T(8,128)S(1)}, f32[64,512]{1,0:T(8,128)S(1)}, u32[]{:S(2)}, u32[]{:S(2)}) collective-permute-start(f32[64,512]{1,0:T(8,128)S(1)} %get-tuple-element.19), channel_id=1, source_target_pairs={{1,2},{2,1},{3,4},{4,3},{5,6},{6,5},{9,10},{10,9},{11,12},{12,11},... | collective-permute-start | bytes 393224 | tf_op jit(solution)/shard_map/ppermute | solution.py:27
  6.5 2.0 %slab.1 = (f32[8,1024]{1,0:T(8,128)S(1)}, f32[8,64,512]{2,1,0:T(8,128)S(1)}) custom-call(f32[64,16,512]{2,1,0:T(8,128)} %p_ref.5, f32[64,16,512]{2,1,0:T(8,128)} %d_ref.5, f32[64,16,512]{2,1,0:T(8,128)} %g_ref.5), custom_call_target="tpu_custom_call" | custom-call | tf_op jit(solution)/shard_map/slab/pallas_call | solution.py:169
  8.5 0.0 copy-start.2
  8.5 0.0 copy-start.3
  9.2 1.1 %gram.1.gram_ref = f32[8,128]{1,0:T(8,128)S(1)} custom-call(s32[1]{0:T(128)S(6)} %copy.12.count_ref, f32[3,32,3072]{2,1,0:T(8,128)S(1)} %bitcast.6), custom_call_target="tpu_custom_call" | custom-call | tf_op jit(solution)/shard_map/gram/pallas_call | solution.py:53
  10.3 0.0 collective-permute-done.first_ref
  10.3 0.0 collective-permute-done.1.second_ref
  10.3 0.0 collective-permute-done.3.y_second_ref
  10.4 1.2 %surface.1 = f32[8,56,128]{2,1,0:T(8,128)} custom-call(s32[1]{0:T(128)} %bitcast.even_x_ref.even_ref, f32[8,1024]{1,0:T(8,128)S(1)} %get-tuple-element.27.planes_ref, f32[64,512]{1,0:T(8,128)S(1)} %collective-permute-done.first_ref, f32[64,512]{1,0:T(8,128)S(1)} %collective-permute-done.1.second_ref, f32[3,1024]{1,0:T(4,128)S(1)} %copy-done.4, ...), custom_call_target="tpu_custom_call" | custom-call | tf_op jit(solution)/shard_map/surface/pallas_call | solution.py:276
  11.5 8.1 %all-to-all-start = ((f32[8,56,128]{2,1,0:T(8,128)}), f32[8,56,128]{2,1,0:T(8,128)S(1)}, u32[]{:S(2)}, u32[]{:S(2)}) async-start(f32[8,56,128]{2,1,0:T(8,128)} %surface.1), calls=%async_computation | async-start | bytes 458752 | tf_op jit(solution)/shard_map/all_to_all | solution.py:630
  19.6 0.3 edges.1
  19.9 2.1 %collective-permute-start.4 = (f32[72,512]{1,0:T(8,128)S(1)}, f32[72,512]{1,0:T(8,128)S(1)}, u32[]{:S(2)}, u32[]{:S(2)}) collective-permute-start(f32[72,512]{1,0:T(8,128)S(1)} %get-tuple-element.25), channel_id=1, source_target_pairs={{0,1},{1,0},{2,3},{3,2},{4,5},{5,4},{6,7},{7,6},{8,9},{9,8},{10,11... | collective-permute-start | bytes 442376 | tf_op jit(solution)/shard_map/ppermute | solution.py:27
  22.0 0.7 %collective-permute-start.5 = (f32[72,512]{1,0:T(8,128)S(1)}, f32[72,512]{1,0:T(8,128)S(1)}, u32[]{:S(2)}, u32[]{:S(2)}) collective-permute-start(f32[72,512]{1,0:T(8,128)S(1)} %get-tuple-element.26), channel_id=1, source_target_pairs={{1,2},{2,1},{3,4},{4,3},{5,6},{6,5},{9,10},{10,9},{11,12},{12,11},... | collective-permute-start | bytes 442376 | tf_op jit(solution)/shard_map/ppermute | solution.py:27
  22.6 6.0 %all-to-all-done.got_ref = f32[8,56,128]{2,1,0:T(8,128)S(1)} async-done(((f32[8,56,128]{2,1,0:T(8,128)}), f32[8,56,128]{2,1,0:T(8,128)S(1)}, u32[]{:S(2)}, u32[]{:S(2)}) %all-to-all-start) | async-done | bytes 229408 | tf_op jit(solution)/shard_map/all_to_all | solution.py:630
  28.7 2.3 %place.1 = (f32[3,3072]{1,0:T(4,128)S(1)}, f32[32,1,256]{2,1,0:T(1,128)}) custom-call(s32[1]{0:T(128)} %bitcast.2.place_ref, s32[1]{0:T(128)S(6)} %copy.12.count_ref, f32[8,56,128]{2,1,0:T(8,128)S(1)} %all-to-all-done.got_ref, s32[64,128]{1,0:T(8,128)S(1)} %bitcast.9, f32[3,3072]{1,0:T(4,128)S(1)} %copy-done.2, f32[3,32,3072]{2,1,0:T(8,128)S(1)} %bitcast.7), custom_call_target="tpu_custom_call" | custom-call | tf_op jit(solution)/shard_map/place/pallas_call | solution.py:383
  31.0 4.7 %all-to-all-start.1 = ((f32[32,1,256]{2,1,0:T(1,128)}), f32[32,1,256]{2,1,0:T(1,128)S(1)}, u32[]{:S(2)}, u32[]{:S(2)}) async-start(f32[32,1,256]{2,1,0:T(1,128)} %get-tuple-element.28), calls=%async_computation.1 | async-start | bytes 65536 | tf_op jit(solution)/shard_map/all_to_all | solution.py:635
  35.7 0.0 copy-start.1
  35.8 6.0 %sweeps.1 = f32[64,16,512]{2,1,0:T(8,128)} custom-call(s32[1]{0:T(128)} %bitcast.even_x_ref.even_ref, s32[1]{0:T(128)} %bitcast.1.even_y_ref, f32[64,16,512]{2,1,0:T(8,128)} %p_ref.5, f32[64,16,512]{2,1,0:T(8,128)} %d_ref.5, f32[64,16,512]{2,1,0:T(8,128)} %g_ref.5, f32[64,512]{1,0:T(8,128)S(1)} %collective-permute-done.first_ref, ...), custom_call_target="tpu_custom_call" | custom-call | tf_op jit(solution)/shard_map/sweeps/pallas_call | solution.py:596
  41.8 1.1 %all-to-all-done.1.got_ref = f32[32,1,256]{2,1,0:T(1,128)S(1)} async-done(((f32[32,1,256]{2,1,0:T(1,128)}), f32[32,1,256]{2,1,0:T(1,128)S(1)}, u32[]{:S(2)}, u32[]{:S(2)}) %all-to-all-start.1) | async-done | bytes 32800 | tf_op jit(solution)/shard_map/all_to_all | solution.py:635
  42.9 2.2 %solve.1 = f32[3,3072]{1,0:T(4,128)} custom-call(s32[1]{0:T(128)S(6)} %copy.12.count_ref, f32[32,1,256]{2,1,0:T(1,128)S(1)} %all-to-all-done.1.got_ref, f32[3,3072]{1,0:T(4,128)S(1)} %get-tuple-element.29.owned_ref, f32[3,32,3072]{2,1,0:T(8,128)S(1)} %bitcast.8), custom_call_target="tpu_custom_call" | custom-call | tf_op jit(solution)/shard_map/solve/pallas_call | solution.py:452
  (12 shorter events, 0.0 us)
Async XLA Ops:
  1.9 8.4 %collective-permute-start = (f32[64,512]{1,0:T(8,128)S(1)}, f32[64,512]{1,0:T(8,128)S(1)}, u32[]{:S(2)}, u32[]{:S(2)}) collective-permute-start(f32[64,512]{1,0:T(8,128)S(1)} %get-tuple-element.16), channel_id=1, source_target_pairs={{0,8},{8,0},{16,24},{24,16},{1,9},{9,1},{17,25},{25,17},{2,10},{10... | collective-permute-start | bytes 393224 | tf_op jit(solution)/shard_map/ppermute | solution.py:27
  2.5 7.9 %collective-permute-start.1 = (f32[64,512]{1,0:T(8,128)S(1)}, f32[64,512]{1,0:T(8,128)S(1)}, u32[]{:S(2)}, u32[]{:S(2)}) collective-permute-start(f32[64,512]{1,0:T(8,128)S(1)} %get-tuple-element.17), channel_id=1, source_target_pairs={{8,16},{16,8},{9,17},{17,9},{10,18},{18,10},{11,19},{19,11},{12,20... | collective-permute-start | bytes 393224 | tf_op jit(solution)/shard_map/ppermute | solution.py:27
  3.1 7.2 %collective-permute-start.2 = (f32[64,512]{1,0:T(8,128)S(1)}, f32[64,512]{1,0:T(8,128)S(1)}, u32[]{:S(2)}, u32[]{:S(2)}) collective-permute-start(f32[64,512]{1,0:T(8,128)S(1)} %get-tuple-element.18), channel_id=1, source_target_pairs={{0,1},{1,0},{2,3},{3,2},{4,5},{5,4},{6,7},{7,6},{8,9},{9,8},{10,11... | collective-permute-start | bytes 393224 | tf_op jit(solution)/shard_map/ppermute | solution.py:27
  5.7 3.5 %copy-start = (f32[32,3,3072]{2,0,1:T(8,128)S(1)}, f32[32,3,3072]{2,0,1:T(8,128)}, u32[]{:S(2)}) copy-start(f32[32,3,3072]{2,0,1:T(8,128)} %param.18) | copy-start | bytes 3538948
  5.7 4.7 %copy-start.4 = (f32[3,1024]{1,0:T(4,128)S(1)}, f32[3,1024]{1,0:T(4,128)}, u32[]{:S(2)}) copy-start(f32[3,1024]{1,0:T(4,128)} %normals_ref.1) | copy-start | bytes 36868
  5.7 4.7 %copy-start.5 = (f32[3,1024]{1,0:T(4,128)S(1)}, f32[3,1024]{1,0:T(4,128)}, u32[]{:S(2)}) copy-start(f32[3,1024]{1,0:T(4,128)} %traction_ref.1) | copy-start | bytes 36868
  5.7 4.6 %collective-permute-start.3 = (f32[64,512]{1,0:T(8,128)S(1)}, f32[64,512]{1,0:T(8,128)S(1)}, u32[]{:S(2)}, u32[]{:S(2)}) collective-permute-start(f32[64,512]{1,0:T(8,128)S(1)} %get-tuple-element.19), channel_id=1, source_target_pairs={{1,2},{2,1},{3,4},{4,3},{5,6},{6,5},{9,10},{10,9},{11,12},{12,11},... | collective-permute-start | bytes 393224 | tf_op jit(solution)/shard_map/ppermute | solution.py:27
  8.5 20.2 %copy-start.2 = (f32[3,3072]{1,0:T(4,128)S(1)}, f32[3,3072]{1,0:T(4,128)}, u32[]{:S(2)}) copy-start(f32[3,3072]{1,0:T(4,128)} %previous_ref.1) | copy-start | bytes 110596
  8.5 20.2 %copy-start.3 = (s32[1,8192]{1,0:T(1,128)S(1)}, s32[1,8192]{1,0:T(1,128)}, u32[]{:S(2)}) copy-start(s32[1,8192]{1,0:T(1,128)} %param.15) | copy-start | bytes 98308
  11.5 17.1 %all-to-all-start = ((f32[8,56,128]{2,1,0:T(8,128)}), f32[8,56,128]{2,1,0:T(8,128)S(1)}, u32[]{:S(2)}, u32[]{:S(2)}) async-start(f32[8,56,128]{2,1,0:T(8,128)} %surface.1), calls=%async_computation | async-start | bytes 458752 | tf_op jit(solution)/shard_map/all_to_all | solution.py:630
  19.9 15.9 %collective-permute-start.4 = (f32[72,512]{1,0:T(8,128)S(1)}, f32[72,512]{1,0:T(8,128)S(1)}, u32[]{:S(2)}, u32[]{:S(2)}) collective-permute-start(f32[72,512]{1,0:T(8,128)S(1)} %get-tuple-element.25), channel_id=1, source_target_pairs={{0,1},{1,0},{2,3},{3,2},{4,5},{5,4},{6,7},{7,6},{8,9},{9,8},{10,11... | collective-permute-start | bytes 442376 | tf_op jit(solution)/shard_map/ppermute | solution.py:27
  22.0 13.8 %collective-permute-start.5 = (f32[72,512]{1,0:T(8,128)S(1)}, f32[72,512]{1,0:T(8,128)S(1)}, u32[]{:S(2)}, u32[]{:S(2)}) collective-permute-start(f32[72,512]{1,0:T(8,128)S(1)} %get-tuple-element.26), channel_id=1, source_target_pairs={{1,2},{2,1},{3,4},{4,3},{5,6},{6,5},{9,10},{10,9},{11,12},{12,11},... | collective-permute-start | bytes 442376 | tf_op jit(solution)/shard_map/ppermute | solution.py:27
  31.0 11.9 %all-to-all-start.1 = ((f32[32,1,256]{2,1,0:T(1,128)}), f32[32,1,256]{2,1,0:T(1,128)S(1)}, u32[]{:S(2)}, u32[]{:S(2)}) async-start(f32[32,1,256]{2,1,0:T(1,128)} %get-tuple-element.28), calls=%async_computation.1 | async-start | bytes 65536 | tf_op jit(solution)/shard_map/all_to_all | solution.py:635
  35.7 7.2 %copy-start.1 = (f32[32,3,3072]{2,0,1:T(8,128)S(1)}, f32[32,3,3072]{2,0,1:T(8,128)}, u32[]{:S(2)}) copy-start(f32[32,3,3072]{2,0,1:T(8,128)} %param.19) | copy-start | bytes 3538948

commit v5 on v4

--- a/solution.py
+++ b/solution.py
@@ -621,10 +621,10 @@
     even_x, even_y = [(1 - lax.axis_index(axis) % 2).astype(jnp.int32).reshape(1) for axis in ("gx", "gy")]
     fluid = (even_x, even_y, pressure, divergence, diagonal)
     first, second, y_first, y_second = outer_faces(*fluid)
+    y_edges = traded(y_first, y_second, "gy")
     faces = traded(first, second, "gx")
-    y_edges = traded(y_first, y_second, "gy")
     planes, columns = slab(pressure, divergence, diagonal)
-    faces, y_edges = lax.optimization_barrier((faces, y_edges))
+    y_edges, faces = lax.optimization_barrier((y_edges, faces))
     gram = gram_tile(counts, v)
     block = surface_message(owners, cy, even_x, planes, *faces, normals, traction, gram)
     got = lax.all_to_all(block, "gy", 0, 0, tiled=True)

time: 45.5 us -> 44.4 us (0.976)
  waiting for transfers between devices: 7.19 us -> 6.2 us
    all_to_all x1, waiting for transfers between devices: 6.04 us -> 5.05 us  [shards(): got = lax.all_to_all(block, 'gy', 0, 0, tiled=True)]
    all_to_all x1, starting transfers between devices: 8.08 us -> 7.58 us  [shards(): got = lax.all_to_all(block, 'gy', 0, 0, tiled=True)]
  transfers between devices with their start and end apart: 8 -> 8, of which waited for: 2 -> 2; matrix products, arithmetic and copies ran while one was open for 0% -> 0% of each run, Pallas kernels for 26% -> 27%
where the time goes in v5:
time: 44.4 us; the launch traced here: 44 us
  starting transfers between devices  20 us (45%)
  Pallas kernels  16.3 us (37%)
  waiting for transfers between devices  6.2 us (14%)
  between operations  1.51 us (3%)
    all_to_all x1, starting transfers between devices, shards(): got = lax.all_to_all(block, 'gy', 0, 0, tiled=True)  7.58 us
    pallas_call x1, Pallas kernels, both_sweeps(): pl.pallas_call(sweeps_kernel, out_shape=jax.ShapeDtypeStruct(p.shape, F32...  6.01 us
    ppermute x3, starting transfers between devices, traded(): lax.ppermute(first, axis, pairs(count, 0))  5.16 us
    all_to_all x1, starting transfers between devices, shards(): shared = lax.all_to_all(message, ('gx', 'gy'), 0, 0, tiled=True)  5.11 us
    all_to_all x1, waiting for transfers between devices, shards(): got = lax.all_to_all(block, 'gy', 0, 0, tiled=True)  5.05 us
    pallas_call x1, Pallas kernels, place(): pl.pallas_call(functools.partial(place_kernel, cy), out_shape=(jax.ShapeD...  2.32 us
    pallas_call x1, Pallas kernels, solve(): pl.pallas_call(functools.partial(solve_kernel, groups), out_shape=jax.Sha...  2.18 us
    ppermute x3, starting transfers between devices, traded(): lax.ppermute(second, axis, pairs(count, 1))  2.12 us
  transfers between devices with their start and end apart: 8, of which 2 were waited for; matrix products, arithmetic and copies ran while one was open for 0% of the time, Pallas kernels for 27%

profile of v5, /device:TPU:0, one launch (start us, length us, event | category | flops | bytes accessed | tf_op | source)
XLA Modules:
  0.0 44.0 jit_solution(11806294211058058937)
XLA Ops:
  0.6 1.3 %faces.1 = (f32[64,512]{1,0:T(8,128)S(1)}, f32[64,512]{1,0:T(8,128)S(1)}, f32[64,512]{1,0:T(8,128)S(1)}, f32[64,512]{1,0:T(8,128)S(1)}) custom-call(s32[1]{0:T(128)} %bitcast.even_x_ref.even_ref, s32[1]{0:T(128)} %bitcast.1.even_y_ref, f32[64,16,512]{2,1,0:T(8,128)} %p_ref.5, f32[64,16,512]{2,1,0:T(8,128)} %d_ref.5, f32[64,16,512]{2,1,0:T(8,128)} %g_ref.5), custom_call_target="tpu_custom_call" | custom-call | tf_op jit(solution)/shard_map/faces/pallas_call | solution.py:119
  1.9 3.0 %collective-permute-start = (f32[64,512]{1,0:T(8,128)S(1)}, f32[64,512]{1,0:T(8,128)S(1)}, u32[]{:S(2)}, u32[]{:S(2)}) collective-permute-start(f32[64,512]{1,0:T(8,128)S(1)} %get-tuple-element.16), channel_id=1, source_target_pairs={{0,1},{1,0},{2,3},{3,2},{4,5},{5,4},{6,7},{7,6},{8,9},{9,8},{10,11... | collective-permute-start | bytes 393224 | tf_op jit(solution)/shard_map/ppermute | solution.py:27
  4.9 0.7 %collective-permute-start.1 = (f32[64,512]{1,0:T(8,128)S(1)}, f32[64,512]{1,0:T(8,128)S(1)}, u32[]{:S(2)}, u32[]{:S(2)}) collective-permute-start(f32[64,512]{1,0:T(8,128)S(1)} %get-tuple-element.17), channel_id=1, source_target_pairs={{1,2},{2,1},{3,4},{4,3},{5,6},{6,5},{9,10},{10,9},{11,12},{12,11},... | collective-permute-start | bytes 393224 | tf_op jit(solution)/shard_map/ppermute | solution.py:27
  5.6 0.1 collective-permute-start.2
  5.7 0.0 copy-start
  5.7 0.0 copy-start.4
  5.7 0.0 copy-start.5
  5.7 0.8 %collective-permute-start.3 = (f32[64,512]{1,0:T(8,128)S(1)}, f32[64,512]{1,0:T(8,128)S(1)}, u32[]{:S(2)}, u32[]{:S(2)}) collective-permute-start(f32[64,512]{1,0:T(8,128)S(1)} %get-tuple-element.19), channel_id=1, source_target_pairs={{8,16},{16,8},{9,17},{17,9},{10,18},{18,10},{11,19},{19,11},{12,20... | collective-permute-start | bytes 393224 | tf_op jit(solution)/shard_map/ppermute | solution.py:27
  6.5 2.0 %slab.1 = (f32[8,1024]{1,0:T(8,128)S(1)}, f32[8,64,512]{2,1,0:T(8,128)S(1)}) custom-call(f32[64,16,512]{2,1,0:T(8,128)} %p_ref.5, f32[64,16,512]{2,1,0:T(8,128)} %d_ref.5, f32[64,16,512]{2,1,0:T(8,128)} %g_ref.5), custom_call_target="tpu_custom_call" | custom-call | tf_op jit(solution)/shard_map/slab/pallas_call | solution.py:169
  8.5 0.0 copy-start.2
  8.5 0.0 copy-start.3
  9.2 1.1 %gram.1.gram_ref = f32[8,128]{1,0:T(8,128)S(1)} custom-call(s32[1]{0:T(128)S(6)} %copy.12.count_ref, f32[3,32,3072]{2,1,0:T(8,128)S(1)} %bitcast.6), custom_call_target="tpu_custom_call" | custom-call | tf_op jit(solution)/shard_map/gram/pallas_call | solution.py:53
  10.4 1.2 %surface.1 = f32[8,56,128]{2,1,0:T(8,128)} custom-call(s32[1]{0:T(128)} %bitcast.even_x_ref.even_ref, f32[8,1024]{1,0:T(8,128)S(1)} %get-tuple-element.27.planes_ref, f32[64,512]{1,0:T(8,128)S(1)} %collective-permute-done.2.first_ref, f32[64,512]{1,0:T(8,128)S(1)} %collective-permute-done.3.second_ref, f32[3,1024]{1,0:T(4,128)S(1)} %copy-done.4, ...), custom_call_target="tpu_custom_call" | custom-call | tf_op jit(solution)/shard_map/surface/pallas_call | solution.py:276
  11.6 7.6 %all-to-all-start = ((f32[8,56,128]{2,1,0:T(8,128)}), f32[8,56,128]{2,1,0:T(8,128)S(1)}, u32[]{:S(2)}, u32[]{:S(2)}) async-start(f32[8,56,128]{2,1,0:T(8,128)} %surface.1), calls=%async_computation | async-start | bytes 458752 | tf_op jit(solution)/shard_map/all_to_all | solution.py:630
  19.1 0.3 edges.1
  19.4 2.1 %collective-permute-start.4 = (f32[72,512]{1,0:T(8,128)S(1)}, f32[72,512]{1,0:T(8,128)S(1)}, u32[]{:S(2)}, u32[]{:S(2)}) collective-permute-start(f32[72,512]{1,0:T(8,128)S(1)} %get-tuple-element.25), channel_id=1, source_target_pairs={{0,1},{1,0},{2,3},{3,2},{4,5},{5,4},{6,7},{7,6},{8,9},{9,8},{10,11... | collective-permute-start | bytes 442376 | tf_op jit(solution)/shard_map/ppermute | solution.py:27
  21.5 0.7 %collective-permute-start.5 = (f32[72,512]{1,0:T(8,128)S(1)}, f32[72,512]{1,0:T(8,128)S(1)}, u32[]{:S(2)}, u32[]{:S(2)}) collective-permute-start(f32[72,512]{1,0:T(8,128)S(1)} %get-tuple-element.26), channel_id=1, source_target_pairs={{1,2},{2,1},{3,4},{4,3},{5,6},{6,5},{9,10},{10,9},{11,12},{12,11},... | collective-permute-start | bytes 442376 | tf_op jit(solution)/shard_map/ppermute | solution.py:27
  22.2 5.0 %all-to-all-done.got_ref = f32[8,56,128]{2,1,0:T(8,128)S(1)} async-done(((f32[8,56,128]{2,1,0:T(8,128)}), f32[8,56,128]{2,1,0:T(8,128)S(1)}, u32[]{:S(2)}, u32[]{:S(2)}) %all-to-all-start) | async-done | bytes 229408 | tf_op jit(solution)/shard_map/all_to_all | solution.py:630
  27.2 2.3 %place.1 = (f32[3,3072]{1,0:T(4,128)S(1)}, f32[32,1,256]{2,1,0:T(1,128)}) custom-call(s32[1]{0:T(128)} %bitcast.2.place_ref, s32[1]{0:T(128)S(6)} %copy.12.count_ref, f32[8,56,128]{2,1,0:T(8,128)S(1)} %all-to-all-done.got_ref, s32[64,128]{1,0:T(8,128)S(1)} %bitcast.9, f32[3,3072]{1,0:T(4,128)S(1)} %copy-done.2, f32[3,32,3072]{2,1,0:T(8,128)S(1)} %bitcast.7), custom_call_target="tpu_custom_call" | custom-call | tf_op jit(solution)/shard_map/place/pallas_call | solution.py:383
  29.5 5.1 %all-to-all-start.1 = ((f32[32,1,256]{2,1,0:T(1,128)}), f32[32,1,256]{2,1,0:T(1,128)S(1)}, u32[]{:S(2)}, u32[]{:S(2)}) async-start(f32[32,1,256]{2,1,0:T(1,128)} %get-tuple-element.28), calls=%async_computation.1 | async-start | bytes 65536 | tf_op jit(solution)/shard_map/all_to_all | solution.py:635
  34.6 0.0 copy-start.1
  34.7 6.0 %sweeps.1 = f32[64,16,512]{2,1,0:T(8,128)} custom-call(s32[1]{0:T(128)} %bitcast.even_x_ref.even_ref, s32[1]{0:T(128)} %bitcast.1.even_y_ref, f32[64,16,512]{2,1,0:T(8,128)} %p_ref.5, f32[64,16,512]{2,1,0:T(8,128)} %d_ref.5, f32[64,16,512]{2,1,0:T(8,128)} %g_ref.5, f32[64,512]{1,0:T(8,128)S(1)} %collective-permute-done.2.first_ref, ...), custom_call_target="tpu_custom_call" | custom-call | tf_op jit(solution)/shard_map/sweeps/pallas_call | solution.py:596
  40.7 1.1 %all-to-all-done.1.got_ref = f32[32,1,256]{2,1,0:T(1,128)S(1)} async-done(((f32[32,1,256]{2,1,0:T(1,128)}), f32[32,1,256]{2,1,0:T(1,128)S(1)}, u32[]{:S(2)}, u32[]{:S(2)}) %all-to-all-start.1) | async-done | bytes 32800 | tf_op jit(solution)/shard_map/all_to_all | solution.py:635
  41.8 2.2 %solve.1 = f32[3,3072]{1,0:T(4,128)} custom-call(s32[1]{0:T(128)S(6)} %copy.12.count_ref, f32[32,1,256]{2,1,0:T(1,128)S(1)} %all-to-all-done.1.got_ref, f32[3,3072]{1,0:T(4,128)S(1)} %get-tuple-element.29.owned_ref, f32[3,32,3072]{2,1,0:T(8,128)S(1)} %bitcast.8), custom_call_target="tpu_custom_call" | custom-call | tf_op jit(solution)/shard_map/solve/pallas_call | solution.py:452
  (12 shorter events, 0.0 us)
Async XLA Ops:
  1.9 8.4 %collective-permute-start = (f32[64,512]{1,0:T(8,128)S(1)}, f32[64,512]{1,0:T(8,128)S(1)}, u32[]{:S(2)}, u32[]{:S(2)}) collective-permute-start(f32[64,512]{1,0:T(8,128)S(1)} %get-tuple-element.16), channel_id=1, source_target_pairs={{0,1},{1,0},{2,3},{3,2},{4,5},{5,4},{6,7},{7,6},{8,9},{9,8},{10,11... | collective-permute-start | bytes 393224 | tf_op jit(solution)/shard_map/ppermute | solution.py:27
  4.9 5.4 %collective-permute-start.1 = (f32[64,512]{1,0:T(8,128)S(1)}, f32[64,512]{1,0:T(8,128)S(1)}, u32[]{:S(2)}, u32[]{:S(2)}) collective-permute-start(f32[64,512]{1,0:T(8,128)S(1)} %get-tuple-element.17), channel_id=1, source_target_pairs={{1,2},{2,1},{3,4},{4,3},{5,6},{6,5},{9,10},{10,9},{11,12},{12,11},... | collective-permute-start | bytes 393224 | tf_op jit(solution)/shard_map/ppermute | solution.py:27
  5.6 4.8 %collective-permute-start.2 = (f32[64,512]{1,0:T(8,128)S(1)}, f32[64,512]{1,0:T(8,128)S(1)}, u32[]{:S(2)}, u32[]{:S(2)}) collective-permute-start(f32[64,512]{1,0:T(8,128)S(1)} %get-tuple-element.18), channel_id=1, source_target_pairs={{0,8},{8,0},{16,24},{24,16},{1,9},{9,1},{17,25},{25,17},{2,10},{10... | collective-permute-start | bytes 393224 | tf_op jit(solution)/shard_map/ppermute | solution.py:27
  5.7 3.5 %copy-start = (f32[32,3,3072]{2,0,1:T(8,128)S(1)}, f32[32,3,3072]{2,0,1:T(8,128)}, u32[]{:S(2)}) copy-start(f32[32,3,3072]{2,0,1:T(8,128)} %param.18) | copy-start | bytes 3538948
  5.7 4.7 %copy-start.4 = (f32[3,1024]{1,0:T(4,128)S(1)}, f32[3,1024]{1,0:T(4,128)}, u32[]{:S(2)}) copy-start(f32[3,1024]{1,0:T(4,128)} %normals_ref.1) | copy-start | bytes 36868
  5.7 4.7 %copy-start.5 = (f32[3,1024]{1,0:T(4,128)S(1)}, f32[3,1024]{1,0:T(4,128)}, u32[]{:S(2)}) copy-start(f32[3,1024]{1,0:T(4,128)} %traction_ref.1) | copy-start | bytes 36868
  5.7 4.7 %collective-permute-start.3 = (f32[64,512]{1,0:T(8,128)S(1)}, f32[64,512]{1,0:T(8,128)S(1)}, u32[]{:S(2)}, u32[]{:S(2)}) collective-permute-start(f32[64,512]{1,0:T(8,128)S(1)} %get-tuple-element.19), channel_id=1, source_target_pairs={{8,16},{16,8},{9,17},{17,9},{10,18},{18,10},{11,19},{19,11},{12,20... | collective-permute-start | bytes 393224 | tf_op jit(solution)/shard_map/ppermute | solution.py:27
  8.5 18.7 %copy-start.2 = (f32[3,3072]{1,0:T(4,128)S(1)}, f32[3,3072]{1,0:T(4,128)}, u32[]{:S(2)}) copy-start(f32[3,3072]{1,0:T(4,128)} %previous_ref.1) | copy-start | bytes 110596
  8.5 18.7 %copy-start.3 = (s32[1,8192]{1,0:T(1,128)S(1)}, s32[1,8192]{1,0:T(1,128)}, u32[]{:S(2)}) copy-start(s32[1,8192]{1,0:T(1,128)} %param.15) | copy-start | bytes 98308
  11.6 15.6 %all-to-all-start = ((f32[8,56,128]{2,1,0:T(8,128)}), f32[8,56,128]{2,1,0:T(8,128)S(1)}, u32[]{:S(2)}, u32[]{:S(2)}) async-start(f32[8,56,128]{2,1,0:T(8,128)} %surface.1), calls=%async_computation | async-start | bytes 458752 | tf_op jit(solution)/shard_map/all_to_all | solution.py:630
  19.4 15.3 %collective-permute-start.4 = (f32[72,512]{1,0:T(8,128)S(1)}, f32[72,512]{1,0:T(8,128)S(1)}, u32[]{:S(2)}, u32[]{:S(2)}) collective-permute-start(f32[72,512]{1,0:T(8,128)S(1)} %get-tuple-element.25), channel_id=1, source_target_pairs={{0,1},{1,0},{2,3},{3,2},{4,5},{5,4},{6,7},{7,6},{8,9},{9,8},{10,11... | collective-permute-start | bytes 442376 | tf_op jit(solution)/shard_map/ppermute | solution.py:27
  21.5 13.2 %collective-permute-start.5 = (f32[72,512]{1,0:T(8,128)S(1)}, f32[72,512]{1,0:T(8,128)S(1)}, u32[]{:S(2)}, u32[]{:S(2)}) collective-permute-start(f32[72,512]{1,0:T(8,128)S(1)} %get-tuple-element.26), channel_id=1, source_target_pairs={{1,2},{2,1},{3,4},{4,3},{5,6},{6,5},{9,10},{10,9},{11,12},{12,11},... | collective-permute-start | bytes 442376 | tf_op jit(solution)/shard_map/ppermute | solution.py:27
  29.5 12.3 %all-to-all-start.1 = ((f32[32,1,256]{2,1,0:T(1,128)}), f32[32,1,256]{2,1,0:T(1,128)S(1)}, u32[]{:S(2)}, u32[]{:S(2)}) async-start(f32[32,1,256]{2,1,0:T(1,128)} %get-tuple-element.28), calls=%async_computation.1 | async-start | bytes 65536 | tf_op jit(solution)/shard_map/all_to_all | solution.py:635
  34.6 7.2 %copy-start.1 = (f32[32,3,3072]{2,0,1:T(8,128)S(1)}, f32[32,3,3072]{2,0,1:T(8,128)}, u32[]{:S(2)}) copy-start(f32[32,3,3072]{2,0,1:T(8,128)} %param.19) | copy-start | bytes 3538948

commit v6 on v5

--- a/solution.py
+++ b/solution.py
@@ -60,12 +60,45 @@
     )(counts, v)
 
 
+def y_edges_kernel(even_ref, p_ref, first_ref, second_ref, sems):
+    last = p_ref.shape[1] - 1
+
+    def edge(out_ref, y, at):
+        return pltpu.make_async_copy(p_ref.at[:, y, :], out_ref, sems.at[at])
+
+    @pl.when(even_ref[0] == 1)
+    def _():
+        edge(first_ref, last, 0).start()
+        edge(second_ref, 0, 1).start()
+
+    @pl.when(even_ref[0] != 1)
+    def _():
+        edge(first_ref, 0, 0).start()
+        edge(second_ref, last, 1).start()
+
+    edge(first_ref, 0, 0).wait()
+    edge(second_ref, 0, 1).wait()
+
+
+def outer_y_edges(even_y, p):
+    cx, cy, cz = p.shape
+    edge = jax.ShapeDtypeStruct((cx, cz), F32)
+    return pl.pallas_call(
+        y_edges_kernel,
+        out_shape=(edge, edge),
+        in_specs=[SMEM, ANY],
+        out_specs=(VMEM, VMEM),
+        scratch_shapes=[pltpu.SemaphoreType.DMA((2,))],
+        compiler_params=limit(8),
+        name="y_edges",
+    )(even_y, in_hbm(p))
+
+
 def faces_kernel(
-    even_x_ref, even_y_ref, p_ref, d_ref, g_ref, first_ref, second_ref, y_first_ref, y_second_ref,
-    ratios, face_sems, y_sems,
+    even_x_ref, p_ref, d_ref, g_ref, first_ref, second_ref, ratios, face_sems
 ):
     cx, cy, cz = p_ref.shape
-    even_x, even_y = even_x_ref[0] == 1, even_y_ref[0] == 1
+    even_x = even_x_ref[0] == 1
 
     def face(out_ref, side, sources):
         return [
@@ -77,9 +110,6 @@
             for k, (ref, plane) in enumerate(sources)
         ]
 
-    def edge(out_ref, y, at):
-        return pltpu.make_async_copy(p_ref.at[:, y, :], out_ref, y_sems.at[at])
-
     head = ((p_ref, 0), (p_ref, 1), (d_ref, 0), (g_ref, 0))
     tail = ((p_ref, cx - 1), (p_ref, cx - 2), (d_ref, cx - 1), (g_ref, cx - 1))
 
@@ -92,43 +122,29 @@
     def _():
         for copy in face(first_ref, 0, head) + face(second_ref, 1, tail):
             copy.start()
-
-    @pl.when(even_y)
-    def _():
-        edge(y_first_ref, cy - 1, 0).start()
-        edge(y_second_ref, 0, 1).start()
-
-    @pl.when(~even_y)
-    def _():
-        edge(y_first_ref, 0, 0).start()
-        edge(y_second_ref, cy - 1, 1).start()
 
     for copy in face(first_ref, 0, head) + face(first_ref, 1, tail):
         copy.wait()
     low, high = 1.0 / (6.0 + ratios[0]), 1.0 / (6.0 + ratios[1])
     for out_ref, above in ((first_ref, even_x), (second_ref, ~even_x)):
         out_ref[3 * cy :] = jnp.where(above, high, low)
-    edge(y_first_ref, 0, 0).wait()
-    edge(y_second_ref, 0, 1).wait()
-
-
-def outer_faces(even_x, even_y, p, d, g):
+
+
+def outer_faces(even_x, p, d, g):
     cx, cy, cz = p.shape
     face = jax.ShapeDtypeStruct((4 * cy, cz), F32)
-    edge = jax.ShapeDtypeStruct((cx, cz), F32)
     return pl.pallas_call(
         faces_kernel,
-        out_shape=(face, face, edge, edge),
-        in_specs=[SMEM, SMEM] + [ANY] * 3,
-        out_specs=(VMEM,) * 4,
+        out_shape=(face, face),
+        in_specs=[SMEM] + [ANY] * 3,
+        out_specs=(VMEM,) * 2,
         scratch_shapes=[
             pltpu.VMEM((2, cy, cz), F32),
             pltpu.SemaphoreType.DMA((2, 4)),
-            pltpu.SemaphoreType.DMA((2,)),
         ],
         compiler_params=limit(8),
         name="faces",
-    )(even_x, even_y, in_hbm(p), in_hbm(d), in_hbm(g))
+    )(even_x, in_hbm(p), in_hbm(d), in_hbm(g))
 
 
 def slab_kernel(p_ref, d_ref, g_ref, planes_ref, columns_ref, held, tile_sems, column_sems):
@@ -620,9 +636,8 @@
     own = lax.axis_index("gy").astype(jnp.int32).reshape(1)
     even_x, even_y = [(1 - lax.axis_index(axis) % 2).astype(jnp.int32).reshape(1) for axis in ("gx", "gy")]
     fluid = (even_x, even_y, pressure, divergence, diagonal)
-    first, second, y_first, y_second = outer_faces(*fluid)
-    y_edges = traded(y_first, y_second, "gy")
-    faces = traded(first, second, "gx")
+    y_edges = traded(*outer_y_edges(even_y, pressure), "gy")
+    faces = traded(*outer_faces(even_x, pressure, divergence, diagonal), "gx")
     planes, columns = slab(pressure, divergence, diagonal)
     y_edges, faces = lax.optimization_barrier((y_edges, faces))
     gram = gram_tile(counts, v)

time: 44.4 us -> 45.3 us (1.020)
  Pallas kernels: 16.3 us -> 17 us
    pallas_call x1 -> x2, Pallas kernels: 1.27 us -> 2.01 us  [the longest x1 1.04 us: outer_y_edges(): pl.pallas_call(y_edges_kernel, out_shape=(edge, edge), in_specs=[SMEM, AN...]
  transfers between devices with their start and end apart: 8 -> 8, of which waited for: 2 -> 2; matrix products, arithmetic and copies ran while one was open for 0% -> 0% of each run, Pallas kernels for 27% -> 28%
where the time goes in v6:
time: 45.3 us; the launch traced here: 44.8 us
  starting transfers between devices  20 us (44%)
  Pallas kernels  17 us (38%)
  waiting for transfers between devices  6.2 us (14%)
  between operations  1.52 us (3%)
    all_to_all x1, starting transfers between devices, shards(): got = lax.all_to_all(block, 'gy', 0, 0, tiled=True)  7.58 us
    pallas_call x1, Pallas kernels, both_sweeps(): pl.pallas_call(sweeps_kernel, out_shape=jax.ShapeDtypeStruct(p.shape, F32...  6.01 us
    ppermute x3, starting transfers between devices, traded(): lax.ppermute(first, axis, pairs(count, 0))  5.18 us
    all_to_all x1, starting transfers between devices, shards(): shared = lax.all_to_all(message, ('gx', 'gy'), 0, 0, tiled=True)  5.11 us
    all_to_all x1, waiting for transfers between devices, shards(): got = lax.all_to_all(block, 'gy', 0, 0, tiled=True)  5.05 us
    pallas_call x1, Pallas kernels, place(): pl.pallas_call(functools.partial(place_kernel, cy), out_shape=(jax.ShapeD...  2.32 us
    pallas_call x1, Pallas kernels, solve(): pl.pallas_call(functools.partial(solve_kernel, groups), out_shape=jax.Sha...  2.18 us
    ppermute x3, starting transfers between devices, traded(): lax.ppermute(second, axis, pairs(count, 1))  2.12 us
  transfers between devices with their start and end apart: 8, of which 2 were waited for; matrix products, arithmetic and copies ran while one was open for 0% of the time, Pallas kernels for 28%

profile of v6, /device:TPU:0, one launch (start us, length us, event | category | flops | bytes accessed | tf_op | source)
XLA Modules:
  0.0 44.8 jit_solution(7825840584614062472)
XLA Ops:
  0.6 1.0 %y_edges.1 = (f32[64,512]{1,0:T(8,128)S(1)}, f32[64,512]{1,0:T(8,128)S(1)}) custom-call(s32[1]{0:T(128)} %bitcast.1.even_ref.even_y_ref, f32[64,16,512]{2,1,0:T(8,128)} %p_ref.7), custom_call_target="tpu_custom_call" | custom-call | tf_op jit(solution)/shard_map/y_edges/pallas_call | solution.py:86
  1.7 3.0 %collective-permute-start = (f32[64,512]{1,0:T(8,128)S(1)}, f32[64,512]{1,0:T(8,128)S(1)}, u32[]{:S(2)}, u32[]{:S(2)}) collective-permute-start(f32[64,512]{1,0:T(8,128)S(1)} %get-tuple-element.16), channel_id=1, source_target_pairs={{0,1},{1,0},{2,3},{3,2},{4,5},{5,4},{6,7},{7,6},{8,9},{9,8},{10,11... | collective-permute-start | bytes 393224 | tf_op jit(solution)/shard_map/ppermute | solution.py:27
  4.7 0.7 %collective-permute-start.1 = (f32[64,512]{1,0:T(8,128)S(1)}, f32[64,512]{1,0:T(8,128)S(1)}, u32[]{:S(2)}, u32[]{:S(2)}) collective-permute-start(f32[64,512]{1,0:T(8,128)S(1)} %get-tuple-element.17), channel_id=1, source_target_pairs={{1,2},{2,1},{3,4},{4,3},{5,6},{6,5},{9,10},{10,9},{11,12},{12,11},... | collective-permute-start | bytes 393224 | tf_op jit(solution)/shard_map/ppermute | solution.py:27
  5.4 1.0 %faces.1 = (f32[64,512]{1,0:T(8,128)S(1)}, f32[64,512]{1,0:T(8,128)S(1)}) custom-call(s32[1]{0:T(128)} %bitcast.even_x_ref.even_ref, f32[64,16,512]{2,1,0:T(8,128)} %p_ref.7, f32[64,16,512]{2,1,0:T(8,128)} %d_ref.5, f32[64,16,512]{2,1,0:T(8,128)} %g_ref.5), custom_call_target="tpu_custom_call" | custom-call | tf_op jit(solution)/shard_map/faces/pallas_call | solution.py:136
  6.4 0.1 collective-permute-start.2
  6.4 0.0 copy-start
  6.5 0.0 copy-start.4
  6.5 0.0 copy-start.5
  6.5 0.8 %collective-permute-start.3 = (f32[64,512]{1,0:T(8,128)S(1)}, f32[64,512]{1,0:T(8,128)S(1)}, u32[]{:S(2)}, u32[]{:S(2)}) collective-permute-start(f32[64,512]{1,0:T(8,128)S(1)} %get-tuple-element.19), channel_id=1, source_target_pairs={{8,16},{16,8},{9,17},{17,9},{10,18},{18,10},{11,19},{19,11},{12,20... | collective-permute-start | bytes 393224 | tf_op jit(solution)/shard_map/ppermute | solution.py:27
  7.3 2.0 %slab.1 = (f32[8,1024]{1,0:T(8,128)S(1)}, f32[8,64,512]{2,1,0:T(8,128)S(1)}) custom-call(f32[64,16,512]{2,1,0:T(8,128)} %p_ref.7, f32[64,16,512]{2,1,0:T(8,128)} %d_ref.5, f32[64,16,512]{2,1,0:T(8,128)} %g_ref.5), custom_call_target="tpu_custom_call" | custom-call | tf_op jit(solution)/shard_map/slab/pallas_call | solution.py:185
  9.3 0.0 copy-start.2
  9.3 0.0 copy-start.3
  10.0 1.1 %gram.1.gram_ref = f32[8,128]{1,0:T(8,128)S(1)} custom-call(s32[1]{0:T(128)S(6)} %copy.12.count_ref, f32[3,32,3072]{2,1,0:T(8,128)S(1)} %bitcast.6), custom_call_target="tpu_custom_call" | custom-call | tf_op jit(solution)/shard_map/gram/pallas_call | solution.py:53
  11.2 1.2 %surface.1 = f32[8,56,128]{2,1,0:T(8,128)} custom-call(s32[1]{0:T(128)} %bitcast.even_x_ref.even_ref, f32[8,1024]{1,0:T(8,128)S(1)} %get-tuple-element.27.planes_ref, f32[64,512]{1,0:T(8,128)S(1)} %collective-permute-done.2.first_ref, f32[64,512]{1,0:T(8,128)S(1)} %collective-permute-done.3.second_ref, f32[3,1024]{1,0:T(4,128)S(1)} %copy-done.4, ...), custom_call_target="tpu_custom_call" | custom-call | tf_op jit(solution)/shard_map/surface/pallas_call | solution.py:292
  12.3 7.6 %all-to-all-start = ((f32[8,56,128]{2,1,0:T(8,128)}), f32[8,56,128]{2,1,0:T(8,128)S(1)}, u32[]{:S(2)}, u32[]{:S(2)}) async-start(f32[8,56,128]{2,1,0:T(8,128)} %surface.1), calls=%async_computation | async-start | bytes 458752 | tf_op jit(solution)/shard_map/all_to_all | solution.py:645
  19.9 0.3 edges.1
  20.2 2.1 %collective-permute-start.4 = (f32[72,512]{1,0:T(8,128)S(1)}, f32[72,512]{1,0:T(8,128)S(1)}, u32[]{:S(2)}, u32[]{:S(2)}) collective-permute-start(f32[72,512]{1,0:T(8,128)S(1)} %get-tuple-element.25), channel_id=1, source_target_pairs={{0,1},{1,0},{2,3},{3,2},{4,5},{5,4},{6,7},{7,6},{8,9},{9,8},{10,11... | collective-permute-start | bytes 442376 | tf_op jit(solution)/shard_map/ppermute | solution.py:27
  22.3 0.7 %collective-permute-start.5 = (f32[72,512]{1,0:T(8,128)S(1)}, f32[72,512]{1,0:T(8,128)S(1)}, u32[]{:S(2)}, u32[]{:S(2)}) collective-permute-start(f32[72,512]{1,0:T(8,128)S(1)} %get-tuple-element.26), channel_id=1, source_target_pairs={{1,2},{2,1},{3,4},{4,3},{5,6},{6,5},{9,10},{10,9},{11,12},{12,11},... | collective-permute-start | bytes 442376 | tf_op jit(solution)/shard_map/ppermute | solution.py:27
  22.9 5.0 %all-to-all-done.got_ref = f32[8,56,128]{2,1,0:T(8,128)S(1)} async-done(((f32[8,56,128]{2,1,0:T(8,128)}), f32[8,56,128]{2,1,0:T(8,128)S(1)}, u32[]{:S(2)}, u32[]{:S(2)}) %all-to-all-start) | async-done | bytes 229408 | tf_op jit(solution)/shard_map/all_to_all | solution.py:645
  28.0 2.3 %place.1 = (f32[3,3072]{1,0:T(4,128)S(1)}, f32[32,1,256]{2,1,0:T(1,128)}) custom-call(s32[1]{0:T(128)} %bitcast.2.place_ref, s32[1]{0:T(128)S(6)} %copy.12.count_ref, f32[8,56,128]{2,1,0:T(8,128)S(1)} %all-to-all-done.got_ref, s32[64,128]{1,0:T(8,128)S(1)} %bitcast.9, f32[3,3072]{1,0:T(4,128)S(1)} %copy-done.2, f32[3,32,3072]{2,1,0:T(8,128)S(1)} %bitcast.7), custom_call_target="tpu_custom_call" | custom-call | tf_op jit(solution)/shard_map/place/pallas_call | solution.py:399
  30.3 5.1 %all-to-all-start.1 = ((f32[32,1,256]{2,1,0:T(1,128)}), f32[32,1,256]{2,1,0:T(1,128)S(1)}, u32[]{:S(2)}, u32[]{:S(2)}) async-start(f32[32,1,256]{2,1,0:T(1,128)} %get-tuple-element.28), calls=%async_computation.1 | async-start | bytes 65536 | tf_op jit(solution)/shard_map/all_to_all | solution.py:650
  35.4 6.0 %sweeps.1 = f32[64,16,512]{2,1,0:T(8,128)} custom-call(s32[1]{0:T(128)} %bitcast.even_x_ref.even_ref, s32[1]{0:T(128)} %bitcast.1.even_ref.even_y_ref, f32[64,16,512]{2,1,0:T(8,128)} %p_ref.7, f32[64,16,512]{2,1,0:T(8,128)} %d_ref.5, f32[64,16,512]{2,1,0:T(8,128)} %g_ref.5, f32[64,512]{1,0:T(8,128)S(1)} %collective-permute-done.2.first_ref, ...), custom_call_target="tpu_custom_call" | custom-call | tf_op jit(solution)/shard_map/sweeps/pallas_call | solution.py:612
  41.5 1.1 %all-to-all-done.1.got_ref = f32[32,1,256]{2,1,0:T(1,128)S(1)} async-done(((f32[32,1,256]{2,1,0:T(1,128)}), f32[32,1,256]{2,1,0:T(1,128)S(1)}, u32[]{:S(2)}, u32[]{:S(2)}) %all-to-all-start.1) | async-done | bytes 32800 | tf_op jit(solution)/shard_map/all_to_all | solution.py:650
  42.6 2.2 %solve.1 = f32[3,3072]{1,0:T(4,128)} custom-call(s32[1]{0:T(128)S(6)} %copy.12.count_ref, f32[32,1,256]{2,1,0:T(1,128)S(1)} %all-to-all-done.1.got_ref, f32[3,3072]{1,0:T(4,128)S(1)} %get-tuple-element.29.owned_ref, f32[3,32,3072]{2,1,0:T(8,128)S(1)} %bitcast.8), custom_call_target="tpu_custom_call" | custom-call | tf_op jit(solution)/shard_map/solve/pallas_call | solution.py:468
  (13 shorter events, 0.0 us)
Async XLA Ops:
  1.7 9.4 %collective-permute-start = (f32[64,512]{1,0:T(8,128)S(1)}, f32[64,512]{1,0:T(8,128)S(1)}, u32[]{:S(2)}, u32[]{:S(2)}) collective-permute-start(f32[64,512]{1,0:T(8,128)S(1)} %get-tuple-element.16), channel_id=1, source_target_pairs={{0,1},{1,0},{2,3},{3,2},{4,5},{5,4},{6,7},{7,6},{8,9},{9,8},{10,11... | collective-permute-start | bytes 393224 | tf_op jit(solution)/shard_map/ppermute | solution.py:27
  4.7 6.4 %collective-permute-start.1 = (f32[64,512]{1,0:T(8,128)S(1)}, f32[64,512]{1,0:T(8,128)S(1)}, u32[]{:S(2)}, u32[]{:S(2)}) collective-permute-start(f32[64,512]{1,0:T(8,128)S(1)} %get-tuple-element.17), channel_id=1, source_target_pairs={{1,2},{2,1},{3,4},{4,3},{5,6},{6,5},{9,10},{10,9},{11,12},{12,11},... | collective-permute-start | bytes 393224 | tf_op jit(solution)/shard_map/ppermute | solution.py:27
  6.4 4.8 %collective-permute-start.2 = (f32[64,512]{1,0:T(8,128)S(1)}, f32[64,512]{1,0:T(8,128)S(1)}, u32[]{:S(2)}, u32[]{:S(2)}) collective-permute-start(f32[64,512]{1,0:T(8,128)S(1)} %get-tuple-element.18), channel_id=1, source_target_pairs={{0,8},{8,0},{16,24},{24,16},{1,9},{9,1},{17,25},{25,17},{2,10},{10... | collective-permute-start | bytes 393224 | tf_op jit(solution)/shard_map/ppermute | solution.py:27
  6.4 3.5 %copy-start = (f32[32,3,3072]{2,0,1:T(8,128)S(1)}, f32[32,3,3072]{2,0,1:T(8,128)}, u32[]{:S(2)}) copy-start(f32[32,3,3072]{2,0,1:T(8,128)} %param.18) | copy-start | bytes 3538948
  6.5 4.7 %copy-start.4 = (f32[3,1024]{1,0:T(4,128)S(1)}, f32[3,1024]{1,0:T(4,128)}, u32[]{:S(2)}) copy-start(f32[3,1024]{1,0:T(4,128)} %normals_ref.1) | copy-start | bytes 36868
  6.5 4.7 %copy-start.5 = (f32[3,1024]{1,0:T(4,128)S(1)}, f32[3,1024]{1,0:T(4,128)}, u32[]{:S(2)}) copy-start(f32[3,1024]{1,0:T(4,128)} %traction_ref.1) | copy-start | bytes 36868
  6.5 4.7 %collective-permute-start.3 = (f32[64,512]{1,0:T(8,128)S(1)}, f32[64,512]{1,0:T(8,128)S(1)}, u32[]{:S(2)}, u32[]{:S(2)}) collective-permute-start(f32[64,512]{1,0:T(8,128)S(1)} %get-tuple-element.19), channel_id=1, source_target_pairs={{8,16},{16,8},{9,17},{17,9},{10,18},{18,10},{11,19},{19,11},{12,20... | collective-permute-start | bytes 393224 | tf_op jit(solution)/shard_map/ppermute | solution.py:27
  9.3 18.7 %copy-start.2 = (f32[3,3072]{1,0:T(4,128)S(1)}, f32[3,3072]{1,0:T(4,128)}, u32[]{:S(2)}) copy-start(f32[3,3072]{1,0:T(4,128)} %previous_ref.1) | copy-start | bytes 110596
  9.3 18.7 %copy-start.3 = (s32[1,8192]{1,0:T(1,128)S(1)}, s32[1,8192]{1,0:T(1,128)}, u32[]{:S(2)}) copy-start(s32[1,8192]{1,0:T(1,128)} %param.15) | copy-start | bytes 98308
  12.3 15.6 %all-to-all-start = ((f32[8,56,128]{2,1,0:T(8,128)}), f32[8,56,128]{2,1,0:T(8,128)S(1)}, u32[]{:S(2)}, u32[]{:S(2)}) async-start(f32[8,56,128]{2,1,0:T(8,128)} %surface.1), calls=%async_computation | async-start | bytes 458752 | tf_op jit(solution)/shard_map/all_to_all | solution.py:645
  20.2 15.3 %collective-permute-start.4 = (f32[72,512]{1,0:T(8,128)S(1)}, f32[72,512]{1,0:T(8,128)S(1)}, u32[]{:S(2)}, u32[]{:S(2)}) collective-permute-start(f32[72,512]{1,0:T(8,128)S(1)} %get-tuple-element.25), channel_id=1, source_target_pairs={{0,1},{1,0},{2,3},{3,2},{4,5},{5,4},{6,7},{7,6},{8,9},{9,8},{10,11... | collective-permute-start | bytes 442376 | tf_op jit(solution)/shard_map/ppermute | solution.py:27
  22.3 13.2 %collective-permute-start.5 = (f32[72,512]{1,0:T(8,128)S(1)}, f32[72,512]{1,0:T(8,128)S(1)}, u32[]{:S(2)}, u32[]{:S(2)}) collective-permute-start(f32[72,512]{1,0:T(8,128)S(1)} %get-tuple-element.26), channel_id=1, source_target_pairs={{1,2},{2,1},{3,4},{4,3},{5,6},{6,5},{9,10},{10,9},{11,12},{12,11},... | collective-permute-start | bytes 442376 | tf_op jit(solution)/shard_map/ppermute | solution.py:27
  30.3 12.3 %all-to-all-start.1 = ((f32[32,1,256]{2,1,0:T(1,128)}), f32[32,1,256]{2,1,0:T(1,128)S(1)}, u32[]{:S(2)}, u32[]{:S(2)}) async-start(f32[32,1,256]{2,1,0:T(1,128)} %get-tuple-element.28), calls=%async_computation.1 | async-start | bytes 65536 | tf_op jit(solution)/shard_map/all_to_all | solution.py:650
  35.4 7.2 %copy-start.1 = (f32[32,3,3072]{2,0,1:T(8,128)S(1)}, f32[32,3,3072]{2,0,1:T(8,128)}, u32[]{:S(2)}) copy-start(f32[32,3,3072]{2,0,1:T(8,128)} %param.19) | copy-start | bytes 3538948
